TPU v7x, 32 devices: a whole 2x2x4 slice. The times are simulated.
32 devices in a mesh: rep: 4 (over y, x), fsdp: 8 (over z, core).
Axes of the slice: x: 2, y: 2, z: 4, core: 2. Of those that a mesh axis runs over, the one named last changes fastest.
Arguments:
- features: bfloat16 [32, 32, 32, 640], P(('rep', 'fsdp')), may hold values from -20 to 20
- out_grad: bfloat16 [32, 32, 32, 640], P(('rep', 'fsdp')), may hold values from -6 to 6
- conv_weight: bfloat16 [5760, 640], P('fsdp'), may hold values from -0.078125 to 0.078125
- conv_bias: bfloat16 [640], P('fsdp'), may hold values from -3 to 3
- norm_gain: bfloat16 [640], P('fsdp'), may hold values from 0.099609375 to 1.8984375
- norm_shift: bfloat16 [640], P('fsdp'), may hold values from -3 to 3
Outputs:
- conv_out: bfloat16 [32, 32, 32, 640], P(('rep', 'fsdp'))
- in_grad: bfloat16 [32, 32, 32, 640], P(('rep', 'fsdp'))
- weight_grad: float32 [5760, 640], P('fsdp')
- bias_grad: float32 [640], P('fsdp')
- gain_grad: float32 [640], P('fsdp')
- shift_grad: float32 [640], P('fsdp')
All inputs are finite; a program needn't handle non-finite values.
Results may differ from a plain program's by a relative error of at most 0.0036.
Values may be sent and summed in bfloat16 or wider, within the bound.
No kernel may reach another device: no remote copies, remote signals or barrier semaphores. Data moves between devices by JAX's collectives and lax.ppermute only.
A program may use at most 128 MiB of HBM per device.

v0:
```python
import functools
import math

import jax
import jax.numpy as jnp
from jax import lax
from jax.experimental import pallas as pl
from jax.experimental.pallas import tpu as pltpu
from jax.sharding import PartitionSpec as P

GROUPS = 16


epsilon = 1e-05

F32 = jnp.float32
BF16 = jnp.bfloat16
VMEM = pl.BlockSpec(memory_space=pltpu.VMEM)
SMEM = pl.BlockSpec(memory_space=pltpu.SMEM)
ANY = pl.BlockSpec(memory_space=pl.ANY)


def params(mib=56):
    return pltpu.CompilerParams(vmem_limit_bytes=mib * 1024 * 1024)


def struct(shape, dtype):
    return jax.ShapeDtypeStruct(shape, dtype)


def shifted_copies(x, side, out_ref, first):
    pixels = x.shape[0]
    column = lax.broadcasted_iota(jnp.int32, x.shape, 0) % side
    edge = jnp.zeros((side, x.shape[1]), BF16)
    for kx in range(3):
        move = (kx - 1) if first else (1 - kx)
        if move == 0:
            moved = x
        elif move == 1:
            moved = jnp.where(column == side - 1, 0.0, pltpu.roll(x, pixels - 1, 0))
        else:
            moved = jnp.where(column == 0, 0.0, pltpu.roll(x, 1, 0))
        out_ref[kx, 0:side, :] = edge
        out_ref[kx, side : side + pixels, :] = moved.astype(BF16)
        out_ref[kx, side + pixels : 2 * side + pixels, :] = edge


def shift_kernel(side, x_ref, out_ref, sum_ref):
    x = x_ref[...].astype(F32)
    sum_ref[...] = jnp.sum(x, axis=0, keepdims=True)
    shifted_copies(x, side, out_ref, False)


def shift_grad(x, side):
    pixels, chans = x.shape
    return pl.pallas_call(
        functools.partial(shift_kernel, side),
        out_shape=(
            struct((3, pixels + 2 * side, chans), BF16),
            struct((1, chans), F32),
        ),
        in_specs=[VMEM],
        out_specs=(VMEM, VMEM),
        compiler_params=params(),
        cost_estimate=pl.CostEstimate(
            flops=8 * x.size, bytes_accessed=8 * x.size, transcendentals=0
        ),
        name="shift_grad",
    )(x)


def same_group(chans):
    size = chans // GROUPS
    a = lax.broadcasted_iota(jnp.int32, (chans, chans), 0) // size
    b = lax.broadcasted_iota(jnp.int32, (chans, chans), 1) // size
    return jnp.where(a == b, 1.0, 0.0).astype(F32)


def group_mean_of(column_sum, pixels):
    chans = column_sum.shape[1]
    count = pixels * (chans // GROUPS)
    total = jnp.dot(
        jnp.broadcast_to(column_sum, (8, chans)),
        same_group(chans),
        preferred_element_type=F32,
        precision=lax.Precision.HIGHEST,
    )
    return total[0:1] * (1.0 / count)


def stats_kernel(x_ref, out_ref):
    pixels = x_ref.shape[0]
    x = x_ref[...].astype(F32)
    mean = group_mean_of(jnp.sum(x, axis=0, keepdims=True), pixels)
    centered = x - mean
    var = group_mean_of(jnp.sum(centered * centered, axis=0, keepdims=True), pixels)
    out_ref[0:1, :] = mean
    out_ref[1:2, :] = lax.rsqrt(var + epsilon)


def stats(x):
    return pl.pallas_call(
        stats_kernel,
        out_shape=struct((2, x.shape[1]), F32),
        in_specs=[VMEM],
        out_specs=VMEM,
        compiler_params=params(),
        cost_estimate=pl.CostEstimate(
            flops=5 * x.size, bytes_accessed=2 * x.size, transcendentals=0
        ),
        name="norm_stats",
    )(x)


def act_kernel(side, x_ref, stat_ref, vec_ref, shifted_ref, turned_ref):
    mean, inv = stat_ref[0:1, :], stat_ref[1:2, :]
    gain = vec_ref[0:1, :].astype(F32)
    shift = vec_ref[1:2, :].astype(F32)
    pre = (x_ref[...].astype(F32) - mean) * inv * gain + shift
    act = (pre / (1.0 + jnp.exp(-pre))).astype(BF16)
    turned_ref[...] = act.T
    shifted_copies(act.astype(F32), side, shifted_ref, True)


def activate(x, stat, vecs, side):
    pixels, chans = x.shape
    return pl.pallas_call(
        functools.partial(act_kernel, side),
        out_shape=(
            struct((3, pixels + 2 * side, chans), BF16),
            struct((chans, pixels), BF16),
        ),
        in_specs=[VMEM, VMEM, VMEM],
        out_specs=(VMEM, VMEM),
        compiler_params=params(),
        cost_estimate=pl.CostEstimate(
            flops=16 * x.size, bytes_accessed=10 * x.size, transcendentals=2 * x.size
        ),
        name="activate",
    )(x, stat, vecs)


def weight_kernel(
    side, extra, piece, place_ref, own_t, sib_t, own_g, sib_g,
    keep_ref, send0_ref, send1_ref, block_ref,
):
    chans, pixels = own_t.shape
    r, z, core = place_ref[0], place_ref[1], place_ref[2]
    blocks = keep_ref.shape[0] * keep_ref.shape[1]
    half = keep_ref.shape[1]
    reps = 2 * keep_ref.shape[2]

    def tap_rows(ref, tap):
        start = pl.multiple_of((2 - tap // 3) * side, side)
        return ref[tap % 3, pl.ds(start, pixels), :]

    for k in range(blocks):
        tap = 2 * k + core
        low, high = 2 * extra * k, 2 * extra * (k + 1)
        first = jnp.dot(
            own_t[low:chans, :], tap_rows(own_g, tap), preferred_element_type=F32
        ) + jnp.dot(sib_t[low:chans, :], tap_rows(sib_g, tap), preferred_element_type=F32)
        block_ref[0 : chans - low, :] = first
        second = jnp.dot(
            own_t[0:high, :], tap_rows(own_g, tap + 1), preferred_element_type=F32
        ) + jnp.dot(sib_t[0:high, :], tap_rows(sib_g, tap + 1), preferred_element_type=F32)
        block_ref[chans - low : chans + 2 * extra, :] = second
        rel_z = k ^ z
        path, slot = rel_z // half, rel_z % half
        step = (chans + extra - piece) // (reps - 1)

        def rows_of(rel):
            at = pl.multiple_of(extra * core + step * (r ^ rel), 16)
            return block_ref[pl.ds(at, piece), :]

        keep_ref[path, slot, 0] = rows_of(0)

        @pl.when(path == 0)
        def _():
            send0_ref[slot, 0] = rows_of(1).astype(BF16)
            keep_ref[0, slot, 1] = rows_of(2)
            send0_ref[slot, 1] = rows_of(3).astype(BF16)

        @pl.when(path == 1)
        def _():
            send1_ref[slot, 0] = rows_of(2).astype(BF16)
            keep_ref[1, slot, 1] = rows_of(1)
            send1_ref[slot, 1] = rows_of(3).astype(BF16)


def weight_pieces(place, own_t, sib_t, own_g, sib_g, side, blocks, extra, piece):
    chans, pixels = own_t.shape
    outs = own_g.shape[2]
    half = blocks // 2
    return pl.pallas_call(
        functools.partial(weight_kernel, side, extra, piece),
        out_shape=(
            struct((2, half, 2, piece, outs), F32),
            struct((half, 2, piece, outs), BF16),
            struct((half, 2, piece, outs), BF16),
        ),
        in_specs=[SMEM, VMEM, VMEM, VMEM, VMEM],
        out_specs=(VMEM, VMEM, VMEM),
        scratch_shapes=[pltpu.VMEM((chans + 2 * extra, outs), F32)],
        compiler_params=params(),
        cost_estimate=pl.CostEstimate(
            flops=4 * blocks * (chans + 2 * extra) * pixels * outs,
            bytes_accessed=30 * chans * pixels,
            transcendentals=0,
        ),
        name="weight_grad",
    )(place, own_t, sib_t, own_g, sib_g)


def fetch_weight(place_ref, gathered, near, far, near_sib, far_sib, weight, sems):
    core, side_half = place_ref[2], place_ref[3]
    shards, window, _ = gathered.shape
    cut = near.shape[1]
    rows = window + 2 * cut
    mine = side_half * (rows - window)
    other = (1 - side_half) * window
    copies = []

    def copy(src, row, count):
        copies.append(
            pltpu.make_async_copy(
                src, weight.at[pl.ds(pl.multiple_of(row, 16), count), :], sems.at[len(copies)]
            )
        )

    for f in range(shards):
        copy(gathered.at[f], f * rows + mine, window)
    for pair, (a, b) in enumerate(((near, far), (near_sib, far_sib))):
        parity = core if pair == 0 else 1 - core
        for z in range(near.shape[0]):
            base = (2 * z + parity) * rows + other
            copy(a.at[z], base, cut)
            copy(b.at[z], base + cut, cut)
    for c in copies:
        c.start()
    return copies


def grad_kernel(
    side, chunk, place_ref, g_ref, x_ref, stat_ref, vec_ref, gathered, near, far, near_sib, far_sib,
    out_ref, sum_ref, weight, scaled, sems,
):
    copies = fetch_weight(
        place_ref, gathered, near, far, near_sib, far_sib, weight, sems
    )
    for c in copies:
        c.wait()
    pixels, chans = x_ref.shape
    mean, inv = stat_ref[0:1, :], stat_ref[1:2, :]
    gain = vec_ref[0:1, :].astype(F32)
    shift = vec_ref[1:2, :].astype(F32)
    sum_ref[...] = jnp.zeros_like(sum_ref)

    @pl.loop(0, pixels // chunk)
    def _(i):
        total = None
        for tap in range(9):
            start = pl.multiple_of(i * chunk + (2 - tap // 3) * side, side)
            part = lax.dot_general(
                g_ref[tap % 3, pl.ds(start, chunk), :],
                weight[tap * chans : (tap + 1) * chans, :],
                (((1,), (1,)), ((), ())),
                preferred_element_type=F32,
            )
            total = part if total is None else total + part
        rows = pl.ds(pl.multiple_of(i * chunk, chunk), chunk)
        normed = (x_ref[rows, :].astype(F32) - mean) * inv
        pre = normed * gain + shift
        sig = 1.0 / (1.0 + jnp.exp(-pre))
        pre_grad = total * sig * (1.0 + pre * (1.0 - sig))
        sum_ref[0:1, :] += jnp.sum(pre_grad * normed, axis=0, keepdims=True)
        sum_ref[1:2, :] += jnp.sum(pre_grad, axis=0, keepdims=True)
        scaled[rows, :] = pre_grad * gain

    cross = group_mean_of(sum_ref[0:1, :] * gain, pixels)
    center = group_mean_of(sum_ref[1:2, :] * gain, pixels)

    @pl.loop(0, pixels // chunk)
    def _(i):
        rows = pl.ds(pl.multiple_of(i * chunk, chunk), chunk)
        normed = (x_ref[rows, :].astype(F32) - mean) * inv
        out_ref[rows, :] = ((scaled[rows, :] - center - normed * cross) * inv).astype(BF16)


def act_grad(place, shifted, x, stat, vecs, weights, side):
    pixels, chans = x.shape
    outs = shifted.shape[2]
    copies = weights[0].shape[0] + 4 * weights[1].shape[0]
    return pl.pallas_call(
        functools.partial(grad_kernel, side, 256),
        out_shape=(struct((pixels, chans), BF16), struct((2, chans), F32)),
        in_specs=[SMEM, VMEM, VMEM, VMEM, VMEM] + [ANY] * 5,
        out_specs=(VMEM, VMEM),
        scratch_shapes=[
            pltpu.VMEM((9 * chans, outs), BF16),
            pltpu.VMEM((pixels, chans), F32),
            pltpu.SemaphoreType.DMA((copies,)),
        ],
        compiler_params=params(),
        cost_estimate=pl.CostEstimate(
            flops=18 * chans * outs * pixels,
            bytes_accessed=18 * chans * outs + 12 * pixels * chans,
            transcendentals=2 * pixels * chans,
        ),
        name="act_grad",
    )(place, shifted, x, stat, vecs, *weights)


def conv_kernel(
    side, chunk, place_ref, a_ref, vec_ref, gathered, near, far, near_sib, far_sib,
    out_ref, weight, sems,
):
    copies = fetch_weight(
        place_ref, gathered, near, far, near_sib, far_sib, weight, sems
    )
    for c in copies:
        c.wait()
    pixels = out_ref.shape[0]
    chans = a_ref.shape[2]
    bias = vec_ref[2:3, :].astype(F32)

    @pl.loop(0, pixels // chunk)
    def _(i):
        total = None
        for tap in range(9):
            start = pl.multiple_of(i * chunk + (tap // 3) * side, side)
            part = jnp.dot(
                a_ref[tap % 3, pl.ds(start, chunk), :],
                weight[tap * chans : (tap + 1) * chans, :],
                preferred_element_type=F32,
            )
            total = part if total is None else total + part
        rows = pl.ds(pl.multiple_of(i * chunk, chunk), chunk)
        out_ref[rows, :] = (total + bias).astype(BF16)


def conv(place, shifted, vecs, weights, side):
    pixels = shifted.shape[1] - 2 * side
    chans = shifted.shape[2]
    outs = weights[0].shape[2]
    copies = weights[0].shape[0] + 4 * weights[1].shape[0]
    return pl.pallas_call(
        functools.partial(conv_kernel, side, 256),
        out_shape=struct((pixels, outs), BF16),
        in_specs=[SMEM, VMEM, VMEM] + [ANY] * 5,
        out_specs=VMEM,
        scratch_shapes=[
            pltpu.VMEM((9 * chans, outs), BF16),
            pltpu.SemaphoreType.DMA((copies,)),
        ],
        compiler_params=params(),
        cost_estimate=pl.CostEstimate(
            flops=18 * chans * outs * pixels,
            bytes_accessed=18 * chans * outs + 8 * pixels * chans,
            transcendentals=0,
        ),
        name="conv_forward",
    )(place, shifted, vecs, *weights)


def join_kernel(scale, place_ref, p0, p1, p2, p3, out_ref):
    r = place_ref[0]
    pieces = (p0, p1, p2, p3)
    piece = p0.shape[0]
    step = (out_ref.shape[0] - piece) // (len(pieces) - 1)
    for q in range(len(pieces)):
        for rel, ref in enumerate(pieces):

            @pl.when((q ^ r) == rel)
            def _():
                out_ref[step * q : step * q + piece, :] = ref[...].astype(F32) * scale


def join(place, pieces, rows, scale):
    outs = pieces[0].shape[1]
    return pl.pallas_call(
        functools.partial(join_kernel, scale),
        out_shape=struct((rows, outs), F32),
        in_specs=[SMEM] + [VMEM] * 4,
        out_specs=VMEM,
        compiler_params=params(),
        cost_estimate=pl.CostEstimate(
            flops=rows * outs, bytes_accessed=6 * rows * outs, transcendentals=0
        ),
        name="join_pieces",
    )(place, *pieces)


def swap(x, axis, mask):
    n = lax.axis_size(axis)
    return lax.ppermute(x, axis, [(i, i ^ mask) for i in range(n)])


def gather_small(x, axis):
    at = lax.axis_index(axis)
    got = x[None]
    mask = 1
    while mask < lax.axis_size(axis):
        other = swap(got, axis, mask)
        bit = (at // mask) % 2 == 1
        got = jnp.where(
            bit, jnp.concatenate([other, got]), jnp.concatenate([got, other])
        )
        mask *= 2
    return got


def sum_all(x, axis, masks):
    terms = [x] + [swap(x, axis, m) for m in masks]
    while len(terms) > 1:
        terms = [terms[i] + terms[i + 1] for i in range(0, len(terms), 2)]
    return terms[0]


def gather_weight(conv_weight, r, core, piece_window):
    rows = conv_weight.shape[0]
    window = piece_window
    upper = ((r ^ (r // 2)) % 2).astype(jnp.int32)
    mine = jnp.where(upper == 1, conv_weight[rows - window :], conv_weight[:window])
    gathered = lax.all_gather(mine, "fsdp", axis=0, tiled=False)
    shards, _, outs = gathered.shape
    by_core = gathered.reshape(shards // 2, 2, window, outs)
    same = jnp.where(core == 1, by_core[:, 1], by_core[:, 0])
    cut = (rows - window) // 2
    lead = window - 2 * cut
    sends = [
        jnp.where(
            upper == 1,
            same[:, lead + s * cut : lead + (s + 1) * cut],
            same[:, s * cut : (s + 1) * cut],
        )
        for s in range(2)
    ]
    near = swap(sends[0], "rep", 1)
    far = swap(sends[1], "rep", 2)
    near_sib = swap(near, "fsdp", 1)
    far_sib = swap(far, "fsdp", 1)
    return (gathered, near, far, near_sib, far_sib), upper


def local_fast(features, out_grad, conv_weight, conv_bias, norm_gain, norm_shift):
    side = features.shape[1]
    chans = features.shape[3]
    outs = out_grad.shape[3]
    pixels = side * side
    rows = conv_weight.shape[0]
    reps, shards = lax.axis_size("rep"), lax.axis_size("fsdp")
    r, f = lax.axis_index("rep"), lax.axis_index("fsdp")
    z, core = f // 2, f % 2
    extra = rows - chans
    piece = round_up(-(-rows // reps), 16)
    window = round_up(-(-rows // 2), 16)
    x = features.reshape(pixels, chans)
    g = out_grad.reshape(pixels, outs)

    small = gather_small(jnp.stack([norm_gain, norm_shift, conv_bias]), "fsdp")
    vecs = jnp.transpose(small, (1, 0, 2)).reshape(3, chans)
    sib_g = swap(g, "fsdp", 1)
    weights, upper = gather_weight(conv_weight, r, core, window)
    place = jnp.stack([r, z, core, upper]).astype(jnp.int32)

    stat = stats(x)
    own_shifted, bias_sum = shift_grad(g, side)
    sib_shifted, _ = shift_grad(sib_g, side)
    act_shifted, own_t = activate(x, stat, vecs, side)
    sib_t = swap(own_t, "fsdp", 1)

    keep, send0, send1 = weight_pieces(
        place, own_t, sib_t, own_shifted, sib_shifted, side, shards // 2, extra, piece
    )
    got0 = swap(send0, "rep", 1)
    got1 = swap(send1, "rep", 2)
    next0 = (keep[0, :, 1] + got0[:, 1].astype(F32)).astype(BF16)
    next1 = (keep[1, :, 1] + got1[:, 1].astype(F32)).astype(BF16)
    last0 = swap(next0, "rep", 2)
    last1 = swap(next1, "rep", 1)
    sum0 = keep[0, :, 0] + got0[:, 0].astype(F32) + last0.astype(F32)
    sum1 = keep[1, :, 0] + got1[:, 0].astype(F32) + last1.astype(F32)
    sums = [sum0[i] for i in range(sum0.shape[0])] + [sum1[i] for i in range(sum1.shape[0])]
    done = sums[0]
    for m in range(1, shards // 2):
        done = done + swap(sums[m].astype(BF16), "fsdp", 2 * m).astype(F32)
    done = done.astype(BF16)
    pieces = [done] + [swap(done, "rep", m) for m in range(1, reps)]

    in_grad, param_sums = act_grad(place, own_shifted, x, stat, vecs, weights, side)
    conv_out = conv(place, act_shifted, vecs, weights, side)

    scale = 1.0 / math.sqrt(reps * shards * pixels)
    weight_grad = join(place, pieces, rows, scale)
    small_sums = jnp.concatenate([bias_sum, param_sums], axis=0)
    small_sums = sum_all(small_sums, "rep", range(1, reps))
    small_sums = sum_all(small_sums, "fsdp", range(2, shards, 2))
    small_sums = sum_all(small_sums, "fsdp", (1,)) * scale
    share = outs // shards
    mine = lax.dynamic_slice_in_dim(small_sums.reshape(3, shards, share), f, 1, axis=1)
    mine = mine.reshape(3, share)
    return (
        conv_out.reshape(1, side, side, outs),
        in_grad.reshape(1, side, side, chans),
        weight_grad,
        mine[0],
        mine[1],
        mine[2],
    )


def round_up(n, m):
    return -(-n // m) * m


def fits(mesh_shape, images, rows, chans, outs, side):
    reps, shards = mesh_shape["rep"], mesh_shape["fsdp"]
    if images != reps * shards or reps != 2 * 2 or shards != 9 - 1:
        return False
    if chans != outs or rows * shards != 9 * chans or chans % 128 or side % 16:
        return False
    extra, piece, window = rows - chans, round_up(-(-rows // reps), 16), round_up(-(-rows // 2), 16)
    step = (rows - piece) // (reps - 1)
    return (
        extra % 16 == 0
        and step * (reps - 1) == rows - piece
        and step % 16 == 0
        and (rows - window) % 32 == 0
    )


def local(features, out_grad, conv_weight, conv_bias, norm_gain, norm_shift):
    images_here = features.shape[0]
    side_cells = features.shape[1]
    channels = features.shape[3]
    pixels = side_cells * side_cells
    group_size = channels // GROUPS
    full_weight, bias_all, gain_all, shift_all = (
        lax.all_gather(conv_weight, "fsdp", axis=0, tiled=True),
        lax.all_gather(conv_bias, "fsdp", axis=0, tiled=True),
        lax.all_gather(norm_gain, "fsdp", axis=0, tiled=True),
        lax.all_gather(norm_shift, "fsdp", axis=0, tiled=True),
    )
    out_chans = full_weight.shape[1]
    values = features.astype(jnp.float32).reshape(images_here, pixels, GROUPS, group_size)
    group_mean = jnp.mean(values, axis=(1, 3), keepdims=True)
    centered = values - group_mean
    group_var = jnp.mean(centered * centered, axis=(1, 3), keepdims=True)
    inv_std = lax.rsqrt(group_var + epsilon)
    normed = centered * inv_std
    gain_cols = gain_all.astype(jnp.float32).reshape(1, 1, GROUPS, group_size)
    shift_cols = shift_all.astype(jnp.float32).reshape(1, 1, GROUPS, group_size)
    pre_act = normed * gain_cols + shift_cols
    activated = (
        jax.nn.silu(pre_act)
        .astype(jnp.bfloat16)
        .reshape(images_here, side_cells, side_cells, channels)
    )
    padded = jnp.pad(activated, ((0, 0), (1, 1), (1, 1), (0, 0)))
    conv_sum = jnp.zeros((images_here * pixels, out_chans), jnp.float32)
    taps_list = []
    for row_off in range(3):
        for col_off in range(3):
            tap_index = 3 * row_off + col_off
            tap_piece = padded[
                :, row_off : row_off + side_cells, col_off : col_off + side_cells, :
            ].reshape(images_here * pixels, channels)
            taps_list.append(tap_piece)
            conv_sum = conv_sum + jnp.dot(
                tap_piece,
                full_weight[tap_index * channels : (tap_index + 1) * channels],
                preferred_element_type=jnp.float32,
            )
    conv_out = (
        (conv_sum + bias_all.astype(jnp.float32)[None, :])
        .astype(jnp.bfloat16)
        .reshape(images_here, side_cells, side_cells, out_chans)
    )
    back_weight, back_gain = (
        lax.all_gather(conv_weight, "fsdp", axis=0, tiled=True),
        lax.all_gather(norm_gain, "fsdp", axis=0, tiled=True),
    )
    grad_rows = out_grad.reshape(images_here * pixels, out_chans)
    grad_padded = jnp.zeros((images_here, side_cells + 2, side_cells + 2, channels), jnp.float32)
    weight_list = []
    for row_off in range(3):
        for col_off in range(3):
            tap_index = 3 * row_off + col_off
            tap_rows = back_weight[tap_index * channels : (tap_index + 1) * channels]
            tap_grad = lax.dot_general(
                grad_rows, tap_rows, (((1,), (1,)), ((), ())), preferred_element_type=jnp.float32
            )
            grad_padded = grad_padded.at[
                :, row_off : row_off + side_cells, col_off : col_off + side_cells, :
            ].add(tap_grad.reshape(images_here, side_cells, side_cells, channels))
            weight_list.append(
                lax.dot_general(
                    taps_list[tap_index],
                    grad_rows,
                    (((0,), (0,)), ((), ())),
                    preferred_element_type=jnp.float32,
                )
            )
    act_grad = grad_padded[:, 1:-1, 1:-1, :].reshape(images_here, pixels, GROUPS, group_size)
    sig_pre = jax.nn.sigmoid(pre_act)
    pre_grad = act_grad * sig_pre * (1.0 + pre_act * (1.0 - sig_pre))
    norm_grad = pre_grad * back_gain.astype(jnp.float32).reshape(1, 1, GROUPS, group_size)
    grad_mean = jnp.mean(norm_grad, axis=(1, 3), keepdims=True)
    cross_mean = jnp.mean(norm_grad * normed, axis=(1, 3), keepdims=True)
    in_grad = (
        ((norm_grad - grad_mean - normed * cross_mean) * inv_std)
        .astype(jnp.bfloat16)
        .reshape(images_here, side_cells, side_cells, channels)
    )
    rep_size = lax.axis_size("rep")
    fsdp_size = lax.axis_size("fsdp")
    grad_scale = 1.0 / math.sqrt(images_here * rep_size * fsdp_size * pixels)
    weight_term = jnp.concatenate(weight_list, axis=0) * grad_scale
    bias_term = jnp.sum(grad_rows.astype(jnp.float32), axis=0) * grad_scale
    gain_term = jnp.sum(pre_grad * normed, axis=(0, 1)).reshape(channels) * grad_scale
    shift_term = jnp.sum(pre_grad, axis=(0, 1)).reshape(channels) * grad_scale
    shards = (
        lax.psum_scatter(weight_term, "fsdp", scatter_dimension=0, tiled=True),
        lax.psum_scatter(bias_term, "fsdp", scatter_dimension=0, tiled=True),
        lax.psum_scatter(gain_term, "fsdp", scatter_dimension=0, tiled=True),
        lax.psum_scatter(shift_term, "fsdp", scatter_dimension=0, tiled=True),
    )
    weight_grad, bias_grad, gain_grad, shift_grad = lax.psum(
        (shards[0], shards[1], shards[2], shards[3]), "rep"
    )
    return (conv_out, in_grad, weight_grad, bias_grad, gain_grad, shift_grad)


def solution(mesh):
    placed = (
        P(("rep", "fsdp"), None, None, None),
        P(("rep", "fsdp"), None, None, None),
        P("fsdp", None),
        P("fsdp"),
        P("fsdp"),
        P("fsdp"),
    )
    out_placed = (
        P(("rep", "fsdp"), None, None, None),
        P(("rep", "fsdp"), None, None, None),
        P("fsdp", None),
        P("fsdp"),
        P("fsdp"),
        P("fsdp"),
    )

    def run(features, out_grad, conv_weight, *vectors):
        images, side, _, chans = features.shape
        rows, outs = conv_weight.shape
        shape = dict(mesh.shape)
        fast = fits(shape, images, rows // shape["fsdp"], chans, outs, side)
        return jax.shard_map(
            local_fast if fast else local,
            mesh=mesh,
            in_specs=placed,
            out_specs=out_placed,
            check_vma=False,
        )(features, out_grad, conv_weight, *vectors)

    return run
```

profile of v0, /device:TPU:1, one launch (start us, length us, event | category | flops | bytes accessed | tf_op | source)
XLA Modules:
  0.0 199.6 jit_solution(12362468853230055085)
XLA Ops:
  7.2 2.0 %slice_select_fusion.2 = bf16[368,640]{1,0:T(8,128)(2,1)} fusion(bf16[720,640]{1,0:T(8,128)(2,1)} %param.8, pred[]{:T(512)S(6)} %eq.24), kind=kLoop, calls=%fused_computation.29 | loop fusion | flops 235520 | bytes 1413121 | tf_op jit(solution)/shard_map/jit(_where)/select_n | solution.py:424
  11.2 2.5 %collective-permute-start.1 = (bf16[2,3,80]{2,1,0:T(4,128)(2,1)S(1)}, bf16[2,3,80]{2,1,0:T(4,128)(2,1)S(1)}, u32[]{:S(2)}, u32[]{:S(2)}) collective-permute-start(bf16[2,3,80]{2,1,0:T(4,128)(2,1)S(1)} %maximum_select_fusion.2), channel_id=1, source_target_pairs={{0,2},{1,3},{2,0},{3,1},{4,6},{5,7},{6,4},{7,5},{8,10},{9,11},{10,... | collective-permute-start | bytes 2888 | tf_op jit(solution)/shard_map/ppermute | solution.py:396
  14.7 2.5 %collective-permute-start.2 = (bf16[4,3,80]{2,1,0:T(4,128)(2,1)S(1)}, bf16[4,3,80]{2,1,0:T(4,128)(2,1)S(1)}, u32[]{:S(2)}, u32[]{:S(2)}) collective-permute-start(bf16[4,3,80]{2,1,0:T(4,128)(2,1)S(1)} %maximum_select_fusion.1), channel_id=1, source_target_pairs={{0,4},{1,5},{2,6},{3,7},{4,0},{5,1},{6,2},{7,3},{8,12},{9,13},{10,... | collective-permute-start | bytes 5768 | tf_op jit(solution)/shard_map/ppermute | solution.py:396
  17.2 1.8 collective-permute-start.8
  19.0 4.0 %norm_stats.1.stat_ref = f32[2,640]{1,0:T(2,128)} custom-call(bf16[1024,640]{1,0:T(8,128)(2,1)} %bitcast.102), custom_call_target="tpu_custom_call" | custom-call | flops 3276800 | bytes 1310720 | tf_op jit(solution)/shard_map/norm_stats/pallas_call | solution.py:102
  23.7 5.5 %activate.1 = (bf16[3,1088,640]{2,1,0:T(8,128)(2,1)}, bf16[640,1024]{1,0:T(8,128)(2,1)}) custom-call(bf16[1024,640]{1,0:T(8,128)(2,1)} %bitcast.103, f32[2,640]{1,0:T(2,128)} %norm_stats.1.stat_ref, bf16[3,640]{1,0:T(4,128)(2,1)} %reshape.54.vec_ref), custom_call_target="tpu_custom_call" | custom-call | flops 10485760 | bytes 6553600 | tf_op jit(solution)/shard_map/activate/pallas_call | solution.py:127
  29.2 4.3 %shift_grad.2 = (bf16[3,1088,640]{2,1,0:T(8,128)(2,1)}, f32[1,640]{1,0:T(1,128)}) custom-call(bf16[1024,640]{1,0:T(8,128)(2,1)} %bitcast.101), custom_call_target="tpu_custom_call" | custom-call | flops 5242880 | bytes 5242880 | tf_op jit(solution)/shard_map/shift_grad/pallas_call | solution.py:56
  35.1 4.3 %shift_grad.3 = (bf16[3,1088,640]{2,1,0:T(8,128)(2,1)}, f32[1,640]{1,0:T(1,128)}) custom-call(bf16[1024,640]{1,0:T(8,128)(2,1)} %copy-done.1), custom_call_target="tpu_custom_call" | custom-call | flops 5242880 | bytes 5242880 | tf_op jit(solution)/shard_map/shift_grad/pallas_call | solution.py:56
  40.5 20.3 %weight_grad.1 = (f32[2,2,2,192,640]{4,3,2,1,0:T(8,128)}, bf16[2,2,192,640]{3,2,1,0:T(8,128)(2,1)}, bf16[2,2,192,640]{3,2,1,0:T(8,128)(2,1)}) custom-call(s32[4]{0:T(128)} %pad_add_fusion.place_ref, bf16[640,1024]{1,0:T(8,128)(2,1)} %get-tuple-element.19.own_t, bf16[640,1024]{1,0:T(8,128)(2,1)} %copy-done.7, ...), custom_call_target="tpu_custom_call" | custom-call | flops 8388608000 | bytes 19660800 | tf_op jit(solution)/shard_map/weight_grad/pallas_call | solution.py:195
  65.9 19.0 %collective-permute-done.12 = bf16[2,2,192,640]{3,2,0,1:T(8,128)(2,1)S(1)} collective-permute-done((bf16[2,2,192,640]{3,2,0,1:T(8,128)(2,1)S(1)}, bf16[2,2,192,640]{3,2,0,1:T(8,128)(2,1)S(1)}, u32[]{:S(2)}, u32[]{:S(2)}) %collective-permute-start.12) | collective-permute-done | bytes 983072 | tf_op jit(solution)/shard_map/ppermute | solution.py:396
  84.9 2.1 %fusion.3 = bf16[2,192,640]{2,1,0:T(8,128)(2,1)} fusion(bf16[2,2,192,640]{3,2,0,1:T(8,128)(2,1)S(1)} %collective-permute-done.12, f32[2,2,2,192,640]{4,3,2,1,0:T(8,128)} %get-tuple-element.21), kind=kLoop, calls=%fused_computation.6 | loop fusion | flops 737280 | bytes 1966080 | tf_op jit(solution)/shard_map/convert_element_type | solution.py:479
  88.2 2.3 %fusion.1 = bf16[4,368,640]{2,1,0:T(8,128)(2,1)S(1)} fusion(bf16[4,2,368,640]{3,2,1,0:T(8,128)(2,1)} %bitcast.97, pred[]{:T(512)S(6)} %eq.23), kind=kLoop, calls=%fused_computation.2 | loop fusion | flops 942080 | bytes 5652481 | tf_op jit(solution)/shard_map/jit(_where)/select_n | solution.py:428
  92.2 6.3 %collective-permute-done.13 = bf16[2,192,640]{2,1,0:T(8,128)(2,1)S(1)} collective-permute-done((bf16[2,192,640]{2,1,0:T(8,128)(2,1)}, bf16[2,192,640]{2,1,0:T(8,128)(2,1)S(1)}, u32[]{:S(2)}, u32[]{:S(2)}) %collective-permute-start.13) | collective-permute-done | bytes 491552 | tf_op jit(solution)/shard_map/ppermute | solution.py:396
  100.1 1.9 collective-permute-start.15
  102.6 15.2 %collective-permute-done.3.near = bf16[4,176,640]{2,1,0:T(8,128)(2,1)S(1)} collective-permute-done((bf16[4,176,640]{2,1,0:T(8,128)(2,1)S(1)}, bf16[4,176,640]{2,1,0:T(8,128)(2,1)S(1)}, u32[]{:S(2)}, u32[]{:S(2)}) %collective-permute-start.3) | collective-permute-done | bytes 901152 | tf_op jit(solution)/shard_map/ppermute | solution.py:396
  117.8 2.3 %collective-permute-start.5 = (bf16[4,176,640]{2,1,0:T(8,128)(2,1)S(1)}, bf16[4,176,640]{2,1,0:T(8,128)(2,1)S(1)}, u32[]{:S(2)}, u32[]{:S(2)}) collective-permute-start(bf16[4,176,640]{2,1,0:T(8,128)(2,1)S(1)} %collective-permute-done.3.near), channel_id=1, source_target_pairs={{0,1},{1,0},{2,3},{3,2},{4,5},{5,4},{6,7},{7,6},{8,9},{9,8},{10,11... | collective-permute-start | bytes 2703368 | tf_op jit(solution)/shard_map/ppermute | solution.py:396
  123.9 3.8 %collective-permute-done.11 = bf16[192,640]{1,0:T(8,128)(2,1)S(1)} collective-permute-done((bf16[192,640]{1,0:T(8,128)(2,1)S(1)}, bf16[192,640]{1,0:T(8,128)(2,1)S(1)}, u32[]{:S(2)}, u32[]{:S(2)}) %collective-permute-start.11) | collective-permute-done | bytes 245792 | tf_op jit(solution)/shard_map/ppermute | solution.py:396
  130.3 21.7 %act_grad.1 = (bf16[1024,640]{1,0:T(8,128)(2,1)}, f32[2,640]{1,0:T(2,128)}) custom-call(s32[4]{0:T(128)} %pad_add_fusion.place_ref, bf16[3,1088,640]{2,1,0:T(8,128)(2,1)} %get-tuple-element.17.g_ref.own_g, bf16[1024,640]{1,0:T(8,128)(2,1)} %bitcast.104, f32[2,640]{1,0:T(2,128)} %norm_stats.1.stat_ref, bf16[3,640]{1,0:T(4,128)(2,1)} %reshape.54.vec_ref, ...), custom_call_target="tpu_custom_call" | custom-call | flops 7549747200 | bytes 15237120 | tf_op jit(solution)/shard_map/act_grad/pallas_call | solution.py:294
  154.3 2.3 %collective-permute-start.21 = (f32[3,640]{1,0:T(4,128)S(1)}, f32[3,640]{1,0:T(4,128)S(1)}, u32[]{:S(2)}, u32[]{:S(2)}) collective-permute-start(f32[3,640]{1,0:T(4,128)S(1)} %pad_maximum_fusion), channel_id=1, source_target_pairs={{0,24},{8,16},{16,8},{24,0},{1,25},{9,17},{17,9},{25,1},{2,26},{10... | collective-permute-start | bytes 23048 | tf_op jit(solution)/shard_map/ppermute | solution.py:396
  156.9 3.5 %collective-permute-done.21 = f32[3,640]{1,0:T(4,128)S(1)} collective-permute-done((f32[3,640]{1,0:T(4,128)S(1)}, f32[3,640]{1,0:T(4,128)S(1)}, u32[]{:S(2)}, u32[]{:S(2)}) %collective-permute-start.21) | collective-permute-done | bytes 7712 | tf_op jit(solution)/shard_map/ppermute | solution.py:396
  161.2 2.3 %collective-permute-start.24 = (f32[3,640]{1,0:T(4,128)S(1)}, f32[3,640]{1,0:T(4,128)S(1)}, u32[]{:S(2)}, u32[]{:S(2)}) collective-permute-start(f32[3,640]{1,0:T(4,128)S(1)} %add_add_fusion.1), channel_id=1, source_target_pairs={{0,6},{1,7},{2,4},{3,5},{4,2},{5,3},{6,0},{7,1},{8,14},{9,15},{10,... | collective-permute-start | bytes 23048 | tf_op jit(solution)/shard_map/ppermute | solution.py:396
  165.6 3.0 %join_pieces.1 = f32[720,640]{1,0:T(8,128)} custom-call(s32[4]{0:T(128)} %pad_add_fusion.place_ref, bf16[192,640]{1,0:T(8,128)(2,1)} %copy-done.2, bf16[192,640]{1,0:T(8,128)(2,1)} %copy-done.3, bf16[192,640]{1,0:T(8,128)(2,1)} %copy-done.4, bf16[192,640]{1,0:T(8,128)(2,1)} %copy-done.5), custom_call_target="tpu_custom_call" | custom-call | flops 460800 | bytes 2764800 | tf_op jit(solution)/shard_map/join_pieces/pallas_call | solution.py:381
  168.6 5.8 %collective-permute-start.25 = (f32[3,640]{1,0:T(4,128)S(1)}, f32[3,640]{1,0:T(4,128)S(1)}, u32[]{:S(2)}, u32[]{:S(2)}) collective-permute-start(f32[3,640]{1,0:T(4,128)S(1)} %add_add_fusion), channel_id=1, source_target_pairs={{0,1},{1,0},{2,3},{3,2},{4,5},{5,4},{6,7},{7,6},{8,9},{9,8},{10,11... | collective-permute-start | bytes 23048 | tf_op jit(solution)/shard_map/ppermute | solution.py:396
  174.4 17.7 %conv_forward.1 = bf16[1024,640]{1,0:T(8,128)(2,1)} custom-call(s32[4]{0:T(128)} %pad_add_fusion.place_ref, bf16[3,1088,640]{2,1,0:T(8,128)(2,1)} %get-tuple-element.16.a_ref, bf16[3,640]{1,0:T(4,128)(2,1)} %reshape.54.vec_ref, bf16[8,368,640]{2,1,0:T(8,128)(2,1)} %bitcast.99, bf16[4,176,640]{2,1,0:T(8,128)(2,1)} %copy-done.8, ...), custom_call_target="tpu_custom_call" | custom-call | flops 7549747200 | bytes 12615680 | tf_op jit(solution)/shard_map/conv_forward/pallas_call | solution.py:347
  (87 shorter events, 29.1 us)
Async XLA Ops:
  7.2 81.0 %all-gather.3.cloned.1.call-start = ((), (), s32[]{:S(2)}) async-start(), calls=%async_computation | async-start | bytes 4239360 | tf_op jit(solution)/shard_map/all_gather | solution.py:425
  14.7 8.3 %collective-permute-start.2 = (bf16[4,3,80]{2,1,0:T(4,128)(2,1)S(1)}, bf16[4,3,80]{2,1,0:T(4,128)(2,1)S(1)}, u32[]{:S(2)}, u32[]{:S(2)}) collective-permute-start(bf16[4,3,80]{2,1,0:T(4,128)(2,1)S(1)} %maximum_select_fusion.1), channel_id=1, source_target_pairs={{0,4},{1,5},{2,6},{3,7},{4,0},{5,1},{6,2},{7,3},{8,12},{9,13},{10,... | collective-permute-start | bytes 5768 | tf_op jit(solution)/shard_map/ppermute | solution.py:396
  17.2 16.8 %collective-permute-start.8 = (bf16[1024,640]{1,0:T(8,128)(2,1)}, bf16[1024,640]{1,0:T(8,128)(2,1)S(1)}, u32[]{:S(2)}, u32[]{:S(2)}) collective-permute-start(bf16[1024,640]{1,0:T(8,128)(2,1)} %bitcast.100), channel_id=1, source_target_pairs={{0,1},{1,0},{2,3},{3,2},{4,5},{5,4},{6,7},{7,6},{8,9},{9,8},{10,11... | collective-permute-start | bytes 3932168 | tf_op jit(solution)/shard_map/ppermute | solution.py:396
  29.2 10.2 %collective-permute-start.7 = (bf16[640,1024]{1,0:T(8,128)(2,1)}, bf16[640,1024]{1,0:T(8,128)(2,1)S(1)}, u32[]{:S(2)}, u32[]{:S(2)}) collective-permute-start(bf16[640,1024]{1,0:T(8,128)(2,1)} %get-tuple-element.19.own_t), channel_id=1, source_target_pairs={{0,1},{1,0},{2,3},{3,2},{4,5},{5,4},{6,7},{7,6},{8,9},{9,8},{10,11... | collective-permute-start | bytes 3932168 | tf_op jit(solution)/shard_map/ppermute | solution.py:396
  62.0 22.9 %collective-permute-start.12 = (bf16[2,2,192,640]{3,2,0,1:T(8,128)(2,1)S(1)}, bf16[2,2,192,640]{3,2,0,1:T(8,128)(2,1)S(1)}, u32[]{:S(2)}, u32[]{:S(2)}) collective-permute-start(bf16[2,2,192,640]{3,2,0,1:T(8,128)(2,1)S(1)} %copy.26), channel_id=1, source_target_pairs={{0,16},{8,24},{16,0},{24,8},{1,17},{9,25},{17,1},{25,9},{2,18},{10... | collective-permute-start | bytes 2949128 | tf_op jit(solution)/shard_map/ppermute | solution.py:396
  64.6 27.6 %collective-permute-start.9 = (bf16[2,2,192,640]{3,2,0,1:T(8,128)(2,1)S(1)}, bf16[2,2,192,640]{3,2,0,1:T(8,128)(2,1)S(1)}, u32[]{:S(2)}, u32[]{:S(2)}) collective-permute-start(bf16[2,2,192,640]{3,2,0,1:T(8,128)(2,1)S(1)} %copy.23), channel_id=1, source_target_pairs={{0,8},{8,0},{16,24},{24,16},{1,9},{9,1},{17,25},{25,17},{2,10},{10... | collective-permute-start | bytes 2949128 | tf_op jit(solution)/shard_map/ppermute | solution.py:396
  87.0 11.5 %collective-permute-start.13 = (bf16[2,192,640]{2,1,0:T(8,128)(2,1)}, bf16[2,192,640]{2,1,0:T(8,128)(2,1)S(1)}, u32[]{:S(2)}, u32[]{:S(2)}) collective-permute-start(bf16[2,192,640]{2,1,0:T(8,128)(2,1)} %fusion.3), channel_id=1, source_target_pairs={{0,8},{8,0},{16,24},{24,16},{1,9},{9,1},{17,25},{25,17},{2,10},{10... | collective-permute-start | bytes 1474568 | tf_op jit(solution)/shard_map/ppermute | solution.py:396
  90.6 27.2 %collective-permute-start.3 = (bf16[4,176,640]{2,1,0:T(8,128)(2,1)S(1)}, bf16[4,176,640]{2,1,0:T(8,128)(2,1)S(1)}, u32[]{:S(2)}, u32[]{:S(2)}) collective-permute-start(bf16[4,176,640]{2,1,0:T(8,128)(2,1)S(1)} %get-tuple-element.29), channel_id=1, source_target_pairs={{0,8},{8,0},{16,24},{24,16},{1,9},{9,1},{17,25},{25,17},{2,10},{10... | collective-permute-start | bytes 2703368 | tf_op jit(solution)/shard_map/ppermute | solution.py:396
  91.0 29.2 %collective-permute-start.4 = (bf16[4,176,640]{2,1,0:T(8,128)(2,1)S(1)}, bf16[4,176,640]{2,1,0:T(8,128)(2,1)S(1)}, u32[]{:S(2)}, u32[]{:S(2)}) collective-permute-start(bf16[4,176,640]{2,1,0:T(8,128)(2,1)S(1)} %get-tuple-element.28), channel_id=1, source_target_pairs={{0,16},{8,24},{16,0},{24,8},{1,17},{9,25},{17,1},{25,9},{2,18},{10... | collective-permute-start | bytes 2703368 | tf_op jit(solution)/shard_map/ppermute | solution.py:396
  98.8 22.2 %collective-permute-start.10 = (bf16[2,192,640]{2,1,0:T(8,128)(2,1)S(1)}, bf16[2,192,640]{2,1,0:T(8,128)(2,1)S(1)}, u32[]{:S(2)}, u32[]{:S(2)}) collective-permute-start(bf16[2,192,640]{2,1,0:T(8,128)(2,1)S(1)} %get-tuple-element.27), channel_id=1, source_target_pairs={{0,16},{8,24},{16,0},{24,8},{1,17},{9,25},{17,1},{25,9},{2,18},{10... | collective-permute-start | bytes 1474568 | tf_op jit(solution)/shard_map/ppermute | solution.py:396
  100.1 22.4 %collective-permute-start.15 = (bf16[192,640]{1,0:T(8,128)(2,1)S(1)}, bf16[192,640]{1,0:T(8,128)(2,1)S(1)}, u32[]{:S(2)}, u32[]{:S(2)}) collective-permute-start(bf16[192,640]{1,0:T(8,128)(2,1)S(1)} %get-tuple-element.31), channel_id=1, source_target_pairs={{0,6},{1,7},{2,4},{3,5},{4,2},{5,3},{6,0},{7,1},{8,14},{9,15},{10,... | collective-permute-start | bytes 737288 | tf_op jit(solution)/shard_map/ppermute | solution.py:396
  102.0 21.8 %collective-permute-start.14 = (bf16[192,640]{1,0:T(8,128)(2,1)S(1)}, bf16[192,640]{1,0:T(8,128)(2,1)S(1)}, u32[]{:S(2)}, u32[]{:S(2)}) collective-permute-start(bf16[192,640]{1,0:T(8,128)(2,1)S(1)} %get-tuple-element.30), channel_id=1, source_target_pairs={{0,4},{1,5},{2,6},{3,7},{4,0},{5,1},{6,2},{7,3},{8,12},{9,13},{10,... | collective-permute-start | bytes 737288 | tf_op jit(solution)/shard_map/ppermute | solution.py:396
  117.8 11.3 %collective-permute-start.5 = (bf16[4,176,640]{2,1,0:T(8,128)(2,1)S(1)}, bf16[4,176,640]{2,1,0:T(8,128)(2,1)S(1)}, u32[]{:S(2)}, u32[]{:S(2)}) collective-permute-start(bf16[4,176,640]{2,1,0:T(8,128)(2,1)S(1)} %collective-permute-done.3.near), channel_id=1, source_target_pairs={{0,1},{1,0},{2,3},{3,2},{4,5},{5,4},{6,7},{7,6},{8,9},{9,8},{10,11... | collective-permute-start | bytes 2703368 | tf_op jit(solution)/shard_map/ppermute | solution.py:396
  120.1 9.0 %collective-permute-start.6 = (bf16[4,176,640]{2,1,0:T(8,128)(2,1)S(1)}, bf16[4,176,640]{2,1,0:T(8,128)(2,1)S(1)}, u32[]{:S(2)}, u32[]{:S(2)}) collective-permute-start(bf16[4,176,640]{2,1,0:T(8,128)(2,1)S(1)} %collective-permute-done.4.far), channel_id=1, source_target_pairs={{0,1},{1,0},{2,3},{3,2},{4,5},{5,4},{6,7},{7,6},{8,9},{9,8},{10,11... | collective-permute-start | bytes 2703368 | tf_op jit(solution)/shard_map/ppermute | solution.py:396
  121.2 6.4 %collective-permute-start.11 = (bf16[192,640]{1,0:T(8,128)(2,1)S(1)}, bf16[192,640]{1,0:T(8,128)(2,1)S(1)}, u32[]{:S(2)}, u32[]{:S(2)}) collective-permute-start(bf16[192,640]{1,0:T(8,128)(2,1)S(1)} %fusion.15), channel_id=1, source_target_pairs={{0,2},{1,3},{2,0},{3,1},{4,6},{5,7},{6,4},{7,5},{8,10},{9,11},{10,... | collective-permute-start | bytes 737288 | tf_op jit(solution)/shard_map/ppermute | solution.py:396
  127.8 35.7 %collective-permute-start.16 = (bf16[192,640]{1,0:T(8,128)(2,1)S(1)}, bf16[192,640]{1,0:T(8,128)(2,1)S(1)}, u32[]{:S(2)}, u32[]{:S(2)}) collective-permute-start(bf16[192,640]{1,0:T(8,128)(2,1)S(1)} %fusion.14.p0), channel_id=1, source_target_pairs={{0,8},{8,0},{16,24},{24,16},{1,9},{9,1},{17,25},{25,17},{2,10},{10... | collective-permute-start | bytes 737288 | tf_op jit(solution)/shard_map/ppermute | solution.py:396
  152.7 3.9 %collective-permute-start.20 = (f32[3,640]{1,0:T(4,128)S(1)}, f32[3,640]{1,0:T(4,128)S(1)}, u32[]{:S(2)}, u32[]{:S(2)}) collective-permute-start(f32[3,640]{1,0:T(4,128)S(1)} %pad_maximum_fusion), channel_id=1, source_target_pairs={{0,16},{8,24},{16,0},{24,8},{1,17},{9,25},{17,1},{25,9},{2,18},{10... | collective-permute-start | bytes 23048 | tf_op jit(solution)/shard_map/ppermute | solution.py:396
  152.8 11.4 %collective-permute-start.17 = (bf16[192,640]{1,0:T(8,128)(2,1)S(1)}, bf16[192,640]{1,0:T(8,128)(2,1)S(1)}, u32[]{:S(2)}, u32[]{:S(2)}) collective-permute-start(bf16[192,640]{1,0:T(8,128)(2,1)S(1)} %fusion.14.p0), channel_id=1, source_target_pairs={{0,16},{8,24},{16,0},{24,8},{1,17},{9,25},{17,1},{25,9},{2,18},{10... | collective-permute-start | bytes 737288 | tf_op jit(solution)/shard_map/ppermute | solution.py:396
  154.2 10.0 %collective-permute-start.18 = (bf16[192,640]{1,0:T(8,128)(2,1)S(1)}, bf16[192,640]{1,0:T(8,128)(2,1)S(1)}, u32[]{:S(2)}, u32[]{:S(2)}) collective-permute-start(bf16[192,640]{1,0:T(8,128)(2,1)S(1)} %fusion.14.p0), channel_id=1, source_target_pairs={{0,24},{8,16},{16,8},{24,0},{1,25},{9,17},{17,9},{25,1},{2,26},{10... | collective-permute-start | bytes 737288 | tf_op jit(solution)/shard_map/ppermute | solution.py:396
  154.3 6.1 %collective-permute-start.21 = (f32[3,640]{1,0:T(4,128)S(1)}, f32[3,640]{1,0:T(4,128)S(1)}, u32[]{:S(2)}, u32[]{:S(2)}) collective-permute-start(f32[3,640]{1,0:T(4,128)S(1)} %pad_maximum_fusion), channel_id=1, source_target_pairs={{0,24},{8,16},{16,8},{24,0},{1,25},{9,17},{17,9},{25,1},{2,26},{10... | collective-permute-start | bytes 23048 | tf_op jit(solution)/shard_map/ppermute | solution.py:396
  161.1 7.5 %collective-permute-start.23 = (f32[3,640]{1,0:T(4,128)S(1)}, f32[3,640]{1,0:T(4,128)S(1)}, u32[]{:S(2)}, u32[]{:S(2)}) collective-permute-start(f32[3,640]{1,0:T(4,128)S(1)} %add_add_fusion.1), channel_id=1, source_target_pairs={{0,4},{1,5},{2,6},{3,7},{4,0},{5,1},{6,2},{7,3},{8,12},{9,13},{10,... | collective-permute-start | bytes 23048 | tf_op jit(solution)/shard_map/ppermute | solution.py:396
  161.2 7.4 %collective-permute-start.24 = (f32[3,640]{1,0:T(4,128)S(1)}, f32[3,640]{1,0:T(4,128)S(1)}, u32[]{:S(2)}, u32[]{:S(2)}) collective-permute-start(f32[3,640]{1,0:T(4,128)S(1)} %add_add_fusion.1), channel_id=1, source_target_pairs={{0,6},{1,7},{2,4},{3,5},{4,2},{5,3},{6,0},{7,1},{8,14},{9,15},{10,... | collective-permute-start | bytes 23048 | tf_op jit(solution)/shard_map/ppermute | solution.py:396
  163.5 5.1 %collective-permute-start.22 = (f32[3,640]{1,0:T(4,128)S(1)}, f32[3,640]{1,0:T(4,128)S(1)}, u32[]{:S(2)}, u32[]{:S(2)}) collective-permute-start(f32[3,640]{1,0:T(4,128)S(1)} %add_add_fusion.1), channel_id=1, source_target_pairs={{0,2},{1,3},{2,0},{3,1},{4,6},{5,7},{6,4},{7,5},{8,10},{9,11},{10,... | collective-permute-start | bytes 23048 | tf_op jit(solution)/shard_map/ppermute | solution.py:396
  168.6 23.4 %collective-permute-start.25 = (f32[3,640]{1,0:T(4,128)S(1)}, f32[3,640]{1,0:T(4,128)S(1)}, u32[]{:S(2)}, u32[]{:S(2)}) collective-permute-start(f32[3,640]{1,0:T(4,128)S(1)} %add_add_fusion), channel_id=1, source_target_pairs={{0,1},{1,0},{2,3},{3,2},{4,5},{5,4},{6,7},{7,6},{8,9},{9,8},{10,11... | collective-permute-start | bytes 23048 | tf_op jit(solution)/shard_map/ppermute | solution.py:396
  (15 other events, 91.3 us)
Sparse Core Ops, SparseCore 0:
  9.6 45.8 all-gather.2
where the time goes:
time: 200 us
  Pallas kernels  80.6 us (40%)
  waiting for transfers between devices  52.5 us (26%)
  starting transfers between devices  33.6 us (17%)
  between operations  14.3 us (7%)
  other arithmetic  9.92 us (5%)
  local copies, waits for them, and re-layouts  8.68 us (4%)
    ppermute x26, waiting for transfers between devices, swap(): return lax.ppermute(x, axis, [(i, i ^ mask) for i in range(n)])  52.5 us
    ppermute x26, starting transfers between devices, swap(): return lax.ppermute(x, axis, [(i, i ^ mask) for i in range(n)])  33.6 us
    pallas_call x1, Pallas kernels, act_grad(): pl.pallas_call(functools.partial(grad_kernel, side, 256), out_shape=(stru...  21.7 us
    pallas_call x1, Pallas kernels, weight_pieces(): pl.pallas_call(functools.partial(weight_kernel, side, extra, piece), out_...  20.3 us
    pallas_call x1, Pallas kernels, conv(): pl.pallas_call(functools.partial(conv_kernel, side, 256), out_shape=struc...  17.7 us
    pallas_call x2, Pallas kernels, shift_grad(): pl.pallas_call(functools.partial(shift_kernel, side), out_shape=(struct((...  8.51 us
    pallas_call x1, Pallas kernels, activate(): pl.pallas_call(functools.partial(act_kernel, side), out_shape=(struct((3,...  5.47 us
    unnamed x24, local copies, waits for them, and re-layouts  4.74 us
  transfers between devices with their start and end apart: 27, of which 10 were waited for; matrix products, arithmetic and copies ran while one was open for 6% of the time, Pallas kernels for 40%

commit v1 on v0

v1 whole, which is shorter than its diff:
```python
import functools
import math

import jax
import jax.numpy as jnp
from jax import lax
from jax.experimental import pallas as pl
from jax.experimental.pallas import tpu as pltpu
from jax.sharding import PartitionSpec as P

GROUPS = 16


epsilon = 1e-05

F32 = jnp.float32
BF16 = jnp.bfloat16
VMEM = pl.BlockSpec(memory_space=pltpu.VMEM)
SMEM = pl.BlockSpec(memory_space=pltpu.SMEM)
ANY = pl.BlockSpec(memory_space=pl.ANY)


def params(mib=24):
    return pltpu.CompilerParams(vmem_limit_bytes=mib * 1024 * 1024)


def call(kernel, operands, in_specs, tokens=(), **options):
    given = len(operands)

    def body(*refs):
        kernel(*refs[:given], *refs[given + len(tokens) :])

    return pl.pallas_call(
        body, in_specs=list(in_specs) + [ANY] * len(tokens), **options
    )(*operands, *tokens)


def struct(shape, dtype):
    return jax.ShapeDtypeStruct(shape, dtype)


def shifted_copies(x, side, out_ref, first):
    pixels = x.shape[0]
    column = lax.broadcasted_iota(jnp.int32, x.shape, 0) % side
    edge = jnp.zeros((side, x.shape[1]), BF16)
    for kx in range(3):
        move = (kx - 1) if first else (1 - kx)
        if move == 0:
            moved = x
        elif move == 1:
            moved = jnp.where(column == side - 1, 0.0, pltpu.roll(x, pixels - 1, 0))
        else:
            moved = jnp.where(column == 0, 0.0, pltpu.roll(x, 1, 0))
        out_ref[kx, 0:side, :] = edge
        out_ref[kx, side : side + pixels, :] = moved.astype(BF16)
        out_ref[kx, side + pixels : 2 * side + pixels, :] = edge


def shift_kernel(side, x_ref, out_ref, sum_ref):
    x = x_ref[...].astype(F32)
    sum_ref[...] = jnp.sum(x, axis=0, keepdims=True)
    shifted_copies(x, side, out_ref, False)


def shift_grad(x, side, tokens):
    pixels, chans = x.shape
    return call(
        functools.partial(shift_kernel, side),
        (x,),
        [VMEM],
        tokens,
        out_shape=(
            struct((3, pixels + 2 * side, chans), BF16),
            struct((1, chans), F32),
        ),
        out_specs=(VMEM, VMEM),
        compiler_params=params(),
        cost_estimate=pl.CostEstimate(
            flops=8 * x.size, bytes_accessed=8 * x.size, transcendentals=0
        ),
        name="shift_grad",
    )


def same_group(chans):
    size = chans // GROUPS
    a = lax.broadcasted_iota(jnp.int32, (chans, chans), 0) // size
    b = lax.broadcasted_iota(jnp.int32, (chans, chans), 1) // size
    return jnp.where(a == b, 1.0, 0.0).astype(F32)


def group_mean_of(column_sum, pixels):
    chans = column_sum.shape[1]
    count = pixels * (chans // GROUPS)
    total = jnp.dot(
        jnp.broadcast_to(column_sum, (8, chans)),
        same_group(chans),
        preferred_element_type=F32,
        precision=lax.Precision.HIGHEST,
    )
    return total[0:1] * (1.0 / count)


def stats_kernel(x_ref, out_ref):
    pixels = x_ref.shape[0]
    x = x_ref[...].astype(F32)
    mean = group_mean_of(jnp.sum(x, axis=0, keepdims=True), pixels)
    centered = x - mean
    var = group_mean_of(jnp.sum(centered * centered, axis=0, keepdims=True), pixels)
    out_ref[0:1, :] = mean
    out_ref[1:2, :] = lax.rsqrt(var + epsilon)


def stats(x):
    return pl.pallas_call(
        stats_kernel,
        out_shape=struct((2, x.shape[1]), F32),
        in_specs=[VMEM],
        out_specs=VMEM,
        compiler_params=params(),
        cost_estimate=pl.CostEstimate(
            flops=5 * x.size, bytes_accessed=2 * x.size, transcendentals=0
        ),
        name="norm_stats",
    )(x)


def activation(x_ref, stat_ref, vec_ref):
    mean, inv = stat_ref[0:1, :], stat_ref[1:2, :]
    gain = vec_ref[0:1, :].astype(F32)
    shift = vec_ref[1:2, :].astype(F32)
    pre = (x_ref[...].astype(F32) - mean) * inv * gain + shift
    return (pre / (1.0 + jnp.exp(-pre))).astype(BF16)


def act_kernel(x_ref, stat_ref, vec_ref, turned_ref):
    turned_ref[...] = activation(x_ref, stat_ref, vec_ref).T


def activate(x, stat, vecs, tokens):
    pixels, chans = x.shape
    return call(
        act_kernel,
        (x, stat, vecs),
        [VMEM, VMEM, VMEM],
        tokens,
        out_shape=struct((chans, pixels), BF16),
        out_specs=VMEM,
        compiler_params=params(),
        cost_estimate=pl.CostEstimate(
            flops=10 * x.size, bytes_accessed=4 * x.size, transcendentals=2 * x.size
        ),
        name="activate",
    )


def weight_blocks(side, extra, blocks, core, own_t, sib_t, own_g, sib_g, first, count, block_ref):
    chans, pixels = own_t.shape

    def tap_rows(ref, tap):
        start = pl.multiple_of((2 - tap // 3) * side, side)
        return ref[tap % 3, pl.ds(start, pixels), first : first + count]

    def product(low, high, tap):
        return jnp.dot(
            own_t[low:high, :], tap_rows(own_g, tap), preferred_element_type=F32
        ) + jnp.dot(sib_t[low:high, :], tap_rows(sib_g, tap), preferred_element_type=F32)

    for k in range(blocks):
        low, high = 2 * extra * k, 2 * extra * (k + 1)
        block_ref[0 : chans - low, :] = product(low, chans, 2 * k + core)
        block_ref[chans - low : chans + 2 * extra, :] = product(0, high, 2 * k + 1 + core)
        yield k


def weight_by_rep_kernel(
    side, extra, first, piece, place_ref, own_t, sib_t, own_g, sib_g,
    keep_ref, send0_ref, send1_ref, block_ref,
):
    chans = own_t.shape[0]
    r, z, core = place_ref[0], place_ref[1], place_ref[2]
    half, count = keep_ref.shape[2], keep_ref.shape[4]
    reps = 2 * keep_ref.shape[1]
    step = (chans + extra - piece) // (reps - 1)

    def rows_of(rel):
        at = pl.multiple_of(extra * core + step * (r ^ rel), 16)
        return block_ref[pl.ds(at, piece), :]

    for k in weight_blocks(
        side, extra, 2 * half, core, own_t, sib_t, own_g, sib_g, first, count, block_ref
    ):
        rel_z = k ^ z
        path, slot = rel_z // half, rel_z % half
        keep_ref[path, 0, slot] = rows_of(0)

        @pl.when(path == 0)
        def _():
            send0_ref[0, slot] = rows_of(1).astype(BF16)
            keep_ref[0, 1, slot] = rows_of(2)
            send0_ref[1, slot] = rows_of(3).astype(BF16)

        @pl.when(path == 1)
        def _():
            send1_ref[0, slot] = rows_of(2).astype(BF16)
            keep_ref[1, 1, slot] = rows_of(1)
            send1_ref[1, slot] = rows_of(3).astype(BF16)


def weight_call(kernel, out_shape, place, operands, extra, first, count, blocks, tokens, name):
    chans, pixels = operands[0].shape
    return call(
        kernel,
        (place,) + operands,
        [SMEM, VMEM, VMEM, VMEM, VMEM],
        tokens,
        out_shape=out_shape,
        out_specs=(VMEM,) * len(out_shape),
        scratch_shapes=[pltpu.VMEM((chans + 2 * extra, count), F32)],
        compiler_params=params(28),
        cost_estimate=pl.CostEstimate(
            flops=4 * blocks * (chans + 2 * extra) * pixels * count,
            bytes_accessed=20 * chans * pixels,
            transcendentals=0,
        ),
        name=name,
    )


def weight_by_rep(place, operands, side, blocks, extra, piece, first, count, tokens):
    half = blocks // 2
    out_shape = (
        struct((2, 2, half, piece, count), F32),
        struct((2, half, piece, count), BF16),
        struct((2, half, piece, count), BF16),
    )
    kernel = functools.partial(weight_by_rep_kernel, side, extra, first, piece)
    return weight_call(
        kernel, out_shape, place, operands, extra, first, count, blocks, tokens, "weight_grad_rep"
    )


def finish_kernel(*refs):
    total = refs[0][...]
    for ref in refs[1:-1]:
        total = total + ref[...].astype(F32)
    refs[-1][...] = total.astype(BF16)


def finish(terms, tokens):
    return call(
        finish_kernel,
        terms,
        [VMEM] * len(terms),
        tokens,
        out_shape=struct(terms[0].shape, BF16),
        out_specs=VMEM,
        compiler_params=params(8),
        cost_estimate=pl.CostEstimate(
            flops=4 * terms[0].size, bytes_accessed=12 * terms[0].size, transcendentals=0
        ),
        name="finish_sum",
    )


def rep_step_kernel(keep_ref, got0, got1, next0, next1):
    next0[...] = (keep_ref[0, 1] + got0[1].astype(F32)).astype(BF16)
    next1[...] = (keep_ref[1, 1] + got1[1].astype(F32)).astype(BF16)


def rep_step(keep, got0, got1, tokens):
    out = struct(keep.shape[2:], BF16)
    return call(
        rep_step_kernel,
        (keep, got0, got1),
        [VMEM] * 3,
        tokens,
        out_shape=(out, out),
        out_specs=(VMEM, VMEM),
        compiler_params=params(12),
        cost_estimate=pl.CostEstimate(
            flops=keep.size, bytes_accessed=4 * keep.size, transcendentals=0
        ),
        name="rep_step",
    )


def rep_sum_kernel(keep_ref, got0, got1, last0, last1, own_ref, *sends):
    half = keep_ref.shape[2]
    for i, out in enumerate((own_ref,) + sends):
        path, slot = i // half, i % half
        got, last = ((got0, last0), (got1, last1))[path]
        total = keep_ref[path, 0, slot] + got[0, slot].astype(F32) + last[slot].astype(F32)
        out[...] = total.astype(out.dtype)


def rep_sum(keep, got0, got1, last0, last1, tokens):
    half, piece, count = keep.shape[2:]
    return call(
        rep_sum_kernel,
        (keep, got0, got1, last0, last1),
        [VMEM] * 5,
        tokens,
        out_shape=(struct((piece, count), F32),)
        + (struct((piece, count), BF16),) * (2 * half - 1),
        out_specs=(VMEM,) * (2 * half),
        compiler_params=params(12),
        cost_estimate=pl.CostEstimate(
            flops=keep.size, bytes_accessed=4 * keep.size, transcendentals=0
        ),
        name="rep_sum",
    )


def prepare_kernel(side, x_ref, stat_ref, vec_ref, shifted_ref, slope_ref):
    mean, inv = stat_ref[0:1, :], stat_ref[1:2, :]
    gain = vec_ref[0:1, :].astype(F32)
    shift = vec_ref[1:2, :].astype(F32)
    pre = (x_ref[...].astype(F32) - mean) * inv * gain + shift
    grown = 1.0 + jnp.exp(-pre)
    shifted_copies((pre / grown).astype(BF16).astype(F32), side, shifted_ref, True)
    sig = 1.0 / grown
    slope_ref[...] = sig * (1.0 + pre * (1.0 - sig))


def prepare(x, stat, vecs, side, tokens):
    pixels, chans = x.shape
    return call(
        functools.partial(prepare_kernel, side),
        (x, stat, vecs),
        [VMEM] * 3,
        tokens,
        out_shape=(
            struct((3, pixels + 2 * side, chans), BF16),
            struct((pixels, chans), F32),
        ),
        out_specs=(VMEM, VMEM),
        compiler_params=params(16),
        cost_estimate=pl.CostEstimate(
            flops=20 * x.size, bytes_accessed=12 * x.size, transcendentals=2 * x.size
        ),
        name="prepare",
    )


def grad_kernel(
    side, chunk, g_ref, x_ref, slope_ref, stat_ref, vec_ref, weight, out_ref, sum_ref, scaled
):
    pixels, chans = x_ref.shape
    mean, inv = stat_ref[0:1, :], stat_ref[1:2, :]
    gain = vec_ref[0:1, :].astype(F32)
    sum_ref[...] = jnp.zeros_like(sum_ref)

    @pl.loop(0, pixels // chunk)
    def _(i):
        total = None
        for tap in range(9):
            start = pl.multiple_of(i * chunk + (2 - tap // 3) * side, side)
            part = lax.dot_general(
                g_ref[tap % 3, pl.ds(start, chunk), :],
                weight[tap * chans : (tap + 1) * chans, :],
                (((1,), (1,)), ((), ())),
                preferred_element_type=F32,
            )
            total = part if total is None else total + part
        rows = pl.ds(pl.multiple_of(i * chunk, chunk), chunk)
        normed = (x_ref[rows, :].astype(F32) - mean) * inv
        pre_grad = total * slope_ref[rows, :]
        sum_ref[0:1, :] += jnp.sum(pre_grad * normed, axis=0, keepdims=True)
        sum_ref[1:2, :] += jnp.sum(pre_grad, axis=0, keepdims=True)
        scaled[rows, :] = pre_grad * gain

    cross = group_mean_of(sum_ref[0:1, :] * gain, pixels)
    center = group_mean_of(sum_ref[1:2, :] * gain, pixels)

    @pl.loop(0, pixels // chunk)
    def _(i):
        rows = pl.ds(pl.multiple_of(i * chunk, chunk), chunk)
        normed = (x_ref[rows, :].astype(F32) - mean) * inv
        out_ref[rows, :] = ((scaled[rows, :] - center - normed * cross) * inv).astype(BF16)


def act_grad(shifted, x, slope, stat, vecs, weight, side, tokens):
    pixels, chans = x.shape
    outs = shifted.shape[2]
    return call(
        functools.partial(grad_kernel, side, 256),
        (shifted, x, slope, stat, vecs, weight),
        [VMEM] * 6,
        tokens,
        out_shape=(struct((pixels, chans), BF16), struct((2, chans), F32)),
        out_specs=(VMEM, VMEM),
        scratch_shapes=[pltpu.VMEM((pixels, chans), F32)],
        compiler_params=params(16),
        cost_estimate=pl.CostEstimate(
            flops=18 * chans * outs * pixels,
            bytes_accessed=18 * chans * outs + 12 * pixels * chans,
            transcendentals=0,
        ),
        name="act_grad",
    )


def conv_kernel(side, chunk, first, a_ref, vec_ref, weight, *rest):
    out_ref, token_ref, held, sems = rest[-4:]
    token_ref[...] = jnp.zeros_like(token_ref)
    chans = a_ref.shape[2]
    bias = vec_ref[2:3, :].astype(F32)
    chunks = held.shape[0] // chunk

    def copy(i):
        rows = pl.ds(pl.multiple_of(i * chunk, chunk), chunk)
        at = pl.ds(pl.multiple_of(first + i * chunk, chunk), chunk)
        return pltpu.make_async_copy(held.at[rows, :], out_ref.at[at, :], sems.at[i])

    for i in range(chunks):
        total = None
        for tap in range(9):
            start = first + i * chunk + (tap // 3) * side
            part = jnp.dot(
                a_ref[tap % 3, start : start + chunk, :],
                weight[tap * chans : (tap + 1) * chans, :],
                preferred_element_type=F32,
            )
            total = part if total is None else total + part
        held[i * chunk : (i + 1) * chunk, :] = (total + bias).astype(BF16)
        copy(i).start()
    for i in range(chunks):
        copy(i).wait()


def conv(shifted, vecs, weight, side, first, count, before, tokens):
    chans = shifted.shape[2]
    pixels = shifted.shape[1] - 2 * side
    outs = weight.shape[1]
    chunk = 256
    operands = (shifted, vecs, weight) + (() if before is None else (before,))
    return call(
        functools.partial(conv_kernel, side, chunk, first),
        operands,
        [VMEM] * 3 + [ANY] * (len(operands) - 3),
        tokens,
        out_shape=(struct((pixels, outs), BF16), struct((1, 128), F32)),
        out_specs=(ANY, VMEM),
        input_output_aliases={} if before is None else {3: 0},
        scratch_shapes=[
            pltpu.VMEM((count, outs), BF16),
            pltpu.SemaphoreType.DMA((count // chunk,)),
        ],
        compiler_params=params(16),
        cost_estimate=pl.CostEstimate(
            flops=18 * chans * outs * count,
            bytes_accessed=18 * chans * outs + 4 * count * chans,
            transcendentals=0,
        ),
        name="conv_forward",
    )


def join_kernel(scale, place_ref, p0, p1, p2, p3, out_ref):
    r = place_ref[0]
    pieces = (p0, p1, p2, p3)
    piece = p0.shape[0]
    step = (out_ref.shape[0] - piece) // (len(pieces) - 1)
    for q in range(len(pieces)):
        for rel, ref in enumerate(pieces):

            @pl.when((q ^ r) == rel)
            def _():
                out_ref[step * q : step * q + piece, :] = ref[...].astype(F32) * scale


def join(place, pieces, rows, scale, tokens):
    outs = pieces[0].shape[1]
    return call(
        functools.partial(join_kernel, scale),
        (place, *pieces),
        [SMEM] + [VMEM] * 4,
        tokens,
        out_shape=struct((rows, outs), F32),
        out_specs=VMEM,
        compiler_params=params(),
        cost_estimate=pl.CostEstimate(
            flops=rows * outs, bytes_accessed=6 * rows * outs, transcendentals=0
        ),
        name="join_pieces",
    )


def tree_sum(terms):
    while len(terms) > 1:
        terms = [terms[i] + terms[i + 1] for i in range(0, len(terms), 2)]
    return terms[0]


def add_kernel(*refs):
    refs[-1][...] = tree_sum([ref[...] for ref in refs[:-1]])


def add_small(terms, tokens):
    return call(
        add_kernel,
        terms,
        [VMEM] * len(terms),
        tokens,
        out_shape=struct(terms[0].shape, F32),
        out_specs=VMEM,
        compiler_params=params(2),
        cost_estimate=pl.CostEstimate(
            flops=4 * terms[0].size, bytes_accessed=16 * terms[0].size, transcendentals=0
        ),
        name="add_small",
    )


def swap(x, axis, mask):
    n = lax.axis_size(axis)
    return lax.ppermute(x, axis, [(i, i ^ mask) for i in range(n)])


def gather_small(x):
    at = lax.axis_index("fsdp")
    other = swap(x, "fsdp", 1)
    pair = jnp.where(at % 2 == 1, jnp.stack([other, x]), jnp.stack([x, other]))
    got = [pair] + [swap(pair, "fsdp", m) for m in range(2, lax.axis_size("fsdp"), 2)]
    mask = 1
    while mask < len(got):
        flip = (at // (2 * mask)) % 2 == 1
        got = [jnp.where(flip, got[i ^ mask], got[i]) for i in range(len(got))]
        mask *= 2
    return jnp.concatenate(got)


def sum_all(x, axis, masks):
    return tree_sum([x] + [swap(x, axis, m) for m in masks])


def local_fast(features, out_grad, conv_weight, conv_bias, norm_gain, norm_shift):
    side = features.shape[1]
    chans = features.shape[3]
    outs = out_grad.shape[3]
    pixels = side * side
    rows = conv_weight.shape[0]
    reps, shards = lax.axis_size("rep"), lax.axis_size("fsdp")
    r, f = lax.axis_index("rep"), lax.axis_index("fsdp")
    z, core = f // 2, f % 2
    extra = rows - chans
    piece = round_up(-(-rows // reps), 16)
    x = features.reshape(pixels, chans)
    g = out_grad.reshape(pixels, outs)
    place = jnp.stack([r, z, core]).astype(jnp.int32)

    weight = lax.all_gather(conv_weight, "fsdp", axis=0, tiled=True)
    small = gather_small(jnp.stack([norm_gain, norm_shift, conv_bias]))
    sib_g = swap(g, "fsdp", 1)

    stat = stats(x)
    vecs = jnp.transpose(small, (1, 0, 2)).reshape(3, chans)
    own_t = activate(x, stat, vecs, ())
    sib_t = swap(own_t, "fsdp", 1)
    own_shifted, bias_sum = shift_grad(g, side, (own_t,))
    sib_shifted, _ = shift_grad(sib_g, side, (own_t,))
    operands = (own_t, sib_t, own_shifted, sib_shifted)

    keep, send0, send1 = weight_by_rep(
        place, operands, side, shards // 2, extra, piece, 0, outs, ()
    )
    got0 = swap(send0, "rep", 1)
    got1 = swap(send1, "rep", 2)
    next0, next1 = rep_step(keep, got0, got1, ())
    last0 = swap(next0, "rep", 2)
    last1 = swap(next1, "rep", 1)
    own_sum, *sends = rep_sum(keep, got0, got1, last0, last1, ())
    got = [swap(a, "fsdp", 2 * (m + 1)) for m, a in enumerate(sends)]
    act_shifted, slope = prepare(x, stat, vecs, side, (keep,))
    in_grad, param_sums = act_grad(
        own_shifted, x, slope, stat, vecs, weight, side, (own_sum,)
    )
    done = finish((own_sum, *got), (param_sums,))
    pieces_done = [done] + [swap(done, "rep", m) for m in range(1, reps)]
    small_sums = jnp.concatenate([bias_sum, param_sums], axis=0)
    over_rep = [small_sums] + [swap(small_sums, "rep", m) for m in range(1, reps)]

    half = pixels // 2
    conv_out, token = conv(act_shifted, vecs, weight, side, 0, half, None, (done,))
    small_sums = add_small(over_rep, (token,))
    over_z = [small_sums] + [swap(small_sums, "fsdp", m) for m in range(2, shards, 2)]
    conv_out, token = conv(act_shifted, vecs, weight, side, half, half, conv_out, (small_sums,))
    small_sums = add_small(over_z, (token, *pieces_done[1:]))
    scale = 1.0 / math.sqrt(reps * shards * pixels)
    small_sums = sum_all(small_sums, "fsdp", (1,)) * scale
    weight_grad = join(place, pieces_done, rows, scale, (token,))
    share = outs // shards
    mine = lax.dynamic_slice_in_dim(small_sums.reshape(3, shards, share), f, 1, axis=1)
    mine = mine.reshape(3, share)
    return (
        conv_out.reshape(1, side, side, outs),
        in_grad.reshape(1, side, side, chans),
        weight_grad,
        mine[0],
        mine[1],
        mine[2],
    )


def round_up(n, m):
    return -(-n // m) * m


def fits(mesh_shape, images, rows, chans, outs, side):
    reps, shards = mesh_shape["rep"], mesh_shape["fsdp"]
    if images != reps * shards or reps != 2 * 2 or shards != 9 - 1:
        return False
    if chans != outs or rows * shards != 9 * chans or chans % 128 or side % 16 or outs < 3 * 128:
        return False
    extra, piece = rows - chans, round_up(-(-rows // reps), 16)
    step = (rows - piece) // (reps - 1)
    return (
        extra % 16 == 0
        and step * (reps - 1) == rows - piece
        and step % 16 == 0
        and piece % 32 == 0
    )


def local(features, out_grad, conv_weight, conv_bias, norm_gain, norm_shift):
    images_here = features.shape[0]
    side_cells = features.shape[1]
    channels = features.shape[3]
    pixels = side_cells * side_cells
    group_size = channels // GROUPS
    full_weight, bias_all, gain_all, shift_all = (
        lax.all_gather(conv_weight, "fsdp", axis=0, tiled=True),
        lax.all_gather(conv_bias, "fsdp", axis=0, tiled=True),
        lax.all_gather(norm_gain, "fsdp", axis=0, tiled=True),
        lax.all_gather(norm_shift, "fsdp", axis=0, tiled=True),
    )
    out_chans = full_weight.shape[1]
    values = features.astype(jnp.float32).reshape(images_here, pixels, GROUPS, group_size)
    group_mean = jnp.mean(values, axis=(1, 3), keepdims=True)
    centered = values - group_mean
    group_var = jnp.mean(centered * centered, axis=(1, 3), keepdims=True)
    inv_std = lax.rsqrt(group_var + epsilon)
    normed = centered * inv_std
    gain_cols = gain_all.astype(jnp.float32).reshape(1, 1, GROUPS, group_size)
    shift_cols = shift_all.astype(jnp.float32).reshape(1, 1, GROUPS, group_size)
    pre_act = normed * gain_cols + shift_cols
    activated = (
        jax.nn.silu(pre_act)
        .astype(jnp.bfloat16)
        .reshape(images_here, side_cells, side_cells, channels)
    )
    padded = jnp.pad(activated, ((0, 0), (1, 1), (1, 1), (0, 0)))
    conv_sum = jnp.zeros((images_here * pixels, out_chans), jnp.float32)
    taps_list = []
    for row_off in range(3):
        for col_off in range(3):
            tap_index = 3 * row_off + col_off
            tap_piece = padded[
                :, row_off : row_off + side_cells, col_off : col_off + side_cells, :
            ].reshape(images_here * pixels, channels)
            taps_list.append(tap_piece)
            conv_sum = conv_sum + jnp.dot(
                tap_piece,
                full_weight[tap_index * channels : (tap_index + 1) * channels],
                preferred_element_type=jnp.float32,
            )
    conv_out = (
        (conv_sum + bias_all.astype(jnp.float32)[None, :])
        .astype(jnp.bfloat16)
        .reshape(images_here, side_cells, side_cells, out_chans)
    )
    back_weight, back_gain = (
        lax.all_gather(conv_weight, "fsdp", axis=0, tiled=True),
        lax.all_gather(norm_gain, "fsdp", axis=0, tiled=True),
    )
    grad_rows = out_grad.reshape(images_here * pixels, out_chans)
    grad_padded = jnp.zeros((images_here, side_cells + 2, side_cells + 2, channels), jnp.float32)
    weight_list = []
    for row_off in range(3):
        for col_off in range(3):
            tap_index = 3 * row_off + col_off
            tap_rows = back_weight[tap_index * channels : (tap_index + 1) * channels]
            tap_grad = lax.dot_general(
                grad_rows, tap_rows, (((1,), (1,)), ((), ())), preferred_element_type=jnp.float32
            )
            grad_padded = grad_padded.at[
                :, row_off : row_off + side_cells, col_off : col_off + side_cells, :
            ].add(tap_grad.reshape(images_here, side_cells, side_cells, channels))
            weight_list.append(
                lax.dot_general(
                    taps_list[tap_index],
                    grad_rows,
                    (((0,), (0,)), ((), ())),
                    preferred_element_type=jnp.float32,
                )
            )
    act_grad = grad_padded[:, 1:-1, 1:-1, :].reshape(images_here, pixels, GROUPS, group_size)
    sig_pre = jax.nn.sigmoid(pre_act)
    pre_grad = act_grad * sig_pre * (1.0 + pre_act * (1.0 - sig_pre))
    norm_grad = pre_grad * back_gain.astype(jnp.float32).reshape(1, 1, GROUPS, group_size)
    grad_mean = jnp.mean(norm_grad, axis=(1, 3), keepdims=True)
    cross_mean = jnp.mean(norm_grad * normed, axis=(1, 3), keepdims=True)
    in_grad = (
        ((norm_grad - grad_mean - normed * cross_mean) * inv_std)
        .astype(jnp.bfloat16)
        .reshape(images_here, side_cells, side_cells, channels)
    )
    rep_size = lax.axis_size("rep")
    fsdp_size = lax.axis_size("fsdp")
    grad_scale = 1.0 / math.sqrt(images_here * rep_size * fsdp_size * pixels)
    weight_term = jnp.concatenate(weight_list, axis=0) * grad_scale
    bias_term = jnp.sum(grad_rows.astype(jnp.float32), axis=0) * grad_scale
    gain_term = jnp.sum(pre_grad * normed, axis=(0, 1)).reshape(channels) * grad_scale
    shift_term = jnp.sum(pre_grad, axis=(0, 1)).reshape(channels) * grad_scale
    shards = (
        lax.psum_scatter(weight_term, "fsdp", scatter_dimension=0, tiled=True),
        lax.psum_scatter(bias_term, "fsdp", scatter_dimension=0, tiled=True),
        lax.psum_scatter(gain_term, "fsdp", scatter_dimension=0, tiled=True),
        lax.psum_scatter(shift_term, "fsdp", scatter_dimension=0, tiled=True),
    )
    weight_grad, bias_grad, gain_grad, shift_grad = lax.psum(
        (shards[0], shards[1], shards[2], shards[3]), "rep"
    )
    return (conv_out, in_grad, weight_grad, bias_grad, gain_grad, shift_grad)


def solution(mesh):
    placed = (
        P(("rep", "fsdp"), None, None, None),
        P(("rep", "fsdp"), None, None, None),
        P("fsdp", None),
        P("fsdp"),
        P("fsdp"),
        P("fsdp"),
    )
    out_placed = (
        P(("rep", "fsdp"), None, None, None),
        P(("rep", "fsdp"), None, None, None),
        P("fsdp", None),
        P("fsdp"),
        P("fsdp"),
        P("fsdp"),
    )

    def run(features, out_grad, conv_weight, *vectors):
        images, side, _, chans = features.shape
        rows, outs = conv_weight.shape
        shape = dict(mesh.shape)
        fast = fits(shape, images, rows // shape["fsdp"], chans, outs, side)
        return jax.shard_map(
            local_fast if fast else local,
            mesh=mesh,
            in_specs=placed,
            out_specs=out_placed,
            check_vma=False,
        )(features, out_grad, conv_weight, *vectors)

    return run
```

time: 200 us -> 144 us (0.72)
  Pallas kernels: 80.6 us -> 53.5 us
  waiting for transfers between devices: 52.5 us -> 33.9 us
  other arithmetic: 9.92 us -> 1.53 us
  starting transfers between devices: 33.6 us -> 27.5 us
  local copies, waits for them, and re-layouts: 8.68 us -> 12.6 us
    pallas_call x7 -> x14, Pallas kernels: 76.6 us -> 51.5 us  [call(): pl.pallas_call(body, in_specs=list(in_specs) + [ANY] * len(tokens), **opt...]
    ppermute x26 -> x23, waiting for transfers between devices: 52.5 us -> 32.1 us  [swap(): return lax.ppermute(x, axis, [(i, i ^ mask) for i in range(n)])]
    unnamed x24 -> x22, local copies, waits for them, and re-layouts: 4.74 us -> 11.9 us
    ppermute x26 -> x23, starting transfers between devices: 33.6 us -> 27.4 us  [swap(): return lax.ppermute(x, axis, [(i, i ^ mask) for i in range(n)])]
    select_n x5 -> x2, other arithmetic: 4.47 us -> 0.03 us  [the longest x1 0.02 us: gather_small(): got = [jnp.where(flip, got[i ^ mask], got[i]) for i in range(len(got))]]
    pallas_call x2 -> x0, local copies, waits for them, and re-layouts: 2.57 us -> none  [weight_pieces(): pl.pallas_call(functools.partial(weight_kernel, side, extra, piece), out_...]
    convert_element_type x2 -> x0, other arithmetic: 2.2 us -> none  [the longest x1 2.07 us: local_fast(): next1 = (keep[1, :, 1] + got1[:, 1].astype(F32)).astype(BF16)]
    pallas_call x1, Pallas kernels: 3.98 us -> 1.97 us  [stats(): pl.pallas_call(stats_kernel, out_shape=struct((2, x.shape[1]), F32), in_s...]
  transfers between devices with their start and end apart: 27 -> 24, of which waited for: 10 -> 6; matrix products, arithmetic and copies ran while one was open for 6% -> 1% of each run, Pallas kernels for 40% -> 37%
where the time goes in v1:
time: 144 us; the launch traced here: 143 us
  Pallas kernels  53.5 us (37%)
  waiting for transfers between devices  33.9 us (24%)
  starting transfers between devices  27.5 us (19%)
  between operations  14.3 us (10%)
  local copies, waits for them, and re-layouts  12.6 us (9%)
  other arithmetic  1.53 us (1%)
    pallas_call x14, Pallas kernels, call(): pl.pallas_call(body, in_specs=list(in_specs) + [ANY] * len(tokens), **opt...  51.5 us
    ppermute x23, waiting for transfers between devices, swap(): return lax.ppermute(x, axis, [(i, i ^ mask) for i in range(n)])  32.1 us
    ppermute x23, starting transfers between devices, swap(): return lax.ppermute(x, axis, [(i, i ^ mask) for i in range(n)])  27.4 us
    unnamed x22, local copies, waits for them, and re-layouts  11.9 us
  transfers between devices with their start and end apart: 24, of which 6 were waited for; matrix products, arithmetic and copies ran while one was open for 1% of the time, Pallas kernels for 37%

profile of v1, /device:TPU:1, one launch (start us, length us, event | category | flops | bytes accessed | tf_op | source)
XLA Modules:
  0.0 143.3 jit_solution(7799338343079416228)
XLA Ops:
  9.9 4.5 %collective-permute-start.1 = (bf16[2,3,80]{2,1,0:T(4,128)(2,1)S(1)}, bf16[2,3,80]{2,1,0:T(4,128)(2,1)S(1)}, u32[]{:S(2)}, u32[]{:S(2)}) collective-permute-start(bf16[2,3,80]{2,1,0:T(4,128)(2,1)S(1)} %maximum_select_fusion), channel_id=1, source_target_pairs={{0,6},{1,7},{2,4},{3,5},{4,2},{5,3},{6,0},{7,1},{8,14},{9,15},{10,... | collective-permute-start | bytes 2888 | tf_op jit(solution)/shard_map/ppermute | solution.py:518
  16.1 2.0 %norm_stats.1.refs_1_.refs_3_ = f32[2,640]{1,0:T(2,128)S(1)} custom-call(bf16[1024,640]{1,0:T(8,128)(2,1)S(1)} %bitcast.21), custom_call_target="tpu_custom_call" | custom-call | flops 3276800 | bytes 1310720 | tf_op jit(solution)/shard_map/norm_stats/pallas_call | solution.py:115
  19.3 1.6 %collective-permute-start.4 = (bf16[640,1024]{1,0:T(8,128)(2,1)S(1)}, bf16[640,1024]{1,0:T(8,128)(2,1)}, u32[]{:S(2)}, u32[]{:S(2)}) collective-permute-start(bf16[640,1024]{1,0:T(8,128)(2,1)S(1)} %activate.1.refs_1_), channel_id=1, source_target_pairs={{0,1},{1,0},{2,3},{3,2},{4,5},{5,4},{6,7},{7,6},{8,9},{9,8},{10,11... | collective-permute-start | bytes 3932168 | tf_op jit(solution)/shard_map/ppermute | solution.py:518
  20.9 1.6 %copy-done.2 = bf16[1,32,32,640]{3,2,1,0:T(8,128)(2,1)S(1)} copy-done((bf16[1,32,32,640]{3,2,1,0:T(8,128)(2,1)S(1)}, bf16[1,32,32,640]{3,2,1,0:T(8,128)(2,1)}, u32[]{:S(2)}) %copy-start.2) | copy-done | bytes 1310744
  23.5 2.3 %shift_grad.3 = (bf16[3,1088,640]{2,1,0:T(8,128)(2,1)S(1)}, f32[1,640]{1,0:T(1,128)}) custom-call(bf16[1024,640]{1,0:T(8,128)(2,1)} %collective-permute-done.5.refs_0_, bf16[640,1024]{1,0:T(8,128)(2,1)S(1)} %activate.1.refs_1_), custom_call_target="tpu_custom_call" | custom-call | flops 5242880 | bytes 5242880 | tf_op jit(solution)/shard_map/shift_grad/pallas_call | solution.py:33
  25.8 15.0 %weight_grad_rep.1 = (f32[2,2,2,192,640]{4,3,2,1,0:T(8,128)S(1)}, bf16[2,2,192,640]{3,2,1,0:T(8,128)(2,1)S(1)}, bf16[2,2,192,640]{3,2,1,0:T(8,128)(2,1)S(1)}) custom-call(s32[3]{0:T(128)S(1)} %pad_add_fusion.refs_0_, bf16[640,1024]{1,0:T(8,128)(2,1)S(1)} %activate.1.refs_1_, bf16[640,1024]{1,0:T(8,128)(2,1)} %collective-permute-done.4.refs_2_, ...), custom_call_target="tpu_custom_call" | custom-call | flops 8388608000 | bytes 13107200 | tf_op jit(solution)/shard_map/weight_grad_rep/pallas_call | solution.py:33
  40.8 1.9 %copy-done.7 = bf16[3,1088,640]{2,1,0:T(8,128)(2,1)} copy-done((bf16[3,1088,640]{2,1,0:T(8,128)(2,1)}, bf16[3,1088,640]{2,1,0:T(8,128)(2,1)S(1)}, u32[]{:S(2)}) %copy-start.7) | copy-done | bytes 4177944
  45.3 20.9 %collective-permute-done.6.refs_1_ = bf16[2,2,192,640]{3,2,1,0:T(8,128)(2,1)S(1)} collective-permute-done((bf16[2,2,192,640]{3,2,1,0:T(8,128)(2,1)S(1)}, bf16[2,2,192,640]{3,2,1,0:T(8,128)(2,1)S(1)}, u32[]{:S(2)}, u32[]{:S(2)}) %collective-permute-start.6) | collective-permute-done | bytes 983072 | tf_op jit(solution)/shard_map/ppermute | solution.py:518
  69.2 2.0 %prepare.1 = (bf16[3,1088,640]{2,1,0:T(8,128)(2,1)S(1)}, f32[1024,640]{1,0:T(8,128)S(1)}) custom-call(bf16[1024,640]{1,0:T(8,128)(2,1)S(1)} %bitcast.23, f32[2,640]{1,0:T(2,128)S(1)} %norm_stats.1.refs_1_.refs_3_, bf16[3,640]{1,0:T(4,128)(2,1)S(1)} %reshape.38.refs_2_.refs_4_.refs_1_, f32[2,2,2,192,640]{4,3,2,1,0:T(8,128)S(1)} %get-tuple-element.28.refs_3_.refs_0_), custom_call_target="tpu_custom_call" | custom-call | flops 13107200 | bytes 7864320 | tf_op jit(solution)/shard_map/prepare/pallas_call | solution.py:33
  71.2 8.6 %collective-permute-done.8.refs_3_ = bf16[2,192,640]{2,1,0:T(8,128)(2,1)S(1)} collective-permute-done((bf16[2,192,640]{2,1,0:T(8,128)(2,1)S(1)}, bf16[2,192,640]{2,1,0:T(8,128)(2,1)S(1)}, u32[]{:S(2)}, u32[]{:S(2)}) %collective-permute-start.8) | collective-permute-done | bytes 491552 | tf_op jit(solution)/shard_map/ppermute | solution.py:518
  81.2 2.9 %collective-permute-start.11 = (bf16[192,640]{1,0:T(8,128)(2,1)S(1)}, bf16[192,640]{1,0:T(8,128)(2,1)S(1)}, u32[]{:S(2)}, u32[]{:S(2)}) collective-permute-start(bf16[192,640]{1,0:T(8,128)(2,1)S(1)} %get-tuple-element.36), channel_id=1, source_target_pairs={{0,4},{1,5},{2,6},{3,7},{4,0},{5,1},{6,2},{7,3},{8,12},{9,13},{10,... | collective-permute-start | bytes 737288 | tf_op jit(solution)/shard_map/ppermute | solution.py:518
  85.9 3.1 %copy-done.3 = bf16[5760,640]{1,0:T(8,128)(2,1)S(1)} copy-done((bf16[5760,640]{1,0:T(8,128)(2,1)S(1)}, bf16[5760,640]{1,0:T(8,128)(2,1)}, u32[]{:S(2)}) %copy-start.3) | copy-done | bytes 7372824
  89.0 2.2 %copy-done.8 = bf16[3,1088,640]{2,1,0:T(8,128)(2,1)S(1)} copy-done((bf16[3,1088,640]{2,1,0:T(8,128)(2,1)S(1)}, bf16[3,1088,640]{2,1,0:T(8,128)(2,1)}, u32[]{:S(2)}) %copy-start.8) | copy-done | bytes 4177944
  91.2 1.7 %copy-done.10 = f32[1024,640]{1,0:T(8,128)S(1)} copy-done((f32[1024,640]{1,0:T(8,128)S(1)}, f32[1024,640]{1,0:T(8,128)}, u32[]{:S(2)}) %copy-start.10) | copy-done | bytes 2621464
  93.0 15.3 %act_grad.1 = (bf16[1024,640]{1,0:T(8,128)(2,1)}, f32[2,640]{1,0:T(2,128)S(1)}) custom-call(bf16[3,1088,640]{2,1,0:T(8,128)(2,1)S(1)} %copy-done.8, bf16[1024,640]{1,0:T(8,128)(2,1)S(1)} %bitcast.24, f32[1024,640]{1,0:T(8,128)S(1)} %copy-done.10, f32[2,640]{1,0:T(2,128)S(1)} %norm_stats.1.refs_1_.refs_3_, ...), custom_call_target="tpu_custom_call" | custom-call | flops 7549747200 | bytes 15237120 | tf_op jit(solution)/shard_map/act_grad/pallas_call | solution.py:33
  108.3 1.4 collective-permute-start.13
  109.7 1.5 %collective-permute-start.14 = (f32[3,640]{1,0:T(4,128)S(1)}, f32[3,640]{1,0:T(4,128)S(1)}, u32[]{:S(2)}, u32[]{:S(2)}) collective-permute-start(f32[3,640]{1,0:T(4,128)S(1)} %pad_maximum_fusion.refs_0_), channel_id=1, source_target_pairs={{0,16},{8,24},{16,0},{24,8},{1,17},{9,25},{17,1},{25,9},{2,18},{10... | collective-permute-start | bytes 23048 | tf_op jit(solution)/shard_map/ppermute | solution.py:518
  111.3 6.1 %conv_forward.2 = (bf16[1024,640]{1,0:T(8,128)(2,1)}, f32[1,128]{1,0:T(1,128)S(1)}) custom-call(bf16[3,1088,640]{2,1,0:T(8,128)(2,1)S(1)} %copy-done.6, bf16[3,640]{1,0:T(4,128)(2,1)S(1)} %reshape.38.refs_2_.refs_4_.refs_1_, bf16[5760,640]{1,0:T(8,128)(2,1)S(1)} %copy-done.4, bf16[192,640]{1,0:T(8,128)(2,1)S(1)} %finish_sum.1.refs_3_.refs_1_), custom_call_target="tpu_custom_call" | custom-call | flops 3774873600 | bytes 8683520 | tf_op jit(solution)/shard_map/conv_forward/pallas_call | solution.py:33
  118.8 1.5 %collective-permute-start.17 = (bf16[192,640]{1,0:T(8,128)(2,1)S(1)}, bf16[192,640]{1,0:T(8,128)(2,1)S(1)}, u32[]{:S(2)}, u32[]{:S(2)}) collective-permute-start(bf16[192,640]{1,0:T(8,128)(2,1)S(1)} %finish_sum.1.refs_3_.refs_1_), channel_id=1, source_target_pairs={{0,16},{8,24},{16,0},{24,8},{1,17},{9,25},{17,1},{25,9},{2,18},{10... | collective-permute-start | bytes 737288 | tf_op jit(solution)/shard_map/ppermute | solution.py:518
  120.3 1.5 %collective-permute-start.20 = (f32[3,640]{1,0:T(4,128)S(1)}, f32[3,640]{1,0:T(4,128)S(1)}, u32[]{:S(2)}, u32[]{:S(2)}) collective-permute-start(f32[3,640]{1,0:T(4,128)S(1)} %add_small.2.refs_4_.refs_0_), channel_id=1, source_target_pairs={{0,4},{1,5},{2,6},{3,7},{4,0},{5,1},{6,2},{7,3},{8,12},{9,13},{10,... | collective-permute-start | bytes 23048 | tf_op jit(solution)/shard_map/ppermute | solution.py:518
  121.8 2.0 %collective-permute-start.21 = (f32[3,640]{1,0:T(4,128)S(1)}, f32[3,640]{1,0:T(4,128)S(1)}, u32[]{:S(2)}, u32[]{:S(2)}) collective-permute-start(f32[3,640]{1,0:T(4,128)S(1)} %add_small.2.refs_4_.refs_0_), channel_id=1, source_target_pairs={{0,6},{1,7},{2,4},{3,5},{4,2},{5,3},{6,0},{7,1},{8,14},{9,15},{10,... | collective-permute-start | bytes 23048 | tf_op jit(solution)/shard_map/ppermute | solution.py:518
  123.8 6.1 %conv_forward.3 = (bf16[1024,640]{1,0:T(8,128)(2,1)}, f32[1,128]{1,0:T(1,128)S(1)}) custom-call(bf16[3,1088,640]{2,1,0:T(8,128)(2,1)S(1)} %copy-done.6, bf16[3,640]{1,0:T(4,128)(2,1)S(1)} %reshape.38.refs_2_.refs_4_.refs_1_, bf16[5760,640]{1,0:T(8,128)(2,1)S(1)} %copy-done.4, ...), custom_call_target="tpu_custom_call", output_to_operand_aliasing={{0}: (3, {})} | custom-call | flops 3774873600 | bytes 8683520 | tf_op jit(solution)/shard_map/conv_forward/pallas_call | solution.py:33
  130.2 3.7 %collective-permute-start.22 = (f32[3,640]{1,0:T(4,128)S(1)}, f32[3,640]{1,0:T(4,128)S(1)}, u32[]{:S(2)}, u32[]{:S(2)}) collective-permute-start(f32[3,640]{1,0:T(4,128)S(1)} %add_small.3), channel_id=1, source_target_pairs={{0,1},{1,0},{2,3},{3,2},{4,5},{5,4},{6,7},{7,6},{8,9},{9,8},{10,11... | collective-permute-start | bytes 23048 | tf_op jit(solution)/shard_map/ppermute | solution.py:518
  133.9 2.0 %join_pieces.1 = f32[720,640]{1,0:T(8,128)} custom-call(s32[3]{0:T(128)S(1)} %pad_add_fusion.refs_0_, bf16[192,640]{1,0:T(8,128)(2,1)S(1)} %finish_sum.1.refs_3_.refs_1_, bf16[192,640]{1,0:T(8,128)(2,1)S(1)} %collective-permute-done.16.refs_2_.refs_5_, bf16[192,640]{1,0:T(8,128)(2,1)S(1)} %collective-permute-done.17.refs_3_.refs_6_, ...), custom_call_target="tpu_custom_call" | custom-call | flops 460800 | bytes 2764800 | tf_op jit(solution)/shard_map/join_pieces/pallas_call | solution.py:33
  (74 shorter events, 17.8 us)
Async XLA Ops:
  7.2 78.8 %all-gather.2.cloned.1.call-start = ((), (), s32[]{:S(2)}) async-start(), calls=%async_computation | async-start | bytes 8294400 | tf_op jit(solution)/shard_map/all_gather | solution.py:553
  8.6 1.3 collective-permute-start
  8.7 14.8 %collective-permute-start.5 = (bf16[1024,640]{1,0:T(8,128)(2,1)}, bf16[1024,640]{1,0:T(8,128)(2,1)}, u32[]{:S(2)}, u32[]{:S(2)}) collective-permute-start(bf16[1024,640]{1,0:T(8,128)(2,1)} %bitcast.25), channel_id=1, source_target_pairs={{0,1},{1,0},{2,3},{3,2},{4,5},{5,4},{6,7},{7,6},{8,9},{9,8},{10,11... | collective-permute-start | bytes 3932168 | tf_op jit(solution)/shard_map/ppermute | solution.py:518
  9.9 8.1 %collective-permute-start.1 = (bf16[2,3,80]{2,1,0:T(4,128)(2,1)S(1)}, bf16[2,3,80]{2,1,0:T(4,128)(2,1)S(1)}, u32[]{:S(2)}, u32[]{:S(2)}) collective-permute-start(bf16[2,3,80]{2,1,0:T(4,128)(2,1)S(1)} %maximum_select_fusion), channel_id=1, source_target_pairs={{0,6},{1,7},{2,4},{3,5},{4,2},{5,3},{6,0},{7,1},{8,14},{9,15},{10,... | collective-permute-start | bytes 2888 | tf_op jit(solution)/shard_map/ppermute | solution.py:518
  14.4 3.7 %collective-permute-start.2 = (bf16[2,3,80]{2,1,0:T(4,128)(2,1)S(1)}, bf16[2,3,80]{2,1,0:T(4,128)(2,1)S(1)}, u32[]{:S(2)}, u32[]{:S(2)}) collective-permute-start(bf16[2,3,80]{2,1,0:T(4,128)(2,1)S(1)} %maximum_select_fusion), channel_id=1, source_target_pairs={{0,4},{1,5},{2,6},{3,7},{4,0},{5,1},{6,2},{7,3},{8,12},{9,13},{10,... | collective-permute-start | bytes 2888 | tf_op jit(solution)/shard_map/ppermute | solution.py:518
  14.4 3.7 %collective-permute-start.3 = (bf16[2,3,80]{2,1,0:T(4,128)(2,1)S(1)}, bf16[2,3,80]{2,1,0:T(4,128)(2,1)S(1)}, u32[]{:S(2)}, u32[]{:S(2)}) collective-permute-start(bf16[2,3,80]{2,1,0:T(4,128)(2,1)S(1)} %maximum_select_fusion), channel_id=1, source_target_pairs={{0,2},{1,3},{2,0},{3,1},{4,6},{5,7},{6,4},{7,5},{8,10},{9,11},{10,... | collective-permute-start | bytes 2888 | tf_op jit(solution)/shard_map/ppermute | solution.py:518
  19.3 6.5 %collective-permute-start.4 = (bf16[640,1024]{1,0:T(8,128)(2,1)S(1)}, bf16[640,1024]{1,0:T(8,128)(2,1)}, u32[]{:S(2)}, u32[]{:S(2)}) collective-permute-start(bf16[640,1024]{1,0:T(8,128)(2,1)S(1)} %activate.1.refs_1_), channel_id=1, source_target_pairs={{0,1},{1,0},{2,3},{3,2},{4,5},{5,4},{6,7},{7,6},{8,9},{9,8},{10,11... | collective-permute-start | bytes 3932168 | tf_op jit(solution)/shard_map/ppermute | solution.py:518
  42.7 23.4 %collective-permute-start.6 = (bf16[2,2,192,640]{3,2,1,0:T(8,128)(2,1)S(1)}, bf16[2,2,192,640]{3,2,1,0:T(8,128)(2,1)S(1)}, u32[]{:S(2)}, u32[]{:S(2)}) collective-permute-start(bf16[2,2,192,640]{3,2,1,0:T(8,128)(2,1)S(1)} %get-tuple-element.30), channel_id=1, source_target_pairs={{0,8},{8,0},{16,24},{24,16},{1,9},{9,1},{17,25},{25,17},{2,10},{10... | collective-permute-start | bytes 2949128 | tf_op jit(solution)/shard_map/ppermute | solution.py:518
  44.0 23.4 %collective-permute-start.7 = (bf16[2,2,192,640]{3,2,1,0:T(8,128)(2,1)S(1)}, bf16[2,2,192,640]{3,2,1,0:T(8,128)(2,1)S(1)}, u32[]{:S(2)}, u32[]{:S(2)}) collective-permute-start(bf16[2,2,192,640]{3,2,1,0:T(8,128)(2,1)S(1)} %get-tuple-element.31), channel_id=1, source_target_pairs={{0,16},{8,24},{16,0},{24,8},{1,17},{9,25},{17,1},{25,9},{2,18},{10... | collective-permute-start | bytes 2949128 | tf_op jit(solution)/shard_map/ppermute | solution.py:518
  67.7 12.2 %collective-permute-start.8 = (bf16[2,192,640]{2,1,0:T(8,128)(2,1)S(1)}, bf16[2,192,640]{2,1,0:T(8,128)(2,1)S(1)}, u32[]{:S(2)}, u32[]{:S(2)}) collective-permute-start(bf16[2,192,640]{2,1,0:T(8,128)(2,1)S(1)} %get-tuple-element.32), channel_id=1, source_target_pairs={{0,16},{8,24},{16,0},{24,8},{1,17},{9,25},{17,1},{25,9},{2,18},{10... | collective-permute-start | bytes 1474568 | tf_op jit(solution)/shard_map/ppermute | solution.py:518
  69.0 11.8 %collective-permute-start.9 = (bf16[2,192,640]{2,1,0:T(8,128)(2,1)S(1)}, bf16[2,192,640]{2,1,0:T(8,128)(2,1)S(1)}, u32[]{:S(2)}, u32[]{:S(2)}) collective-permute-start(bf16[2,192,640]{2,1,0:T(8,128)(2,1)S(1)} %get-tuple-element.33), channel_id=1, source_target_pairs={{0,8},{8,0},{16,24},{24,16},{1,9},{9,1},{17,25},{25,17},{2,10},{10... | collective-permute-start | bytes 1474568 | tf_op jit(solution)/shard_map/ppermute | solution.py:518
  81.1 30.0 %collective-permute-start.10 = (bf16[192,640]{1,0:T(8,128)(2,1)S(1)}, bf16[192,640]{1,0:T(8,128)(2,1)S(1)}, u32[]{:S(2)}, u32[]{:S(2)}) collective-permute-start(bf16[192,640]{1,0:T(8,128)(2,1)S(1)} %get-tuple-element.35), channel_id=1, source_target_pairs={{0,2},{1,3},{2,0},{3,1},{4,6},{5,7},{6,4},{7,5},{8,10},{9,11},{10,... | collective-permute-start | bytes 737288 | tf_op jit(solution)/shard_map/ppermute | solution.py:518
  81.2 30.0 %collective-permute-start.11 = (bf16[192,640]{1,0:T(8,128)(2,1)S(1)}, bf16[192,640]{1,0:T(8,128)(2,1)S(1)}, u32[]{:S(2)}, u32[]{:S(2)}) collective-permute-start(bf16[192,640]{1,0:T(8,128)(2,1)S(1)} %get-tuple-element.36), channel_id=1, source_target_pairs={{0,4},{1,5},{2,6},{3,7},{4,0},{5,1},{6,2},{7,3},{8,12},{9,13},{10,... | collective-permute-start | bytes 737288 | tf_op jit(solution)/shard_map/ppermute | solution.py:518
  84.1 27.0 %collective-permute-start.12 = (bf16[192,640]{1,0:T(8,128)(2,1)S(1)}, bf16[192,640]{1,0:T(8,128)(2,1)S(1)}, u32[]{:S(2)}, u32[]{:S(2)}) collective-permute-start(bf16[192,640]{1,0:T(8,128)(2,1)S(1)} %get-tuple-element.37), channel_id=1, source_target_pairs={{0,6},{1,7},{2,4},{3,5},{4,2},{5,3},{6,0},{7,1},{8,14},{9,15},{10,... | collective-permute-start | bytes 737288 | tf_op jit(solution)/shard_map/ppermute | solution.py:518
  108.3 9.2 %collective-permute-start.13 = (f32[3,640]{1,0:T(4,128)S(1)}, f32[3,640]{1,0:T(4,128)S(1)}, u32[]{:S(2)}, u32[]{:S(2)}) collective-permute-start(f32[3,640]{1,0:T(4,128)S(1)} %pad_maximum_fusion.refs_0_), channel_id=1, source_target_pairs={{0,8},{8,0},{16,24},{24,16},{1,9},{9,1},{17,25},{25,17},{2,10},{10... | collective-permute-start | bytes 23048 | tf_op jit(solution)/shard_map/ppermute | solution.py:518
  109.7 7.8 %collective-permute-start.14 = (f32[3,640]{1,0:T(4,128)S(1)}, f32[3,640]{1,0:T(4,128)S(1)}, u32[]{:S(2)}, u32[]{:S(2)}) collective-permute-start(f32[3,640]{1,0:T(4,128)S(1)} %pad_maximum_fusion.refs_0_), channel_id=1, source_target_pairs={{0,16},{8,24},{16,0},{24,8},{1,17},{9,25},{17,1},{25,9},{2,18},{10... | collective-permute-start | bytes 23048 | tf_op jit(solution)/shard_map/ppermute | solution.py:518
  111.2 6.3 %collective-permute-start.15 = (f32[3,640]{1,0:T(4,128)S(1)}, f32[3,640]{1,0:T(4,128)S(1)}, u32[]{:S(2)}, u32[]{:S(2)}) collective-permute-start(f32[3,640]{1,0:T(4,128)S(1)} %pad_maximum_fusion.refs_0_), channel_id=1, source_target_pairs={{0,24},{8,16},{16,8},{24,0},{1,25},{9,17},{17,9},{25,1},{2,26},{10... | collective-permute-start | bytes 23048 | tf_op jit(solution)/shard_map/ppermute | solution.py:518
  117.5 4.3 %collective-permute-start.19 = (f32[3,640]{1,0:T(4,128)S(1)}, f32[3,640]{1,0:T(4,128)S(1)}, u32[]{:S(2)}, u32[]{:S(2)}) collective-permute-start(f32[3,640]{1,0:T(4,128)S(1)} %add_small.2.refs_4_.refs_0_), channel_id=1, source_target_pairs={{0,2},{1,3},{2,0},{3,1},{4,6},{5,7},{6,4},{7,5},{8,10},{9,11},{10,... | collective-permute-start | bytes 23048 | tf_op jit(solution)/shard_map/ppermute | solution.py:518
  117.6 12.3 %collective-permute-start.16 = (bf16[192,640]{1,0:T(8,128)(2,1)S(1)}, bf16[192,640]{1,0:T(8,128)(2,1)S(1)}, u32[]{:S(2)}, u32[]{:S(2)}) collective-permute-start(bf16[192,640]{1,0:T(8,128)(2,1)S(1)} %finish_sum.1.refs_3_.refs_1_), channel_id=1, source_target_pairs={{0,8},{8,0},{16,24},{24,16},{1,9},{9,1},{17,25},{25,17},{2,10},{10... | collective-permute-start | bytes 737288 | tf_op jit(solution)/shard_map/ppermute | solution.py:518
  118.8 11.1 %collective-permute-start.17 = (bf16[192,640]{1,0:T(8,128)(2,1)S(1)}, bf16[192,640]{1,0:T(8,128)(2,1)S(1)}, u32[]{:S(2)}, u32[]{:S(2)}) collective-permute-start(bf16[192,640]{1,0:T(8,128)(2,1)S(1)} %finish_sum.1.refs_3_.refs_1_), channel_id=1, source_target_pairs={{0,16},{8,24},{16,0},{24,8},{1,17},{9,25},{17,1},{25,9},{2,18},{10... | collective-permute-start | bytes 737288 | tf_op jit(solution)/shard_map/ppermute | solution.py:518
  120.3 9.9 %collective-permute-start.18 = (bf16[192,640]{1,0:T(8,128)(2,1)S(1)}, bf16[192,640]{1,0:T(8,128)(2,1)S(1)}, u32[]{:S(2)}, u32[]{:S(2)}) collective-permute-start(bf16[192,640]{1,0:T(8,128)(2,1)S(1)} %finish_sum.1.refs_3_.refs_1_), channel_id=1, source_target_pairs={{0,24},{8,16},{16,8},{24,0},{1,25},{9,17},{17,9},{25,1},{2,26},{10... | collective-permute-start | bytes 737288 | tf_op jit(solution)/shard_map/ppermute | solution.py:518
  120.3 9.6 %collective-permute-start.20 = (f32[3,640]{1,0:T(4,128)S(1)}, f32[3,640]{1,0:T(4,128)S(1)}, u32[]{:S(2)}, u32[]{:S(2)}) collective-permute-start(f32[3,640]{1,0:T(4,128)S(1)} %add_small.2.refs_4_.refs_0_), channel_id=1, source_target_pairs={{0,4},{1,5},{2,6},{3,7},{4,0},{5,1},{6,2},{7,3},{8,12},{9,13},{10,... | collective-permute-start | bytes 23048 | tf_op jit(solution)/shard_map/ppermute | solution.py:518
  121.8 8.1 %collective-permute-start.21 = (f32[3,640]{1,0:T(4,128)S(1)}, f32[3,640]{1,0:T(4,128)S(1)}, u32[]{:S(2)}, u32[]{:S(2)}) collective-permute-start(f32[3,640]{1,0:T(4,128)S(1)} %add_small.2.refs_4_.refs_0_), channel_id=1, source_target_pairs={{0,6},{1,7},{2,4},{3,5},{4,2},{5,3},{6,0},{7,1},{8,14},{9,15},{10,... | collective-permute-start | bytes 23048 | tf_op jit(solution)/shard_map/ppermute | solution.py:518
  130.2 5.7 %collective-permute-start.22 = (f32[3,640]{1,0:T(4,128)S(1)}, f32[3,640]{1,0:T(4,128)S(1)}, u32[]{:S(2)}, u32[]{:S(2)}) collective-permute-start(f32[3,640]{1,0:T(4,128)S(1)} %add_small.3), channel_id=1, source_target_pairs={{0,1},{1,0},{2,3},{3,2},{4,5},{5,4},{6,7},{7,6},{8,9},{9,8},{10,11... | collective-permute-start | bytes 23048 | tf_op jit(solution)/shard_map/ppermute | solution.py:518
  (11 other events, 70.6 us)
Sparse Core Ops, SparseCore 0:
  9.6 76.2 all-gather.1

commit v2 on v1

--- a/solution.py
+++ b/solution.py
@@ -240,26 +240,61 @@
     )
 
 
-def finish_kernel(*refs):
+def finish_kernel(bias_ref, param_ref, *refs):
+    out_ref = refs[-1]
     total = refs[0][...]
     for ref in refs[1:-1]:
         total = total + ref[...].astype(F32)
-    refs[-1][...] = total.astype(BF16)
-
-
-def finish(terms, tokens):
+    piece = total.shape[0]
+    out_ref[0:piece, :] = total.astype(BF16)
+    small = jnp.concatenate([bias_ref[...], param_ref[...]], axis=0)
+    high = small.astype(BF16).astype(F32)
+    middle = (small - high).astype(BF16).astype(F32)
+    parts = [high, middle, small - high - middle]
+    spare = out_ref.shape[0] - piece - 3 * small.shape[0]
+    parts.append(jnp.zeros((spare, small.shape[1]), F32))
+    out_ref[piece:, :] = jnp.concatenate(parts, axis=0).astype(BF16)
+
+
+def finish(terms, small):
+    piece, outs = terms[0].shape
     return call(
         finish_kernel,
-        terms,
-        [VMEM] * len(terms),
-        tokens,
-        out_shape=struct(terms[0].shape, BF16),
+        (*small, *terms),
+        [VMEM] * (2 + len(terms)),
+        out_shape=struct((piece + 16, outs), BF16),
         out_specs=VMEM,
         compiler_params=params(8),
         cost_estimate=pl.CostEstimate(
             flops=4 * terms[0].size, bytes_accessed=12 * terms[0].size, transcendentals=0
         ),
         name="finish_sum",
+    )
+
+
+def add_small_kernel(piece, *refs):
+    out_ref = refs[-1]
+    count = out_ref.shape[0]
+    terms = []
+    for ref in refs[:-1]:
+        rows = ref[piece:, :].astype(F32)
+        terms.append(rows[0:count] + rows[count : 2 * count] + rows[2 * count : 3 * count])
+    out_ref[...] = tree_sum(terms)
+
+
+def add_small_of(pieces, piece, count, tokens):
+    return call(
+        functools.partial(add_small_kernel, piece),
+        pieces,
+        [VMEM] * len(pieces),
+        tokens,
+        out_shape=struct((count, pieces[0].shape[1]), F32),
+        out_specs=VMEM,
+        compiler_params=params(4),
+        cost_estimate=pl.CostEstimate(
+            flops=4 * pieces[0].size, bytes_accessed=4 * pieces[0].size, transcendentals=0
+        ),
+        name="add_small_of",
     )
 
 
@@ -312,60 +347,65 @@
     )
 
 
-def prepare_kernel(side, x_ref, stat_ref, vec_ref, shifted_ref, slope_ref):
+def prepare_kernel(side, x_ref, stat_ref, vec_ref, shifted_ref):
+    act = activation(x_ref, stat_ref, vec_ref)
+    shifted_copies(act.astype(F32), side, shifted_ref, True)
+
+
+def prepare(x, stat, vecs, side, tokens):
+    pixels, chans = x.shape
+    return call(
+        functools.partial(prepare_kernel, side),
+        (x, stat, vecs),
+        [VMEM] * 3,
+        tokens,
+        out_shape=struct((3, pixels + 2 * side, chans), BF16),
+        out_specs=VMEM,
+        compiler_params=params(16),
+        cost_estimate=pl.CostEstimate(
+            flops=20 * x.size, bytes_accessed=8 * x.size, transcendentals=2 * x.size
+        ),
+        name="prepare",
+    )
+
+
+def grad_kernel(
+    side, chunk, raw_ref, x_ref, stat_ref, vec_ref, weight, out_ref, sum_ref, scaled, g_ref
+):
+    pixels, chans = x_ref.shape
+    edge = jnp.zeros((side, raw_ref.shape[1]), BF16)
+    g_ref[0:side, :] = edge
+    g_ref[side : side + pixels, :] = raw_ref[...]
+    g_ref[side + pixels :, :] = edge
+    column = lax.broadcasted_iota(jnp.int32, (chunk, chans), 0) % side
     mean, inv = stat_ref[0:1, :], stat_ref[1:2, :]
     gain = vec_ref[0:1, :].astype(F32)
     shift = vec_ref[1:2, :].astype(F32)
-    pre = (x_ref[...].astype(F32) - mean) * inv * gain + shift
-    grown = 1.0 + jnp.exp(-pre)
-    shifted_copies((pre / grown).astype(BF16).astype(F32), side, shifted_ref, True)
-    sig = 1.0 / grown
-    slope_ref[...] = sig * (1.0 + pre * (1.0 - sig))
-
-
-def prepare(x, stat, vecs, side, tokens):
-    pixels, chans = x.shape
-    return call(
-        functools.partial(prepare_kernel, side),
-        (x, stat, vecs),
-        [VMEM] * 3,
-        tokens,
-        out_shape=(
-            struct((3, pixels + 2 * side, chans), BF16),
-            struct((pixels, chans), F32),
-        ),
-        out_specs=(VMEM, VMEM),
-        compiler_params=params(16),
-        cost_estimate=pl.CostEstimate(
-            flops=20 * x.size, bytes_accessed=12 * x.size, transcendentals=2 * x.size
-        ),
-        name="prepare",
-    )
-
-
-def grad_kernel(
-    side, chunk, g_ref, x_ref, slope_ref, stat_ref, vec_ref, weight, out_ref, sum_ref, scaled
-):
-    pixels, chans = x_ref.shape
-    mean, inv = stat_ref[0:1, :], stat_ref[1:2, :]
-    gain = vec_ref[0:1, :].astype(F32)
     sum_ref[...] = jnp.zeros_like(sum_ref)
 
     @pl.loop(0, pixels // chunk)
     def _(i):
         total = None
-        for tap in range(9):
-            start = pl.multiple_of(i * chunk + (2 - tap // 3) * side, side)
+        for ky in range(3):
+            start = pl.multiple_of(i * chunk + (2 - ky) * side, side)
             part = lax.dot_general(
-                g_ref[tap % 3, pl.ds(start, chunk), :],
-                weight[tap * chans : (tap + 1) * chans, :],
+                g_ref[pl.ds(start, chunk), :],
+                weight[3 * ky * chans : 3 * (ky + 1) * chans, :],
                 (((1,), (1,)), ((), ())),
                 preferred_element_type=F32,
             )
             total = part if total is None else total + part
+        before, same, later = (total[:, kx * chans : (kx + 1) * chans] for kx in range(3))
+        total = (
+            same
+            + jnp.where(column == side - 1, 0.0, pltpu.roll(before, chunk - 1, 0))
+            + jnp.where(column == 0, 0.0, pltpu.roll(later, 1, 0))
+        )
         rows = pl.ds(pl.multiple_of(i * chunk, chunk), chunk)
         normed = (x_ref[rows, :].astype(F32) - mean) * inv
-        pre_grad = total * slope_ref[rows, :]
+        pre = normed * gain + shift
+        sig = 1.0 / (1.0 + jnp.exp(-pre))
+        pre_grad = total * sig * (1.0 + pre * (1.0 - sig))
         sum_ref[0:1, :] += jnp.sum(pre_grad * normed, axis=0, keepdims=True)
         sum_ref[1:2, :] += jnp.sum(pre_grad, axis=0, keepdims=True)
         scaled[rows, :] = pre_grad * gain
@@ -380,22 +420,25 @@
         out_ref[rows, :] = ((scaled[rows, :] - center - normed * cross) * inv).astype(BF16)
 
 
-def act_grad(shifted, x, slope, stat, vecs, weight, side, tokens):
+def act_grad(g, x, stat, vecs, weight, side, tokens):
     pixels, chans = x.shape
-    outs = shifted.shape[2]
-    return call(
-        functools.partial(grad_kernel, side, 256),
-        (shifted, x, slope, stat, vecs, weight),
-        [VMEM] * 6,
+    outs = g.shape[1]
+    return call(
+        functools.partial(grad_kernel, side, pixels // 2),
+        (g, x, stat, vecs, weight),
+        [VMEM] * 5,
         tokens,
         out_shape=(struct((pixels, chans), BF16), struct((2, chans), F32)),
         out_specs=(VMEM, VMEM),
-        scratch_shapes=[pltpu.VMEM((pixels, chans), F32)],
-        compiler_params=params(16),
+        scratch_shapes=[
+            pltpu.VMEM((pixels, chans), F32),
+            pltpu.VMEM((pixels + 2 * side, outs), BF16),
+        ],
+        compiler_params=params(24),
         cost_estimate=pl.CostEstimate(
             flops=18 * chans * outs * pixels,
             bytes_accessed=18 * chans * outs + 12 * pixels * chans,
-            transcendentals=0,
+            transcendentals=2 * pixels * chans,
         ),
         name="act_grad",
     )
@@ -414,15 +457,15 @@
         return pltpu.make_async_copy(held.at[rows, :], out_ref.at[at, :], sems.at[i])
 
     for i in range(chunks):
-        total = None
-        for tap in range(9):
-            start = first + i * chunk + (tap // 3) * side
-            part = jnp.dot(
-                a_ref[tap % 3, start : start + chunk, :],
-                weight[tap * chans : (tap + 1) * chans, :],
-                preferred_element_type=F32,
-            )
-            total = part if total is None else total + part
+        start = first + i * chunk
+        taps = jnp.concatenate(
+            [
+                a_ref[tap % 3, start + (tap // 3) * side : start + (tap // 3) * side + chunk, :]
+                for tap in range(9)
+            ],
+            axis=1,
+        )
+        total = jnp.dot(taps, weight[...], preferred_element_type=F32)
         held[i * chunk : (i + 1) * chunk, :] = (total + bias).astype(BF16)
         copy(i).start()
     for i in range(chunks):
@@ -457,23 +500,22 @@
     )
 
 
-def join_kernel(scale, place_ref, p0, p1, p2, p3, out_ref):
+def join_kernel(scale, piece, place_ref, p0, p1, p2, p3, out_ref):
     r = place_ref[0]
     pieces = (p0, p1, p2, p3)
-    piece = p0.shape[0]
     step = (out_ref.shape[0] - piece) // (len(pieces) - 1)
     for q in range(len(pieces)):
         for rel, ref in enumerate(pieces):
 
             @pl.when((q ^ r) == rel)
             def _():
-                out_ref[step * q : step * q + piece, :] = ref[...].astype(F32) * scale
-
-
-def join(place, pieces, rows, scale, tokens):
+                out_ref[step * q : step * q + piece, :] = ref[0:piece, :].astype(F32) * scale
+
+
+def join(place, pieces, rows, piece, scale, tokens):
     outs = pieces[0].shape[1]
     return call(
-        functools.partial(join_kernel, scale),
+        functools.partial(join_kernel, scale, piece),
         (place, *pieces),
         [SMEM] + [VMEM] * 4,
         tokens,
@@ -572,24 +614,22 @@
     last1 = swap(next1, "rep", 1)
     own_sum, *sends = rep_sum(keep, got0, got1, last0, last1, ())
     got = [swap(a, "fsdp", 2 * (m + 1)) for m, a in enumerate(sends)]
-    act_shifted, slope = prepare(x, stat, vecs, side, (keep,))
-    in_grad, param_sums = act_grad(
-        own_shifted, x, slope, stat, vecs, weight, side, (own_sum,)
-    )
-    done = finish((own_sum, *got), (param_sums,))
+    act_shifted = prepare(x, stat, vecs, side, (keep,))
+    in_grad, param_sums = act_grad(g, x, stat, vecs, weight, side, (own_sum,))
+    done = finish((own_sum, *got), (bias_sum, param_sums))
     pieces_done = [done] + [swap(done, "rep", m) for m in range(1, reps)]
-    small_sums = jnp.concatenate([bias_sum, param_sums], axis=0)
-    over_rep = [small_sums] + [swap(small_sums, "rep", m) for m in range(1, reps)]
-
-    half = pixels // 2
-    conv_out, token = conv(act_shifted, vecs, weight, side, 0, half, None, (done,))
-    small_sums = add_small(over_rep, (token,))
+
+    part = 3 * pixels // 4
+    conv_out, token = conv(act_shifted, vecs, weight, side, 0, part, None, (done,))
+    small_sums = add_small_of(pieces_done, piece, 3, (token,))
     over_z = [small_sums] + [swap(small_sums, "fsdp", m) for m in range(2, shards, 2)]
-    conv_out, token = conv(act_shifted, vecs, weight, side, half, half, conv_out, (small_sums,))
-    small_sums = add_small(over_z, (token, *pieces_done[1:]))
+    conv_out, token = conv(
+        act_shifted, vecs, weight, side, part, pixels - part, conv_out, (small_sums,)
+    )
+    small_sums = add_small(over_z, (token,))
     scale = 1.0 / math.sqrt(reps * shards * pixels)
     small_sums = sum_all(small_sums, "fsdp", (1,)) * scale
-    weight_grad = join(place, pieces_done, rows, scale, (token,))
+    weight_grad = join(place, pieces_done, rows, piece, scale, (token,))
     share = outs // shards
     mine = lax.dynamic_slice_in_dim(small_sums.reshape(3, shards, share), f, 1, axis=1)
     mine = mine.reshape(3, share)

time: 144 us -> 139 us (0.965)
  local copies, waits for them, and re-layouts: 12.6 us -> 8.74 us
  starting transfers between devices: 27.5 us -> 23.7 us
  waiting for transfers between devices: 33.9 us -> 37.4 us
    unnamed x22 -> x16, local copies, waits for them, and re-layouts: 11.9 us -> 8.03 us
    ppermute x23 -> x20, starting transfers between devices: 27.4 us -> 23.7 us  [swap(): return lax.ppermute(x, axis, [(i, i ^ mask) for i in range(n)])]
    ppermute x23 -> x20, waiting for transfers between devices: 32.1 us -> 34.2 us  [swap(): return lax.ppermute(x, axis, [(i, i ^ mask) for i in range(n)])]
  transfers between devices with their start and end apart: 24 -> 21, of which waited for: 6 -> 7; matrix products, arithmetic and copies ran while one was open for 1% -> 1% of each run, Pallas kernels for 37% -> 37%
where the time goes in v2:
time: 139 us
  Pallas kernels  53.3 us (38%)
  waiting for transfers between devices  37.4 us (27%)
  starting transfers between devices  23.7 us (17%)
  between operations  14.3 us (10%)
  local copies, waits for them, and re-layouts  8.74 us (6%)
  other arithmetic  1.52 us (1%)
    pallas_call x14, Pallas kernels, call(): pl.pallas_call(body, in_specs=list(in_specs) + [ANY] * len(tokens), **opt...  51.3 us
    ppermute x20, waiting for transfers between devices, swap(): return lax.ppermute(x, axis, [(i, i ^ mask) for i in range(n)])  34.2 us
    ppermute x20, starting transfers between devices, swap(): return lax.ppermute(x, axis, [(i, i ^ mask) for i in range(n)])  23.7 us
    unnamed x16, local copies, waits for them, and re-layouts  8.03 us
  transfers between devices with their start and end apart: 21, of which 7 were waited for; matrix products, arithmetic and copies ran while one was open for 1% of the time, Pallas kernels for 37%

profile of v2, /device:TPU:1, one launch (start us, length us, event | category | flops | bytes accessed | tf_op | source)
XLA Modules:
  0.0 139.0 jit_solution(17840967038817825707)
XLA Ops:
  9.9 4.5 %collective-permute-start.1 = (bf16[2,3,80]{2,1,0:T(4,128)(2,1)S(1)}, bf16[2,3,80]{2,1,0:T(4,128)(2,1)S(1)}, u32[]{:S(2)}, u32[]{:S(2)}) collective-permute-start(bf16[2,3,80]{2,1,0:T(4,128)(2,1)S(1)} %maximum_select_fusion), channel_id=1, source_target_pairs={{0,6},{1,7},{2,4},{3,5},{4,2},{5,3},{6,0},{7,1},{8,14},{9,15},{10,... | collective-permute-start | bytes 2888 | tf_op jit(solution)/shard_map/ppermute | solution.py:560
  16.1 2.0 %norm_stats.1.refs_1_.refs_2_ = f32[2,640]{1,0:T(2,128)S(1)} custom-call(bf16[1024,640]{1,0:T(8,128)(2,1)S(1)} %bitcast.21), custom_call_target="tpu_custom_call" | custom-call | flops 3276800 | bytes 1310720 | tf_op jit(solution)/shard_map/norm_stats/pallas_call | solution.py:115
  19.3 1.6 %collective-permute-start.4 = (bf16[640,1024]{1,0:T(8,128)(2,1)S(1)}, bf16[640,1024]{1,0:T(8,128)(2,1)}, u32[]{:S(2)}, u32[]{:S(2)}) collective-permute-start(bf16[640,1024]{1,0:T(8,128)(2,1)S(1)} %activate.1.refs_1_), channel_id=1, source_target_pairs={{0,1},{1,0},{2,3},{3,2},{4,5},{5,4},{6,7},{7,6},{8,9},{9,8},{10,11... | collective-permute-start | bytes 3932168 | tf_op jit(solution)/shard_map/ppermute | solution.py:560
  20.9 1.6 %copy-done.6 = bf16[1,32,32,640]{3,2,1,0:T(8,128)(2,1)S(1)} copy-done((bf16[1,32,32,640]{3,2,1,0:T(8,128)(2,1)S(1)}, bf16[1,32,32,640]{3,2,1,0:T(8,128)(2,1)}, u32[]{:S(2)}) %copy-start.6) | copy-done | bytes 1310744
  23.5 2.3 %shift_grad.3 = (bf16[3,1088,640]{2,1,0:T(8,128)(2,1)S(1)}, f32[1,640]{1,0:T(1,128)}) custom-call(bf16[1024,640]{1,0:T(8,128)(2,1)} %collective-permute-done.5.refs_0_, bf16[640,1024]{1,0:T(8,128)(2,1)S(1)} %activate.1.refs_1_), custom_call_target="tpu_custom_call" | custom-call | flops 5242880 | bytes 5242880 | tf_op jit(solution)/shard_map/shift_grad/pallas_call | solution.py:33
  25.8 15.0 %weight_grad_rep.1 = (f32[2,2,2,192,640]{4,3,2,1,0:T(8,128)S(1)}, bf16[2,2,192,640]{3,2,1,0:T(8,128)(2,1)S(1)}, bf16[2,2,192,640]{3,2,1,0:T(8,128)(2,1)S(1)}) custom-call(s32[3]{0:T(128)S(1)} %pad_add_fusion.refs_0_, bf16[640,1024]{1,0:T(8,128)(2,1)S(1)} %activate.1.refs_1_, bf16[640,1024]{1,0:T(8,128)(2,1)} %collective-permute-done.4.refs_2_, ...), custom_call_target="tpu_custom_call" | custom-call | flops 8388608000 | bytes 13107200 | tf_op jit(solution)/shard_map/weight_grad_rep/pallas_call | solution.py:33
  40.8 1.4 collective-permute-start.6
  43.4 20.9 %collective-permute-done.6.refs_1_ = bf16[2,2,192,640]{3,2,1,0:T(8,128)(2,1)S(1)} collective-permute-done((bf16[2,2,192,640]{3,2,1,0:T(8,128)(2,1)S(1)}, bf16[2,2,192,640]{3,2,1,0:T(8,128)(2,1)S(1)}, u32[]{:S(2)}, u32[]{:S(2)}) %collective-permute-start.6) | collective-permute-done | bytes 983072 | tf_op jit(solution)/shard_map/ppermute | solution.py:560
  67.3 1.7 %prepare.1.refs_0_ = bf16[3,1088,640]{2,1,0:T(8,128)(2,1)S(1)} custom-call(bf16[1024,640]{1,0:T(8,128)(2,1)S(1)} %bitcast.23, f32[2,640]{1,0:T(2,128)S(1)} %norm_stats.1.refs_1_.refs_2_, bf16[3,640]{1,0:T(4,128)(2,1)S(1)} %reshape.38.refs_2_.refs_3_.refs_1_, f32[2,2,2,192,640]{4,3,2,1,0:T(8,128)S(1)} %get-tuple-element.26.refs_3_.refs_0_), custom_call_target="tpu_custom_call" | custom-call | flops 13107200 | bytes 5242880 | tf_op jit(solution)/shard_map/prepare/pallas_call | solution.py:33
  69.0 2.0 %copy-done = bf16[3,1088,640]{2,1,0:T(8,128)(2,1)} copy-done((bf16[3,1088,640]{2,1,0:T(8,128)(2,1)}, bf16[3,1088,640]{2,1,0:T(8,128)(2,1)S(1)}, u32[]{:S(2)}) %copy-start) | copy-done | bytes 4177944
  71.0 7.0 %collective-permute-done.8.refs_3_ = bf16[2,192,640]{2,1,0:T(8,128)(2,1)S(1)} collective-permute-done((bf16[2,192,640]{2,1,0:T(8,128)(2,1)S(1)}, bf16[2,192,640]{2,1,0:T(8,128)(2,1)S(1)}, u32[]{:S(2)}, u32[]{:S(2)}) %collective-permute-start.8) | collective-permute-done | bytes 491552 | tf_op jit(solution)/shard_map/ppermute | solution.py:560
  79.9 2.9 %collective-permute-start.11 = (bf16[192,640]{1,0:T(8,128)(2,1)}, bf16[192,640]{1,0:T(8,128)(2,1)}, u32[]{:S(2)}, u32[]{:S(2)}) collective-permute-start(bf16[192,640]{1,0:T(8,128)(2,1)} %get-tuple-element.35), channel_id=1, source_target_pairs={{0,4},{1,5},{2,6},{3,7},{4,0},{5,1},{6,2},{7,3},{8,12},{9,13},{10,... | collective-permute-start | bytes 737288 | tf_op jit(solution)/shard_map/ppermute | solution.py:560
  83.5 2.5 %all-gather.2.cloned.1.call-done.refs_4_.refs_2_ = bf16[5760,640]{1,0:T(8,128)(2,1)} async-done(((bf16[720,640]{1,0:T(8,128)(2,1)}), bf16[5760,640]{1,0:T(8,128)(2,1)}) %all-gather.2.cloned.1.call-update) | async-done | bytes 7372816 | tf_op jit(solution)/shard_map/all_gather | solution.py:595
  86.0 3.1 %copy-done.4 = bf16[5760,640]{1,0:T(8,128)(2,1)S(1)} copy-done((bf16[5760,640]{1,0:T(8,128)(2,1)S(1)}, bf16[5760,640]{1,0:T(8,128)(2,1)}, u32[]{:S(2)}) %copy-start.4) | copy-done | bytes 7372824
  89.1 14.8 %act_grad.1 = (bf16[1024,640]{1,0:T(8,128)(2,1)}, f32[2,640]{1,0:T(2,128)S(1)}) custom-call(bf16[1024,640]{1,0:T(8,128)(2,1)S(1)} %bitcast.27, bf16[1024,640]{1,0:T(8,128)(2,1)S(1)} %bitcast.24, f32[2,640]{1,0:T(2,128)S(1)} %norm_stats.1.refs_1_.refs_2_, bf16[3,640]{1,0:T(4,128)(2,1)S(1)} %reshape.38.refs_2_.refs_3_.refs_1_, ...), custom_call_target="tpu_custom_call" | custom-call | flops 7549747200 | bytes 15237120 | tf_op jit(solution)/shard_map/act_grad/pallas_call | solution.py:33
  105.2 1.8 %collective-permute-start.13 = (bf16[208,640]{1,0:T(8,128)(2,1)S(1)}, bf16[208,640]{1,0:T(8,128)(2,1)S(1)}, u32[]{:S(2)}, u32[]{:S(2)}) collective-permute-start(bf16[208,640]{1,0:T(8,128)(2,1)S(1)} %finish_sum.1.refs_3_.refs_0_.refs_1_), channel_id=1, source_target_pairs={{0,8},{8,0},{16,24},{24,16},{1,9},{9,1},{17,25},{25,17},{2,10},{10... | collective-permute-start | bytes 798728 | tf_op jit(solution)/shard_map/ppermute | solution.py:560
  107.0 1.7 %collective-permute-start.14 = (bf16[208,640]{1,0:T(8,128)(2,1)S(1)}, bf16[208,640]{1,0:T(8,128)(2,1)S(1)}, u32[]{:S(2)}, u32[]{:S(2)}) collective-permute-start(bf16[208,640]{1,0:T(8,128)(2,1)S(1)} %finish_sum.1.refs_3_.refs_0_.refs_1_), channel_id=1, source_target_pairs={{0,16},{8,24},{16,0},{24,8},{1,17},{9,25},{17,1},{25,9},{2,18},{10... | collective-permute-start | bytes 798728 | tf_op jit(solution)/shard_map/ppermute | solution.py:560
  108.6 7.9 %conv_forward.2 = (bf16[1024,640]{1,0:T(8,128)(2,1)}, f32[1,128]{1,0:T(1,128)S(1)}) custom-call(bf16[3,1088,640]{2,1,0:T(8,128)(2,1)S(1)} %copy-done.1, bf16[3,640]{1,0:T(4,128)(2,1)S(1)} %reshape.38.refs_2_.refs_3_.refs_1_, bf16[5760,640]{1,0:T(8,128)(2,1)S(1)} %copy-done.5, bf16[208,640]{1,0:T(8,128)(2,1)S(1)} %finish_sum.1.refs_3_.refs_0_.refs_1_), custom_call_target="tpu_custom_call" | custom-call | flops 5662310400 | bytes 9338880 | tf_op jit(solution)/shard_map/conv_forward/pallas_call | solution.py:33
  116.5 3.0 %collective-permute-done.14.refs_2_.refs_3_ = bf16[208,640]{1,0:T(8,128)(2,1)S(1)} collective-permute-done((bf16[208,640]{1,0:T(8,128)(2,1)S(1)}, bf16[208,640]{1,0:T(8,128)(2,1)S(1)}, u32[]{:S(2)}, u32[]{:S(2)}) %collective-permute-start.14) | collective-permute-done | bytes 266272 | tf_op jit(solution)/shard_map/ppermute | solution.py:560
  120.7 1.5 %collective-permute-start.17 = (f32[3,640]{1,0:T(4,128)S(1)}, f32[3,640]{1,0:T(4,128)S(1)}, u32[]{:S(2)}, u32[]{:S(2)}) collective-permute-start(f32[3,640]{1,0:T(4,128)S(1)} %add_small_of.1.refs_4_.refs_0_), channel_id=1, source_target_pairs={{0,4},{1,5},{2,6},{3,7},{4,0},{5,1},{6,2},{7,3},{8,12},{9,13},{10,... | collective-permute-start | bytes 23048 | tf_op jit(solution)/shard_map/ppermute | solution.py:560
  122.2 2.1 %collective-permute-start.18 = (f32[3,640]{1,0:T(4,128)S(1)}, f32[3,640]{1,0:T(4,128)S(1)}, u32[]{:S(2)}, u32[]{:S(2)}) collective-permute-start(f32[3,640]{1,0:T(4,128)S(1)} %add_small_of.1.refs_4_.refs_0_), channel_id=1, source_target_pairs={{0,6},{1,7},{2,4},{3,5},{4,2},{5,3},{6,0},{7,1},{8,14},{9,15},{10,... | collective-permute-start | bytes 23048 | tf_op jit(solution)/shard_map/ppermute | solution.py:560
  124.2 3.2 %conv_forward.3 = (bf16[1024,640]{1,0:T(8,128)(2,1)}, f32[1,128]{1,0:T(1,128)S(1)}) custom-call(bf16[3,1088,640]{2,1,0:T(8,128)(2,1)S(1)} %copy-done.1, bf16[3,640]{1,0:T(4,128)(2,1)S(1)} %reshape.38.refs_2_.refs_3_.refs_1_, bf16[5760,640]{1,0:T(8,128)(2,1)S(1)} %copy-done.5, ...), custom_call_target="tpu_custom_call", output_to_operand_aliasing={{0}: (3, {})} | custom-call | flops 1887436800 | bytes 8028160 | tf_op jit(solution)/shard_map/conv_forward/pallas_call | solution.py:33
  127.5 2.0 %collective-permute-start.19 = (f32[3,640]{1,0:T(4,128)S(1)}, f32[3,640]{1,0:T(4,128)S(1)}, u32[]{:S(2)}, u32[]{:S(2)}) collective-permute-start(f32[3,640]{1,0:T(4,128)S(1)} %add_small.1), channel_id=1, source_target_pairs={{0,1},{1,0},{2,3},{3,2},{4,5},{5,4},{6,7},{7,6},{8,9},{9,8},{10,11... | collective-permute-start | bytes 23048 | tf_op jit(solution)/shard_map/ppermute | solution.py:560
  129.5 2.0 %join_pieces.1 = f32[720,640]{1,0:T(8,128)} custom-call(s32[3]{0:T(128)S(1)} %pad_add_fusion.refs_0_, bf16[208,640]{1,0:T(8,128)(2,1)S(1)} %finish_sum.1.refs_3_.refs_0_.refs_1_, bf16[208,640]{1,0:T(8,128)(2,1)S(1)} %collective-permute-done.13.refs_1_.refs_2_, bf16[208,640]{1,0:T(8,128)(2,1)S(1)} %collective-permute-done.14.refs_2_.refs_3_, ...), custom_call_target="tpu_custom_call" | custom-call | flops 460800 | bytes 2764800 | tf_op jit(solution)/shard_map/join_pieces/pallas_call | solution.py:33
  (61 shorter events, 16.5 us)
Async XLA Ops:
  7.2 78.8 %all-gather.2.cloned.1.call-start = ((), (), s32[]{:S(2)}) async-start(), calls=%async_computation | async-start | bytes 8294400 | tf_op jit(solution)/shard_map/all_gather | solution.py:595
  8.6 1.3 collective-permute-start
  8.7 14.8 %collective-permute-start.5 = (bf16[1024,640]{1,0:T(8,128)(2,1)}, bf16[1024,640]{1,0:T(8,128)(2,1)}, u32[]{:S(2)}, u32[]{:S(2)}) collective-permute-start(bf16[1024,640]{1,0:T(8,128)(2,1)} %bitcast.25), channel_id=1, source_target_pairs={{0,1},{1,0},{2,3},{3,2},{4,5},{5,4},{6,7},{7,6},{8,9},{9,8},{10,11... | collective-permute-start | bytes 3932168 | tf_op jit(solution)/shard_map/ppermute | solution.py:560
  9.9 8.1 %collective-permute-start.1 = (bf16[2,3,80]{2,1,0:T(4,128)(2,1)S(1)}, bf16[2,3,80]{2,1,0:T(4,128)(2,1)S(1)}, u32[]{:S(2)}, u32[]{:S(2)}) collective-permute-start(bf16[2,3,80]{2,1,0:T(4,128)(2,1)S(1)} %maximum_select_fusion), channel_id=1, source_target_pairs={{0,6},{1,7},{2,4},{3,5},{4,2},{5,3},{6,0},{7,1},{8,14},{9,15},{10,... | collective-permute-start | bytes 2888 | tf_op jit(solution)/shard_map/ppermute | solution.py:560
  14.4 3.7 %collective-permute-start.2 = (bf16[2,3,80]{2,1,0:T(4,128)(2,1)S(1)}, bf16[2,3,80]{2,1,0:T(4,128)(2,1)S(1)}, u32[]{:S(2)}, u32[]{:S(2)}) collective-permute-start(bf16[2,3,80]{2,1,0:T(4,128)(2,1)S(1)} %maximum_select_fusion), channel_id=1, source_target_pairs={{0,4},{1,5},{2,6},{3,7},{4,0},{5,1},{6,2},{7,3},{8,12},{9,13},{10,... | collective-permute-start | bytes 2888 | tf_op jit(solution)/shard_map/ppermute | solution.py:560
  14.4 3.7 %collective-permute-start.3 = (bf16[2,3,80]{2,1,0:T(4,128)(2,1)S(1)}, bf16[2,3,80]{2,1,0:T(4,128)(2,1)S(1)}, u32[]{:S(2)}, u32[]{:S(2)}) collective-permute-start(bf16[2,3,80]{2,1,0:T(4,128)(2,1)S(1)} %maximum_select_fusion), channel_id=1, source_target_pairs={{0,2},{1,3},{2,0},{3,1},{4,6},{5,7},{6,4},{7,5},{8,10},{9,11},{10,... | collective-permute-start | bytes 2888 | tf_op jit(solution)/shard_map/ppermute | solution.py:560
  19.3 6.5 %collective-permute-start.4 = (bf16[640,1024]{1,0:T(8,128)(2,1)S(1)}, bf16[640,1024]{1,0:T(8,128)(2,1)}, u32[]{:S(2)}, u32[]{:S(2)}) collective-permute-start(bf16[640,1024]{1,0:T(8,128)(2,1)S(1)} %activate.1.refs_1_), channel_id=1, source_target_pairs={{0,1},{1,0},{2,3},{3,2},{4,5},{5,4},{6,7},{7,6},{8,9},{9,8},{10,11... | collective-permute-start | bytes 3932168 | tf_op jit(solution)/shard_map/ppermute | solution.py:560
  40.8 23.5 %collective-permute-start.6 = (bf16[2,2,192,640]{3,2,1,0:T(8,128)(2,1)S(1)}, bf16[2,2,192,640]{3,2,1,0:T(8,128)(2,1)S(1)}, u32[]{:S(2)}, u32[]{:S(2)}) collective-permute-start(bf16[2,2,192,640]{3,2,1,0:T(8,128)(2,1)S(1)} %get-tuple-element.28), channel_id=1, source_target_pairs={{0,8},{8,0},{16,24},{24,16},{1,9},{9,1},{17,25},{25,17},{2,10},{10... | collective-permute-start | bytes 2949128 | tf_op jit(solution)/shard_map/ppermute | solution.py:560
  42.1 23.4 %collective-permute-start.7 = (bf16[2,2,192,640]{3,2,1,0:T(8,128)(2,1)S(1)}, bf16[2,2,192,640]{3,2,1,0:T(8,128)(2,1)S(1)}, u32[]{:S(2)}, u32[]{:S(2)}) collective-permute-start(bf16[2,2,192,640]{3,2,1,0:T(8,128)(2,1)S(1)} %get-tuple-element.29), channel_id=1, source_target_pairs={{0,16},{8,24},{16,0},{24,8},{1,17},{9,25},{17,1},{25,9},{2,18},{10... | collective-permute-start | bytes 2949128 | tf_op jit(solution)/shard_map/ppermute | solution.py:560
  65.8 12.2 %collective-permute-start.8 = (bf16[2,192,640]{2,1,0:T(8,128)(2,1)S(1)}, bf16[2,192,640]{2,1,0:T(8,128)(2,1)S(1)}, u32[]{:S(2)}, u32[]{:S(2)}) collective-permute-start(bf16[2,192,640]{2,1,0:T(8,128)(2,1)S(1)} %get-tuple-element.30), channel_id=1, source_target_pairs={{0,16},{8,24},{16,0},{24,8},{1,17},{9,25},{17,1},{25,9},{2,18},{10... | collective-permute-start | bytes 1474568 | tf_op jit(solution)/shard_map/ppermute | solution.py:560
  67.1 11.8 %collective-permute-start.9 = (bf16[2,192,640]{2,1,0:T(8,128)(2,1)S(1)}, bf16[2,192,640]{2,1,0:T(8,128)(2,1)S(1)}, u32[]{:S(2)}, u32[]{:S(2)}) collective-permute-start(bf16[2,192,640]{2,1,0:T(8,128)(2,1)S(1)} %get-tuple-element.31), channel_id=1, source_target_pairs={{0,8},{8,0},{16,24},{24,16},{1,9},{9,1},{17,25},{25,17},{2,10},{10... | collective-permute-start | bytes 1474568 | tf_op jit(solution)/shard_map/ppermute | solution.py:560
  71.0 15.0 %copy-start.7 = (bf16[1,32,32,640]{3,2,1,0:T(8,128)(2,1)S(1)}, bf16[1,32,32,640]{3,2,1,0:T(8,128)(2,1)}, u32[]{:S(2)}) copy-start(bf16[1,32,32,640]{3,2,1,0:T(8,128)(2,1)} %param.7) | copy-start | bytes 3932164
  79.9 24.0 %collective-permute-start.10 = (bf16[192,640]{1,0:T(8,128)(2,1)}, bf16[192,640]{1,0:T(8,128)(2,1)S(1)}, u32[]{:S(2)}, u32[]{:S(2)}) collective-permute-start(bf16[192,640]{1,0:T(8,128)(2,1)} %get-tuple-element.34), channel_id=1, source_target_pairs={{0,2},{1,3},{2,0},{3,1},{4,6},{5,7},{6,4},{7,5},{8,10},{9,11},{10,... | collective-permute-start | bytes 737288 | tf_op jit(solution)/shard_map/ppermute | solution.py:560
  79.9 24.0 %collective-permute-start.11 = (bf16[192,640]{1,0:T(8,128)(2,1)}, bf16[192,640]{1,0:T(8,128)(2,1)}, u32[]{:S(2)}, u32[]{:S(2)}) collective-permute-start(bf16[192,640]{1,0:T(8,128)(2,1)} %get-tuple-element.35), channel_id=1, source_target_pairs={{0,4},{1,5},{2,6},{3,7},{4,0},{5,1},{6,2},{7,3},{8,12},{9,13},{10,... | collective-permute-start | bytes 737288 | tf_op jit(solution)/shard_map/ppermute | solution.py:560
  82.8 21.1 %collective-permute-start.12 = (bf16[192,640]{1,0:T(8,128)(2,1)}, bf16[192,640]{1,0:T(8,128)(2,1)}, u32[]{:S(2)}, u32[]{:S(2)}) collective-permute-start(bf16[192,640]{1,0:T(8,128)(2,1)} %get-tuple-element.36), channel_id=1, source_target_pairs={{0,6},{1,7},{2,4},{3,5},{4,2},{5,3},{6,0},{7,1},{8,14},{9,15},{10,... | collective-permute-start | bytes 737288 | tf_op jit(solution)/shard_map/ppermute | solution.py:560
  89.1 19.5 %copy-start.1 = (bf16[3,1088,640]{2,1,0:T(8,128)(2,1)S(1)}, bf16[3,1088,640]{2,1,0:T(8,128)(2,1)}, u32[]{:S(2)}) copy-start(bf16[3,1088,640]{2,1,0:T(8,128)(2,1)} %copy-done) | copy-start | bytes 12533764
  89.1 19.5 %copy-start.5 = (bf16[5760,640]{1,0:T(8,128)(2,1)S(1)}, bf16[5760,640]{1,0:T(8,128)(2,1)}, u32[]{:S(2)}) copy-start(bf16[5760,640]{1,0:T(8,128)(2,1)} %all-gather.2.cloned.1.call-done.refs_4_.refs_2_) | copy-start | bytes 22118404
  105.2 11.4 %collective-permute-start.13 = (bf16[208,640]{1,0:T(8,128)(2,1)S(1)}, bf16[208,640]{1,0:T(8,128)(2,1)S(1)}, u32[]{:S(2)}, u32[]{:S(2)}) collective-permute-start(bf16[208,640]{1,0:T(8,128)(2,1)S(1)} %finish_sum.1.refs_3_.refs_0_.refs_1_), channel_id=1, source_target_pairs={{0,8},{8,0},{16,24},{24,16},{1,9},{9,1},{17,25},{25,17},{2,10},{10... | collective-permute-start | bytes 798728 | tf_op jit(solution)/shard_map/ppermute | solution.py:560
  107.0 12.6 %collective-permute-start.14 = (bf16[208,640]{1,0:T(8,128)(2,1)S(1)}, bf16[208,640]{1,0:T(8,128)(2,1)S(1)}, u32[]{:S(2)}, u32[]{:S(2)}) collective-permute-start(bf16[208,640]{1,0:T(8,128)(2,1)S(1)} %finish_sum.1.refs_3_.refs_0_.refs_1_), channel_id=1, source_target_pairs={{0,16},{8,24},{16,0},{24,8},{1,17},{9,25},{17,1},{25,9},{2,18},{10... | collective-permute-start | bytes 798728 | tf_op jit(solution)/shard_map/ppermute | solution.py:560
  108.6 12.0 %collective-permute-start.15 = (bf16[208,640]{1,0:T(8,128)(2,1)S(1)}, bf16[208,640]{1,0:T(8,128)(2,1)S(1)}, u32[]{:S(2)}, u32[]{:S(2)}) collective-permute-start(bf16[208,640]{1,0:T(8,128)(2,1)S(1)} %finish_sum.1.refs_3_.refs_0_.refs_1_), channel_id=1, source_target_pairs={{0,24},{8,16},{16,8},{24,0},{1,25},{9,17},{17,9},{25,1},{2,26},{10... | collective-permute-start | bytes 798728 | tf_op jit(solution)/shard_map/ppermute | solution.py:560
  120.6 6.8 %collective-permute-start.16 = (f32[3,640]{1,0:T(4,128)S(1)}, f32[3,640]{1,0:T(4,128)S(1)}, u32[]{:S(2)}, u32[]{:S(2)}) collective-permute-start(f32[3,640]{1,0:T(4,128)S(1)} %add_small_of.1.refs_4_.refs_0_), channel_id=1, source_target_pairs={{0,2},{1,3},{2,0},{3,1},{4,6},{5,7},{6,4},{7,5},{8,10},{9,11},{10,... | collective-permute-start | bytes 23048 | tf_op jit(solution)/shard_map/ppermute | solution.py:560
  120.7 6.8 %collective-permute-start.17 = (f32[3,640]{1,0:T(4,128)S(1)}, f32[3,640]{1,0:T(4,128)S(1)}, u32[]{:S(2)}, u32[]{:S(2)}) collective-permute-start(f32[3,640]{1,0:T(4,128)S(1)} %add_small_of.1.refs_4_.refs_0_), channel_id=1, source_target_pairs={{0,4},{1,5},{2,6},{3,7},{4,0},{5,1},{6,2},{7,3},{8,12},{9,13},{10,... | collective-permute-start | bytes 23048 | tf_op jit(solution)/shard_map/ppermute | solution.py:560
  122.2 5.3 %collective-permute-start.18 = (f32[3,640]{1,0:T(4,128)S(1)}, f32[3,640]{1,0:T(4,128)S(1)}, u32[]{:S(2)}, u32[]{:S(2)}) collective-permute-start(f32[3,640]{1,0:T(4,128)S(1)} %add_small_of.1.refs_4_.refs_0_), channel_id=1, source_target_pairs={{0,6},{1,7},{2,4},{3,5},{4,2},{5,3},{6,0},{7,1},{8,14},{9,15},{10,... | collective-permute-start | bytes 23048 | tf_op jit(solution)/shard_map/ppermute | solution.py:560
  127.5 4.0 %collective-permute-start.19 = (f32[3,640]{1,0:T(4,128)S(1)}, f32[3,640]{1,0:T(4,128)S(1)}, u32[]{:S(2)}, u32[]{:S(2)}) collective-permute-start(f32[3,640]{1,0:T(4,128)S(1)} %add_small.1), channel_id=1, source_target_pairs={{0,1},{1,0},{2,3},{3,2},{4,5},{5,4},{6,7},{7,6},{8,9},{9,8},{10,11... | collective-permute-start | bytes 23048 | tf_op jit(solution)/shard_map/ppermute | solution.py:560
  (5 other events, 10.2 us)
Sparse Core Ops, SparseCore 0:
  9.6 76.3 all-gather.1

commit v3 on v2

--- a/solution.py
+++ b/solution.py
@@ -82,31 +82,28 @@
     )
 
 
-def same_group(chans):
+def group_means(sums, pixels):
+    chans = sums.shape[1]
     size = chans // GROUPS
-    a = lax.broadcasted_iota(jnp.int32, (chans, chans), 0) // size
-    b = lax.broadcasted_iota(jnp.int32, (chans, chans), 1) // size
-    return jnp.where(a == b, 1.0, 0.0).astype(F32)
-
-
-def group_mean_of(column_sum, pixels):
-    chans = column_sum.shape[1]
-    count = pixels * (chans // GROUPS)
-    total = jnp.dot(
-        jnp.broadcast_to(column_sum, (8, chans)),
-        same_group(chans),
-        preferred_element_type=F32,
-        precision=lax.Precision.HIGHEST,
-    )
-    return total[0:1] * (1.0 / count)
+    lanes = round_up(GROUPS, 128)
+    channel = lax.broadcasted_iota(jnp.int32, (chans, lanes), 0)
+    first = lax.broadcasted_iota(jnp.int32, (chans, lanes), 1) * size
+    member = jnp.where((channel >= first) & (channel < first + size), 1.0, 0.0).astype(F32)
+    exact = {"preferred_element_type": F32, "precision": lax.Precision.HIGHEST}
+    total = jnp.dot(sums, member, **exact)
+    spread = lax.dot_general(total, member, (((1,), (1,)), ((), ())), **exact)
+    return spread * (1.0 / (pixels * size))
 
 
 def stats_kernel(x_ref, out_ref):
     pixels = x_ref.shape[0]
     x = x_ref[...].astype(F32)
-    mean = group_mean_of(jnp.sum(x, axis=0, keepdims=True), pixels)
+    spread = (8, x.shape[1])
+    column_sum = jnp.sum(x, axis=0, keepdims=True)
+    mean = group_means(jnp.broadcast_to(column_sum, spread), pixels)[0:1]
     centered = x - mean
-    var = group_mean_of(jnp.sum(centered * centered, axis=0, keepdims=True), pixels)
+    column_sum = jnp.sum(centered * centered, axis=0, keepdims=True)
+    var = group_means(jnp.broadcast_to(column_sum, spread), pixels)[0:1]
     out_ref[0:1, :] = mean
     out_ref[1:2, :] = lax.rsqrt(var + epsilon)
 
@@ -369,6 +366,39 @@
     )
 
 
+def arrange_kernel(source, out_ref, sems):
+    rows, outs = out_ref.shape[0] // 3, source.shape[1]
+    copies = [
+        pltpu.make_async_copy(
+            source.at[pl.ds(tap * rows, rows), :],
+            out_ref.at[pl.ds(tap % 3 * rows, rows), pl.ds(tap // 3 * outs, outs)],
+            sems.at[tap],
+        )
+        for tap in range(9)
+    ]
+    for c in copies:
+        c.start()
+    for c in copies:
+        c.wait()
+
+
+def arrange(weight):
+    rows, outs = weight.shape
+    return call(
+        arrange_kernel,
+        (weight,),
+        [ANY],
+        out_shape=struct((rows // 3, 3 * outs), BF16),
+        out_specs=VMEM,
+        scratch_shapes=[pltpu.SemaphoreType.DMA((9,))],
+        compiler_params=params(44),
+        cost_estimate=pl.CostEstimate(
+            flops=0, bytes_accessed=4 * weight.size, transcendentals=0
+        ),
+        name="arrange_weight",
+    )
+
+
 def grad_kernel(
     side, chunk, raw_ref, x_ref, stat_ref, vec_ref, weight, out_ref, sum_ref, scaled, g_ref
 ):
@@ -385,16 +415,16 @@
 
     @pl.loop(0, pixels // chunk)
     def _(i):
-        total = None
-        for ky in range(3):
-            start = pl.multiple_of(i * chunk + (2 - ky) * side, side)
-            part = lax.dot_general(
-                g_ref[pl.ds(start, chunk), :],
-                weight[3 * ky * chans : 3 * (ky + 1) * chans, :],
-                (((1,), (1,)), ((), ())),
-                preferred_element_type=F32,
-            )
-            total = part if total is None else total + part
+        rows_of = [
+            g_ref[pl.ds(pl.multiple_of(i * chunk + (2 - ky) * side, side), chunk), :]
+            for ky in range(3)
+        ]
+        total = lax.dot_general(
+            jnp.concatenate(rows_of, axis=1),
+            weight[...],
+            (((1,), (1,)), ((), ())),
+            preferred_element_type=F32,
+        )
         before, same, later = (total[:, kx * chans : (kx + 1) * chans] for kx in range(3))
         total = (
             same
@@ -410,12 +440,13 @@
         sum_ref[1:2, :] += jnp.sum(pre_grad, axis=0, keepdims=True)
         scaled[rows, :] = pre_grad * gain
 
-    cross = group_mean_of(sum_ref[0:1, :] * gain, pixels)
-    center = group_mean_of(sum_ref[1:2, :] * gain, pixels)
-
-    @pl.loop(0, pixels // chunk)
+    rest = jnp.zeros((6, chans), F32)
+    means = group_means(jnp.concatenate([sum_ref[...] * gain, rest], axis=0), pixels)
+    cross, center = means[0:1], means[1:2]
+
+    @pl.loop(0, pixels // 128)
     def _(i):
-        rows = pl.ds(pl.multiple_of(i * chunk, chunk), chunk)
+        rows = pl.ds(pl.multiple_of(i * 128, 128), 128)
         normed = (x_ref[rows, :].astype(F32) - mean) * inv
         out_ref[rows, :] = ((scaled[rows, :] - center - normed * cross) * inv).astype(BF16)
 
@@ -444,53 +475,46 @@
     )
 
 
-def conv_kernel(side, chunk, first, a_ref, vec_ref, weight, *rest):
-    out_ref, token_ref, held, sems = rest[-4:]
+def conv_kernel(side, first, a_ref, vec_ref, weight, *rest):
+    out_ref, token_ref, held, sem = rest[-4:]
     token_ref[...] = jnp.zeros_like(token_ref)
-    chans = a_ref.shape[2]
-    bias = vec_ref[2:3, :].astype(F32)
-    chunks = held.shape[0] // chunk
-
-    def copy(i):
-        rows = pl.ds(pl.multiple_of(i * chunk, chunk), chunk)
-        at = pl.ds(pl.multiple_of(first + i * chunk, chunk), chunk)
-        return pltpu.make_async_copy(held.at[rows, :], out_ref.at[at, :], sems.at[i])
-
-    for i in range(chunks):
-        start = first + i * chunk
-        taps = jnp.concatenate(
-            [
-                a_ref[tap % 3, start + (tap // 3) * side : start + (tap // 3) * side + chunk, :]
-                for tap in range(9)
-            ],
-            axis=1,
-        )
-        total = jnp.dot(taps, weight[...], preferred_element_type=F32)
-        held[i * chunk : (i + 1) * chunk, :] = (total + bias).astype(BF16)
-        copy(i).start()
-    for i in range(chunks):
-        copy(i).wait()
+    count, outs = held.shape
+    pixels = out_ref.shape[0]
+    low, high = max(0, first - side), min(pixels, first + count + side)
+    shifted = jnp.concatenate([a_ref[kx, side + low : side + high, :] for kx in range(3)], axis=1)
+    parts = jnp.dot(shifted, weight[...], preferred_element_type=F32)
+    total = None
+    for ky in range(3):
+        begin = first + (ky - 1) * side
+        end = begin + count
+        part = parts[max(begin, 0) - low : min(end, pixels) - low, ky * outs : (ky + 1) * outs]
+        edge = jnp.zeros((side, outs), F32)
+        if begin < 0:
+            part = jnp.concatenate([edge, part], axis=0)
+        if end > pixels:
+            part = jnp.concatenate([part, edge], axis=0)
+        total = part if total is None else total + part
+    held[...] = (total + vec_ref[2:3, :].astype(F32)).astype(BF16)
+    copy = pltpu.make_async_copy(held, out_ref.at[pl.ds(first, count), :], sem)
+    copy.start()
+    copy.wait()
 
 
 def conv(shifted, vecs, weight, side, first, count, before, tokens):
     chans = shifted.shape[2]
     pixels = shifted.shape[1] - 2 * side
-    outs = weight.shape[1]
-    chunk = 256
+    outs = weight.shape[1] // 3
     operands = (shifted, vecs, weight) + (() if before is None else (before,))
     return call(
-        functools.partial(conv_kernel, side, chunk, first),
+        functools.partial(conv_kernel, side, first),
         operands,
         [VMEM] * 3 + [ANY] * (len(operands) - 3),
         tokens,
         out_shape=(struct((pixels, outs), BF16), struct((1, 128), F32)),
         out_specs=(ANY, VMEM),
         input_output_aliases={} if before is None else {3: 0},
-        scratch_shapes=[
-            pltpu.VMEM((count, outs), BF16),
-            pltpu.SemaphoreType.DMA((count // chunk,)),
-        ],
-        compiler_params=params(16),
+        scratch_shapes=[pltpu.VMEM((count, outs), BF16), pltpu.SemaphoreType.DMA],
+        compiler_params=params(24),
         cost_estimate=pl.CostEstimate(
             flops=18 * chans * outs * count,
             bytes_accessed=18 * chans * outs + 4 * count * chans,
@@ -615,11 +639,12 @@
     own_sum, *sends = rep_sum(keep, got0, got1, last0, last1, ())
     got = [swap(a, "fsdp", 2 * (m + 1)) for m, a in enumerate(sends)]
     act_shifted = prepare(x, stat, vecs, side, (keep,))
+    weight = arrange(weight)
     in_grad, param_sums = act_grad(g, x, stat, vecs, weight, side, (own_sum,))
     done = finish((own_sum, *got), (bias_sum, param_sums))
     pieces_done = [done] + [swap(done, "rep", m) for m in range(1, reps)]
 
-    part = 3 * pixels // 4
+    part = 7 * pixels // 8
     conv_out, token = conv(act_shifted, vecs, weight, side, 0, part, None, (done,))
     small_sums = add_small_of(pieces_done, piece, 3, (token,))
     over_z = [small_sums] + [swap(small_sums, "fsdp", m) for m in range(2, shards, 2)]

time: 139 us -> 137 us (0.986)
  local copies, waits for them, and re-layouts: 8.74 us -> 5.65 us
  Pallas kernels: 53.3 us -> 54.8 us
    unnamed x16 -> x12, local copies, waits for them, and re-layouts: 8.03 us -> 4.94 us
    pallas_call x14 -> x15, Pallas kernels: 51.3 us -> 52.8 us  [call(): pl.pallas_call(body, in_specs=list(in_specs) + [ANY] * len(tokens), **opt...]
  transfers between devices with their start and end apart: 21 -> 21, of which waited for: 7 -> 7; matrix products, arithmetic and copies ran while one was open for 1% -> 1% of each run, Pallas kernels for 37% -> 39%
where the time goes in v3:
time: 137 us
  Pallas kernels  54.8 us (40%)
  waiting for transfers between devices  36.2 us (26%)
  starting transfers between devices  24.5 us (18%)
  between operations  14.3 us (10%)
  local copies, waits for them, and re-layouts  5.65 us (4%)
  other arithmetic  1.52 us (1%)
    pallas_call x15, Pallas kernels, call(): pl.pallas_call(body, in_specs=list(in_specs) + [ANY] * len(tokens), **opt...  52.8 us
    ppermute x20, waiting for transfers between devices, swap(): return lax.ppermute(x, axis, [(i, i ^ mask) for i in range(n)])  33.1 us
    ppermute x20, starting transfers between devices, swap(): return lax.ppermute(x, axis, [(i, i ^ mask) for i in range(n)])  24.4 us
    unnamed x12, local copies, waits for them, and re-layouts  4.94 us
  transfers between devices with their start and end apart: 21, of which 7 were waited for; matrix products, arithmetic and copies ran while one was open for 1% of the time, Pallas kernels for 39%

profile of v3, /device:TPU:1, one launch (start us, length us, event | category | flops | bytes accessed | tf_op | source)
XLA Modules:
  0.0 136.9 jit_solution(5673613797598190187)
XLA Ops:
  9.9 4.5 %collective-permute-start.1 = (bf16[2,3,80]{2,1,0:T(4,128)(2,1)S(1)}, bf16[2,3,80]{2,1,0:T(4,128)(2,1)S(1)}, u32[]{:S(2)}, u32[]{:S(2)}) collective-permute-start(bf16[2,3,80]{2,1,0:T(4,128)(2,1)S(1)} %maximum_select_fusion), channel_id=1, source_target_pairs={{0,6},{1,7},{2,4},{3,5},{4,2},{5,3},{6,0},{7,1},{8,14},{9,15},{10,... | collective-permute-start | bytes 2888 | tf_op jit(solution)/shard_map/ppermute | solution.py:584
  16.1 2.0 %norm_stats.1.refs_1_.refs_2_ = f32[2,640]{1,0:T(2,128)S(1)} custom-call(bf16[1024,640]{1,0:T(8,128)(2,1)S(1)} %bitcast.21), custom_call_target="tpu_custom_call" | custom-call | flops 3276800 | bytes 1310720 | tf_op jit(solution)/shard_map/norm_stats/pallas_call | solution.py:112
  19.4 1.5 %collective-permute-start.4 = (bf16[640,1024]{1,0:T(8,128)(2,1)S(1)}, bf16[640,1024]{1,0:T(8,128)(2,1)}, u32[]{:S(2)}, u32[]{:S(2)}) collective-permute-start(bf16[640,1024]{1,0:T(8,128)(2,1)S(1)} %activate.1.refs_1_), channel_id=1, source_target_pairs={{0,1},{1,0},{2,3},{3,2},{4,5},{5,4},{6,7},{7,6},{8,9},{9,8},{10,11... | collective-permute-start | bytes 3932168 | tf_op jit(solution)/shard_map/ppermute | solution.py:584
  20.9 1.6 %copy-done.4 = bf16[1,32,32,640]{3,2,1,0:T(8,128)(2,1)S(1)} copy-done((bf16[1,32,32,640]{3,2,1,0:T(8,128)(2,1)S(1)}, bf16[1,32,32,640]{3,2,1,0:T(8,128)(2,1)}, u32[]{:S(2)}) %copy-start.4) | copy-done | bytes 1310744
  23.5 2.3 %shift_grad.3 = (bf16[3,1088,640]{2,1,0:T(8,128)(2,1)S(1)}, f32[1,640]{1,0:T(1,128)}) custom-call(bf16[1024,640]{1,0:T(8,128)(2,1)} %collective-permute-done.5.refs_0_, bf16[640,1024]{1,0:T(8,128)(2,1)S(1)} %activate.1.refs_1_), custom_call_target="tpu_custom_call" | custom-call | flops 5242880 | bytes 5242880 | tf_op jit(solution)/shard_map/shift_grad/pallas_call | solution.py:33
  25.8 15.0 %weight_grad_rep.1 = (f32[2,2,2,192,640]{4,3,2,1,0:T(8,128)S(1)}, bf16[2,2,192,640]{3,2,1,0:T(8,128)(2,1)S(1)}, bf16[2,2,192,640]{3,2,1,0:T(8,128)(2,1)S(1)}) custom-call(s32[3]{0:T(128)S(1)} %pad_add_fusion.refs_0_, bf16[640,1024]{1,0:T(8,128)(2,1)S(1)} %activate.1.refs_1_, bf16[640,1024]{1,0:T(8,128)(2,1)} %collective-permute-done.4.refs_2_, ...), custom_call_target="tpu_custom_call" | custom-call | flops 8388608000 | bytes 13107200 | tf_op jit(solution)/shard_map/weight_grad_rep/pallas_call | solution.py:33
  40.8 1.4 collective-permute-start.6
  43.4 20.9 %collective-permute-done.6.refs_1_ = bf16[2,2,192,640]{3,2,1,0:T(8,128)(2,1)S(1)} collective-permute-done((bf16[2,2,192,640]{3,2,1,0:T(8,128)(2,1)S(1)}, bf16[2,2,192,640]{3,2,1,0:T(8,128)(2,1)S(1)}, u32[]{:S(2)}, u32[]{:S(2)}) %collective-permute-start.6) | collective-permute-done | bytes 983072 | tf_op jit(solution)/shard_map/ppermute | solution.py:584
  65.8 1.3 collective-permute-start.8
  67.4 1.7 %prepare.1.refs_0_ = bf16[3,1088,640]{2,1,0:T(8,128)(2,1)S(1)} custom-call(bf16[1024,640]{1,0:T(8,128)(2,1)S(1)} %bitcast.23, f32[2,640]{1,0:T(2,128)S(1)} %norm_stats.1.refs_1_.refs_2_, bf16[3,640]{1,0:T(4,128)(2,1)S(1)} %reshape.38.refs_2_.refs_3_.refs_1_, f32[2,2,2,192,640]{4,3,2,1,0:T(8,128)S(1)} %get-tuple-element.26.refs_3_.refs_0_), custom_call_target="tpu_custom_call" | custom-call | flops 13107200 | bytes 5242880 | tf_op jit(solution)/shard_map/prepare/pallas_call | solution.py:33
  69.0 2.0 %copy-done = bf16[3,1088,640]{2,1,0:T(8,128)(2,1)} copy-done((bf16[3,1088,640]{2,1,0:T(8,128)(2,1)}, bf16[3,1088,640]{2,1,0:T(8,128)(2,1)S(1)}, u32[]{:S(2)}) %copy-start) | copy-done | bytes 4177944
  71.0 6.9 %collective-permute-done.8.refs_3_ = bf16[2,192,640]{2,1,0:T(8,128)(2,1)S(1)} collective-permute-done((bf16[2,192,640]{2,1,0:T(8,128)(2,1)S(1)}, bf16[2,192,640]{2,1,0:T(8,128)(2,1)S(1)}, u32[]{:S(2)}, u32[]{:S(2)}) %collective-permute-start.8) | collective-permute-done | bytes 491552 | tf_op jit(solution)/shard_map/ppermute | solution.py:584
  80.0 3.2 %collective-permute-start.11 = (bf16[192,640]{1,0:T(8,128)(2,1)}, bf16[192,640]{1,0:T(8,128)(2,1)}, u32[]{:S(2)}, u32[]{:S(2)}) collective-permute-start(bf16[192,640]{1,0:T(8,128)(2,1)} %get-tuple-element.35), channel_id=1, source_target_pairs={{0,4},{1,5},{2,6},{3,7},{4,0},{5,1},{6,2},{7,3},{8,12},{9,13},{10,... | collective-permute-start | bytes 737288 | tf_op jit(solution)/shard_map/ppermute | solution.py:584
  83.5 2.4 %all-gather.2.cloned.1.call-done.refs_0_ = bf16[5760,640]{1,0:T(8,128)(2,1)} async-done(((bf16[720,640]{1,0:T(8,128)(2,1)}), bf16[5760,640]{1,0:T(8,128)(2,1)}) %all-gather.2.cloned.1.call-update) | async-done | bytes 7372816 | tf_op jit(solution)/shard_map/all_gather | solution.py:619
  85.9 3.2 %arrange_weight.1.refs_4_.refs_2_ = bf16[1920,1920]{1,0:T(8,128)(2,1)S(1)} custom-call(bf16[5760,640]{1,0:T(8,128)(2,1)} %all-gather.2.cloned.1.call-done.refs_0_), custom_call_target="tpu_custom_call" | custom-call | bytes 14745600 | tf_op jit(solution)/shard_map/arrange_weight/pallas_call | solution.py:33
  89.1 13.0 %act_grad.1 = (bf16[1024,640]{1,0:T(8,128)(2,1)}, f32[2,640]{1,0:T(2,128)S(1)}) custom-call(bf16[1024,640]{1,0:T(8,128)(2,1)S(1)} %bitcast.27, bf16[1024,640]{1,0:T(8,128)(2,1)S(1)} %bitcast.24, f32[2,640]{1,0:T(2,128)S(1)} %norm_stats.1.refs_1_.refs_2_, bf16[3,640]{1,0:T(4,128)(2,1)S(1)} %reshape.38.refs_2_.refs_3_.refs_1_, ...), custom_call_target="tpu_custom_call" | custom-call | flops 7549747200 | bytes 15237120 | tf_op jit(solution)/shard_map/act_grad/pallas_call | solution.py:33
  103.3 1.7 %collective-permute-start.13 = (bf16[208,640]{1,0:T(8,128)(2,1)S(1)}, bf16[208,640]{1,0:T(8,128)(2,1)S(1)}, u32[]{:S(2)}, u32[]{:S(2)}) collective-permute-start(bf16[208,640]{1,0:T(8,128)(2,1)S(1)} %finish_sum.1.refs_3_.refs_0_.refs_1_), channel_id=1, source_target_pairs={{0,8},{8,0},{16,24},{24,16},{1,9},{9,1},{17,25},{25,17},{2,10},{10... | collective-permute-start | bytes 798728 | tf_op jit(solution)/shard_map/ppermute | solution.py:584
  105.0 1.7 %collective-permute-start.14 = (bf16[208,640]{1,0:T(8,128)(2,1)S(1)}, bf16[208,640]{1,0:T(8,128)(2,1)S(1)}, u32[]{:S(2)}, u32[]{:S(2)}) collective-permute-start(bf16[208,640]{1,0:T(8,128)(2,1)S(1)} %finish_sum.1.refs_3_.refs_0_.refs_1_), channel_id=1, source_target_pairs={{0,16},{8,24},{16,0},{24,8},{1,17},{9,25},{17,1},{25,9},{2,18},{10... | collective-permute-start | bytes 798728 | tf_op jit(solution)/shard_map/ppermute | solution.py:584
  106.8 9.0 %conv_forward.2 = (bf16[1024,640]{1,0:T(8,128)(2,1)}, f32[1,128]{1,0:T(1,128)S(1)}) custom-call(bf16[3,1088,640]{2,1,0:T(8,128)(2,1)S(1)} %copy-done.1, bf16[3,640]{1,0:T(4,128)(2,1)S(1)} %reshape.38.refs_2_.refs_3_.refs_1_, bf16[1920,1920]{1,0:T(8,128)(2,1)S(1)} %arrange_weight.1.refs_4_.refs_2_, bf16[208,640]{1,0:T(8,128)(2,1)S(1)} %finish_sum.1.refs_3_.refs_0_.refs_1_), custom_call_target="tpu_custom_call" | custom-call | flops 6606028800 | bytes 9666560 | tf_op jit(solution)/shard_map/conv_forward/pallas_call | solution.py:33
  115.8 1.8 %collective-permute-done.14.refs_2_.refs_3_ = bf16[208,640]{1,0:T(8,128)(2,1)S(1)} collective-permute-done((bf16[208,640]{1,0:T(8,128)(2,1)S(1)}, bf16[208,640]{1,0:T(8,128)(2,1)S(1)}, u32[]{:S(2)}, u32[]{:S(2)}) %collective-permute-start.14) | collective-permute-done | bytes 266272 | tf_op jit(solution)/shard_map/ppermute | solution.py:584
  119.2 3.3 %collective-permute-start.18 = (f32[3,640]{1,0:T(4,128)S(1)}, f32[3,640]{1,0:T(4,128)S(1)}, u32[]{:S(2)}, u32[]{:S(2)}) collective-permute-start(f32[3,640]{1,0:T(4,128)S(1)} %add_small_of.1.refs_4_.refs_0_), channel_id=1, source_target_pairs={{0,6},{1,7},{2,4},{3,5},{4,2},{5,3},{6,0},{7,1},{8,14},{9,15},{10,... | collective-permute-start | bytes 23048 | tf_op jit(solution)/shard_map/ppermute | solution.py:584
  122.5 2.2 %conv_forward.3 = (bf16[1024,640]{1,0:T(8,128)(2,1)}, f32[1,128]{1,0:T(1,128)S(1)}) custom-call(bf16[3,1088,640]{2,1,0:T(8,128)(2,1)S(1)} %copy-done.1, bf16[3,640]{1,0:T(4,128)(2,1)S(1)} %reshape.38.refs_2_.refs_3_.refs_1_, bf16[1920,1920]{1,0:T(8,128)(2,1)S(1)} %arrange_weight.1.refs_4_.refs_2_, ...), custom_call_target="tpu_custom_call", output_to_operand_aliasing={{0}: (3, {})} | custom-call | flops 943718400 | bytes 7700480 | tf_op jit(solution)/shard_map/conv_forward/pallas_call | solution.py:33
  124.7 2.7 %collective-permute-start.19 = (f32[3,640]{1,0:T(4,128)S(1)}, f32[3,640]{1,0:T(4,128)S(1)}, u32[]{:S(2)}, u32[]{:S(2)}) collective-permute-start(f32[3,640]{1,0:T(4,128)S(1)} %add_small.1), channel_id=1, source_target_pairs={{0,1},{1,0},{2,3},{3,2},{4,5},{5,4},{6,7},{7,6},{8,9},{9,8},{10,11... | collective-permute-start | bytes 23048 | tf_op jit(solution)/shard_map/ppermute | solution.py:584
  127.5 2.0 %join_pieces.1 = f32[720,640]{1,0:T(8,128)} custom-call(s32[3]{0:T(128)S(1)} %pad_add_fusion.refs_0_, bf16[208,640]{1,0:T(8,128)(2,1)S(1)} %finish_sum.1.refs_3_.refs_0_.refs_1_, bf16[208,640]{1,0:T(8,128)(2,1)S(1)} %collective-permute-done.13.refs_1_.refs_2_, bf16[208,640]{1,0:T(8,128)(2,1)S(1)} %collective-permute-done.14.refs_2_.refs_3_, ...), custom_call_target="tpu_custom_call" | custom-call | flops 460800 | bytes 2764800 | tf_op jit(solution)/shard_map/join_pieces/pallas_call | solution.py:33
  (58 shorter events, 15.4 us)
Async XLA Ops:
  7.2 78.8 %all-gather.2.cloned.1.call-start = ((), (), s32[]{:S(2)}) async-start(), calls=%async_computation | async-start | bytes 8294400 | tf_op jit(solution)/shard_map/all_gather | solution.py:619
  8.6 1.3 collective-permute-start
  8.7 14.8 %collective-permute-start.5 = (bf16[1024,640]{1,0:T(8,128)(2,1)}, bf16[1024,640]{1,0:T(8,128)(2,1)}, u32[]{:S(2)}, u32[]{:S(2)}) collective-permute-start(bf16[1024,640]{1,0:T(8,128)(2,1)} %bitcast.25), channel_id=1, source_target_pairs={{0,1},{1,0},{2,3},{3,2},{4,5},{5,4},{6,7},{7,6},{8,9},{9,8},{10,11... | collective-permute-start | bytes 3932168 | tf_op jit(solution)/shard_map/ppermute | solution.py:584
  9.9 8.2 %collective-permute-start.1 = (bf16[2,3,80]{2,1,0:T(4,128)(2,1)S(1)}, bf16[2,3,80]{2,1,0:T(4,128)(2,1)S(1)}, u32[]{:S(2)}, u32[]{:S(2)}) collective-permute-start(bf16[2,3,80]{2,1,0:T(4,128)(2,1)S(1)} %maximum_select_fusion), channel_id=1, source_target_pairs={{0,6},{1,7},{2,4},{3,5},{4,2},{5,3},{6,0},{7,1},{8,14},{9,15},{10,... | collective-permute-start | bytes 2888 | tf_op jit(solution)/shard_map/ppermute | solution.py:584
  14.4 3.7 %collective-permute-start.2 = (bf16[2,3,80]{2,1,0:T(4,128)(2,1)S(1)}, bf16[2,3,80]{2,1,0:T(4,128)(2,1)S(1)}, u32[]{:S(2)}, u32[]{:S(2)}) collective-permute-start(bf16[2,3,80]{2,1,0:T(4,128)(2,1)S(1)} %maximum_select_fusion), channel_id=1, source_target_pairs={{0,4},{1,5},{2,6},{3,7},{4,0},{5,1},{6,2},{7,3},{8,12},{9,13},{10,... | collective-permute-start | bytes 2888 | tf_op jit(solution)/shard_map/ppermute | solution.py:584
  14.4 3.7 %collective-permute-start.3 = (bf16[2,3,80]{2,1,0:T(4,128)(2,1)S(1)}, bf16[2,3,80]{2,1,0:T(4,128)(2,1)S(1)}, u32[]{:S(2)}, u32[]{:S(2)}) collective-permute-start(bf16[2,3,80]{2,1,0:T(4,128)(2,1)S(1)} %maximum_select_fusion), channel_id=1, source_target_pairs={{0,2},{1,3},{2,0},{3,1},{4,6},{5,7},{6,4},{7,5},{8,10},{9,11},{10,... | collective-permute-start | bytes 2888 | tf_op jit(solution)/shard_map/ppermute | solution.py:584
  16.1 2.2 %copy-start.3 = (bf16[1,32,32,640]{3,2,1,0:T(8,128)(2,1)S(1)}, bf16[1,32,32,640]{3,2,1,0:T(8,128)(2,1)}, u32[]{:S(2)}) copy-start(bf16[1,32,32,640]{3,2,1,0:T(8,128)(2,1)} %param.6) | copy-start | bytes 3932164
  19.4 6.4 %collective-permute-start.4 = (bf16[640,1024]{1,0:T(8,128)(2,1)S(1)}, bf16[640,1024]{1,0:T(8,128)(2,1)}, u32[]{:S(2)}, u32[]{:S(2)}) collective-permute-start(bf16[640,1024]{1,0:T(8,128)(2,1)S(1)} %activate.1.refs_1_), channel_id=1, source_target_pairs={{0,1},{1,0},{2,3},{3,2},{4,5},{5,4},{6,7},{7,6},{8,9},{9,8},{10,11... | collective-permute-start | bytes 3932168 | tf_op jit(solution)/shard_map/ppermute | solution.py:584
  40.8 23.5 %collective-permute-start.6 = (bf16[2,2,192,640]{3,2,1,0:T(8,128)(2,1)S(1)}, bf16[2,2,192,640]{3,2,1,0:T(8,128)(2,1)S(1)}, u32[]{:S(2)}, u32[]{:S(2)}) collective-permute-start(bf16[2,2,192,640]{3,2,1,0:T(8,128)(2,1)S(1)} %get-tuple-element.28), channel_id=1, source_target_pairs={{0,8},{8,0},{16,24},{24,16},{1,9},{9,1},{17,25},{25,17},{2,10},{10... | collective-permute-start | bytes 2949128 | tf_op jit(solution)/shard_map/ppermute | solution.py:584
  42.1 23.4 %collective-permute-start.7 = (bf16[2,2,192,640]{3,2,1,0:T(8,128)(2,1)S(1)}, bf16[2,2,192,640]{3,2,1,0:T(8,128)(2,1)S(1)}, u32[]{:S(2)}, u32[]{:S(2)}) collective-permute-start(bf16[2,2,192,640]{3,2,1,0:T(8,128)(2,1)S(1)} %get-tuple-element.29), channel_id=1, source_target_pairs={{0,16},{8,24},{16,0},{24,8},{1,17},{9,25},{17,1},{25,9},{2,18},{10... | collective-permute-start | bytes 2949128 | tf_op jit(solution)/shard_map/ppermute | solution.py:584
  65.8 12.2 %collective-permute-start.8 = (bf16[2,192,640]{2,1,0:T(8,128)(2,1)S(1)}, bf16[2,192,640]{2,1,0:T(8,128)(2,1)S(1)}, u32[]{:S(2)}, u32[]{:S(2)}) collective-permute-start(bf16[2,192,640]{2,1,0:T(8,128)(2,1)S(1)} %get-tuple-element.30), channel_id=1, source_target_pairs={{0,16},{8,24},{16,0},{24,8},{1,17},{9,25},{17,1},{25,9},{2,18},{10... | collective-permute-start | bytes 1474568 | tf_op jit(solution)/shard_map/ppermute | solution.py:584
  67.1 11.8 %collective-permute-start.9 = (bf16[2,192,640]{2,1,0:T(8,128)(2,1)S(1)}, bf16[2,192,640]{2,1,0:T(8,128)(2,1)S(1)}, u32[]{:S(2)}, u32[]{:S(2)}) collective-permute-start(bf16[2,192,640]{2,1,0:T(8,128)(2,1)S(1)} %get-tuple-element.31), channel_id=1, source_target_pairs={{0,8},{8,0},{16,24},{24,16},{1,9},{9,1},{17,25},{25,17},{2,10},{10... | collective-permute-start | bytes 1474568 | tf_op jit(solution)/shard_map/ppermute | solution.py:584
  80.0 22.1 %collective-permute-start.10 = (bf16[192,640]{1,0:T(8,128)(2,1)}, bf16[192,640]{1,0:T(8,128)(2,1)S(1)}, u32[]{:S(2)}, u32[]{:S(2)}) collective-permute-start(bf16[192,640]{1,0:T(8,128)(2,1)} %get-tuple-element.34), channel_id=1, source_target_pairs={{0,2},{1,3},{2,0},{3,1},{4,6},{5,7},{6,4},{7,5},{8,10},{9,11},{10,... | collective-permute-start | bytes 737288 | tf_op jit(solution)/shard_map/ppermute | solution.py:584
  80.0 22.1 %collective-permute-start.11 = (bf16[192,640]{1,0:T(8,128)(2,1)}, bf16[192,640]{1,0:T(8,128)(2,1)}, u32[]{:S(2)}, u32[]{:S(2)}) collective-permute-start(bf16[192,640]{1,0:T(8,128)(2,1)} %get-tuple-element.35), channel_id=1, source_target_pairs={{0,4},{1,5},{2,6},{3,7},{4,0},{5,1},{6,2},{7,3},{8,12},{9,13},{10,... | collective-permute-start | bytes 737288 | tf_op jit(solution)/shard_map/ppermute | solution.py:584
  83.2 6.0 %copy-start.5 = (bf16[1,32,32,640]{3,2,1,0:T(8,128)(2,1)S(1)}, bf16[1,32,32,640]{3,2,1,0:T(8,128)(2,1)}, u32[]{:S(2)}) copy-start(bf16[1,32,32,640]{3,2,1,0:T(8,128)(2,1)} %param.7) | copy-start | bytes 3932164
  83.2 19.0 %collective-permute-start.12 = (bf16[192,640]{1,0:T(8,128)(2,1)}, bf16[192,640]{1,0:T(8,128)(2,1)}, u32[]{:S(2)}, u32[]{:S(2)}) collective-permute-start(bf16[192,640]{1,0:T(8,128)(2,1)} %get-tuple-element.36), channel_id=1, source_target_pairs={{0,6},{1,7},{2,4},{3,5},{4,2},{5,3},{6,0},{7,1},{8,14},{9,15},{10,... | collective-permute-start | bytes 737288 | tf_op jit(solution)/shard_map/ppermute | solution.py:584
  89.1 17.6 %copy-start.1 = (bf16[3,1088,640]{2,1,0:T(8,128)(2,1)S(1)}, bf16[3,1088,640]{2,1,0:T(8,128)(2,1)}, u32[]{:S(2)}) copy-start(bf16[3,1088,640]{2,1,0:T(8,128)(2,1)} %copy-done) | copy-start | bytes 12533764
  103.3 12.5 %collective-permute-start.13 = (bf16[208,640]{1,0:T(8,128)(2,1)S(1)}, bf16[208,640]{1,0:T(8,128)(2,1)S(1)}, u32[]{:S(2)}, u32[]{:S(2)}) collective-permute-start(bf16[208,640]{1,0:T(8,128)(2,1)S(1)} %finish_sum.1.refs_3_.refs_0_.refs_1_), channel_id=1, source_target_pairs={{0,8},{8,0},{16,24},{24,16},{1,9},{9,1},{17,25},{25,17},{2,10},{10... | collective-permute-start | bytes 798728 | tf_op jit(solution)/shard_map/ppermute | solution.py:584
  105.0 12.6 %collective-permute-start.14 = (bf16[208,640]{1,0:T(8,128)(2,1)S(1)}, bf16[208,640]{1,0:T(8,128)(2,1)S(1)}, u32[]{:S(2)}, u32[]{:S(2)}) collective-permute-start(bf16[208,640]{1,0:T(8,128)(2,1)S(1)} %finish_sum.1.refs_3_.refs_0_.refs_1_), channel_id=1, source_target_pairs={{0,16},{8,24},{16,0},{24,8},{1,17},{9,25},{17,1},{25,9},{2,18},{10... | collective-permute-start | bytes 798728 | tf_op jit(solution)/shard_map/ppermute | solution.py:584
  106.8 12.1 %collective-permute-start.15 = (bf16[208,640]{1,0:T(8,128)(2,1)S(1)}, bf16[208,640]{1,0:T(8,128)(2,1)S(1)}, u32[]{:S(2)}, u32[]{:S(2)}) collective-permute-start(bf16[208,640]{1,0:T(8,128)(2,1)S(1)} %finish_sum.1.refs_3_.refs_0_.refs_1_), channel_id=1, source_target_pairs={{0,24},{8,16},{16,8},{24,0},{1,25},{9,17},{17,9},{25,1},{2,26},{10... | collective-permute-start | bytes 798728 | tf_op jit(solution)/shard_map/ppermute | solution.py:584
  118.8 5.8 %collective-permute-start.16 = (f32[3,640]{1,0:T(4,128)S(1)}, f32[3,640]{1,0:T(4,128)S(1)}, u32[]{:S(2)}, u32[]{:S(2)}) collective-permute-start(f32[3,640]{1,0:T(4,128)S(1)} %add_small_of.1.refs_4_.refs_0_), channel_id=1, source_target_pairs={{0,2},{1,3},{2,0},{3,1},{4,6},{5,7},{6,4},{7,5},{8,10},{9,11},{10,... | collective-permute-start | bytes 23048 | tf_op jit(solution)/shard_map/ppermute | solution.py:584
  119.2 5.5 %collective-permute-start.17 = (f32[3,640]{1,0:T(4,128)S(1)}, f32[3,640]{1,0:T(4,128)S(1)}, u32[]{:S(2)}, u32[]{:S(2)}) collective-permute-start(f32[3,640]{1,0:T(4,128)S(1)} %add_small_of.1.refs_4_.refs_0_), channel_id=1, source_target_pairs={{0,4},{1,5},{2,6},{3,7},{4,0},{5,1},{6,2},{7,3},{8,12},{9,13},{10,... | collective-permute-start | bytes 23048 | tf_op jit(solution)/shard_map/ppermute | solution.py:584
  119.2 5.5 %collective-permute-start.18 = (f32[3,640]{1,0:T(4,128)S(1)}, f32[3,640]{1,0:T(4,128)S(1)}, u32[]{:S(2)}, u32[]{:S(2)}) collective-permute-start(f32[3,640]{1,0:T(4,128)S(1)} %add_small_of.1.refs_4_.refs_0_), channel_id=1, source_target_pairs={{0,6},{1,7},{2,4},{3,5},{4,2},{5,3},{6,0},{7,1},{8,14},{9,15},{10,... | collective-permute-start | bytes 23048 | tf_op jit(solution)/shard_map/ppermute | solution.py:584
  124.7 4.7 %collective-permute-start.19 = (f32[3,640]{1,0:T(4,128)S(1)}, f32[3,640]{1,0:T(4,128)S(1)}, u32[]{:S(2)}, u32[]{:S(2)}) collective-permute-start(f32[3,640]{1,0:T(4,128)S(1)} %add_small.1), channel_id=1, source_target_pairs={{0,1},{1,0},{2,3},{3,2},{4,5},{5,4},{6,7},{7,6},{8,9},{9,8},{10,11... | collective-permute-start | bytes 23048 | tf_op jit(solution)/shard_map/ppermute | solution.py:584
  (3 other events, 4.9 us)
Sparse Core Ops, SparseCore 0:
  9.6 76.2 all-gather.1

commit v4 on v3

--- a/solution.py
+++ b/solution.py
@@ -20,18 +20,30 @@
 ANY = pl.BlockSpec(memory_space=pl.ANY)
 
 
-def params(mib=24):
+def params(mib=10):
     return pltpu.CompilerParams(vmem_limit_bytes=mib * 1024 * 1024)
 
 
-def call(kernel, operands, in_specs, tokens=(), **options):
-    given = len(operands)
+def call(kernel, operands, in_specs, tokens=(), token=False, **options):
+    given, after = len(operands), len(operands) + len(tokens)
+    if token:
+        out_shape, out_specs = options["out_shape"], options["out_specs"]
+        if not isinstance(out_shape, tuple):
+            out_shape, out_specs = (out_shape,), (out_specs,)
+        options["out_shape"] = out_shape + (struct((1, 128), F32),)
+        options["out_specs"] = out_specs + (VMEM,)
+    outs = len(options["out_shape"]) - 1 if token else 0
 
     def body(*refs):
-        kernel(*refs[:given], *refs[given + len(tokens) :])
+        refs = refs[:given] + refs[after:]
+        if token:
+            at = given + outs
+            refs[at][...] = jnp.zeros_like(refs[at])
+            refs = refs[:at] + refs[at + 1 :]
+        kernel(*refs)
 
     return pl.pallas_call(
-        body, in_specs=list(in_specs) + [ANY] * len(tokens), **options
+        body, in_specs=list(in_specs) + [VMEM] * len(tokens), **options
     )(*operands, *tokens)
 
 
@@ -141,6 +153,7 @@
         (x, stat, vecs),
         [VMEM, VMEM, VMEM],
         tokens,
+        True,
         out_shape=struct((chans, pixels), BF16),
         out_specs=VMEM,
         compiler_params=params(),
@@ -211,10 +224,11 @@
         (place,) + operands,
         [SMEM, VMEM, VMEM, VMEM, VMEM],
         tokens,
+        True,
         out_shape=out_shape,
         out_specs=(VMEM,) * len(out_shape),
         scratch_shapes=[pltpu.VMEM((chans + 2 * extra, count), F32)],
-        compiler_params=params(28),
+        compiler_params=params(12),
         cost_estimate=pl.CostEstimate(
             flops=4 * blocks * (chans + 2 * extra) * pixels * count,
             bytes_accessed=20 * chans * pixels,
@@ -259,6 +273,8 @@
         finish_kernel,
         (*small, *terms),
         [VMEM] * (2 + len(terms)),
+        (),
+        True,
         out_shape=struct((piece + 16, outs), BF16),
         out_specs=VMEM,
         compiler_params=params(8),
@@ -333,6 +349,7 @@
         (keep, got0, got1, last0, last1),
         [VMEM] * 5,
         tokens,
+        True,
         out_shape=(struct((piece, count), F32),)
         + (struct((piece, count), BF16),) * (2 * half - 1),
         out_specs=(VMEM,) * (2 * half),
@@ -543,6 +560,7 @@
         (place, *pieces),
         [SMEM] + [VMEM] * 4,
         tokens,
+        True,
         out_shape=struct((rows, outs), F32),
         out_specs=VMEM,
         compiler_params=params(),
@@ -622,13 +640,13 @@
 
     stat = stats(x)
     vecs = jnp.transpose(small, (1, 0, 2)).reshape(3, chans)
-    own_t = activate(x, stat, vecs, ())
+    own_t, act_token = activate(x, stat, vecs, ())
     sib_t = swap(own_t, "fsdp", 1)
-    own_shifted, bias_sum = shift_grad(g, side, (own_t,))
-    sib_shifted, _ = shift_grad(sib_g, side, (own_t,))
+    own_shifted, bias_sum = shift_grad(g, side, (act_token,))
+    sib_shifted, _ = shift_grad(sib_g, side, (act_token,))
     operands = (own_t, sib_t, own_shifted, sib_shifted)
 
-    keep, send0, send1 = weight_by_rep(
+    keep, send0, send1, weight_token = weight_by_rep(
         place, operands, side, shards // 2, extra, piece, 0, outs, ()
     )
     got0 = swap(send0, "rep", 1)
@@ -636,25 +654,20 @@
     next0, next1 = rep_step(keep, got0, got1, ())
     last0 = swap(next0, "rep", 2)
     last1 = swap(next1, "rep", 1)
-    own_sum, *sends = rep_sum(keep, got0, got1, last0, last1, ())
+    own_sum, *sends, sum_token = rep_sum(keep, got0, got1, last0, last1, ())
     got = [swap(a, "fsdp", 2 * (m + 1)) for m, a in enumerate(sends)]
-    act_shifted = prepare(x, stat, vecs, side, (keep,))
+    act_shifted = prepare(x, stat, vecs, side, (weight_token,))
     weight = arrange(weight)
-    in_grad, param_sums = act_grad(g, x, stat, vecs, weight, side, (own_sum,))
-    done = finish((own_sum, *got), (bias_sum, param_sums))
+    in_grad, param_sums = act_grad(g, x, stat, vecs, weight, side, (sum_token,))
+    done, done_token = finish((own_sum, *got), (bias_sum, param_sums))
     pieces_done = [done] + [swap(done, "rep", m) for m in range(1, reps)]
 
-    part = 7 * pixels // 8
-    conv_out, token = conv(act_shifted, vecs, weight, side, 0, part, None, (done,))
+    conv_out, token = conv(act_shifted, vecs, weight, side, 0, pixels, None, (done_token,))
     small_sums = add_small_of(pieces_done, piece, 3, (token,))
     over_z = [small_sums] + [swap(small_sums, "fsdp", m) for m in range(2, shards, 2)]
-    conv_out, token = conv(
-        act_shifted, vecs, weight, side, part, pixels - part, conv_out, (small_sums,)
-    )
-    small_sums = add_small(over_z, (token,))
     scale = 1.0 / math.sqrt(reps * shards * pixels)
-    small_sums = sum_all(small_sums, "fsdp", (1,)) * scale
-    weight_grad = join(place, pieces_done, rows, piece, scale, (token,))
+    weight_grad, token = join(place, pieces_done, rows, piece, scale, (token,))
+    small_sums = sum_all(add_small(over_z, (token,)), "fsdp", (1,)) * scale
     share = outs // shards
     mine = lax.dynamic_slice_in_dim(small_sums.reshape(3, shards, share), f, 1, axis=1)
     mine = mine.reshape(3, share)

time: 137 us -> 136 us (level)
    pallas_call x15 -> x14, Pallas kernels: 52.8 us -> 51.5 us  [call(): pl.pallas_call(body, in_specs=list(in_specs) + [VMEM] * len(tokens), **op...]
  transfers between devices with their start and end apart: 21 -> 21, of which waited for: 7 -> 9; matrix products, arithmetic and copies ran while one was open for 1% -> 1% of each run, Pallas kernels for 39% -> 38%
where the time goes in v4:
time: 136 us
  Pallas kernels  53.5 us (39%)
  waiting for transfers between devices  36.3 us (27%)
  starting transfers between devices  24.7 us (18%)
  between operations  14.2 us (10%)
  local copies, waits for them, and re-layouts  5.45 us (4%)
  other arithmetic  1.52 us (1%)
    pallas_call x14, Pallas kernels, call(): pl.pallas_call(body, in_specs=list(in_specs) + [VMEM] * len(tokens), **op...  51.5 us
    ppermute x20, waiting for transfers between devices, swap(): return lax.ppermute(x, axis, [(i, i ^ mask) for i in range(n)])  32.5 us
    ppermute x20, starting transfers between devices, swap(): return lax.ppermute(x, axis, [(i, i ^ mask) for i in range(n)])  24.7 us
    unnamed x12, local copies, waits for them, and re-layouts  4.74 us
    all_gather x1, waiting for transfers between devices, local_fast(): weight = lax.all_gather(conv_weight, 'fsdp', axis=0, tiled=True)  3.19 us
  transfers between devices with their start and end apart: 21, of which 9 were waited for; matrix products, arithmetic and copies ran while one was open for 1% of the time, Pallas kernels for 38%

profile of v4, /device:TPU:1, one launch (start us, length us, event | category | flops | bytes accessed | tf_op | source)
XLA Modules:
  0.0 135.7 jit_solution(427690318199315151)
XLA Ops:
  9.9 4.5 %collective-permute-start.1 = (bf16[2,3,80]{2,1,0:T(4,128)(2,1)S(1)}, bf16[2,3,80]{2,1,0:T(4,128)(2,1)S(1)}, u32[]{:S(2)}, u32[]{:S(2)}) collective-permute-start(bf16[2,3,80]{2,1,0:T(4,128)(2,1)S(1)} %maximum_select_fusion), channel_id=1, source_target_pairs={{0,6},{1,7},{2,4},{3,5},{4,2},{5,3},{6,0},{7,1},{8,14},{9,15},{10,... | collective-permute-start | bytes 2888 | tf_op jit(solution)/shard_map/ppermute | solution.py:602
  14.7 1.3 copy-done
  16.1 2.0 %norm_stats.1.refs_1_.refs_2_ = f32[2,640]{1,0:T(2,128)S(1)} custom-call(bf16[1024,640]{1,0:T(8,128)(2,1)S(1)} %bitcast.21), custom_call_target="tpu_custom_call" | custom-call | flops 3276800 | bytes 1310720 | tf_op jit(solution)/shard_map/norm_stats/pallas_call | solution.py:124
  18.3 1.4 %copy-done.1 = bf16[1,32,32,640]{3,2,1,0:T(8,128)(2,1)S(1)} copy-done((bf16[1,32,32,640]{3,2,1,0:T(8,128)(2,1)S(1)}, bf16[1,32,32,640]{3,2,1,0:T(8,128)(2,1)}, u32[]{:S(2)}) %copy-start.1) | copy-done | bytes 1310744
  19.7 2.1 %activate.1 = (bf16[640,1024]{1,0:T(8,128)(2,1)}, f32[1,128]{1,0:T(1,128)S(1)}) custom-call(bf16[1024,640]{1,0:T(8,128)(2,1)S(1)} %bitcast.22, f32[2,640]{1,0:T(2,128)S(1)} %norm_stats.1.refs_1_.refs_2_, bf16[3,640]{1,0:T(4,128)(2,1)S(1)} %reshape.38.refs_2_.refs_3_.refs_1_), custom_call_target="tpu_custom_call" | custom-call | flops 6553600 | bytes 2621440 | tf_op jit(solution)/shard_map/activate/pallas_call | solution.py:45
  21.8 1.5 %collective-permute-start.4 = (bf16[640,1024]{1,0:T(8,128)(2,1)}, bf16[640,1024]{1,0:T(8,128)(2,1)}, u32[]{:S(2)}, u32[]{:S(2)}) collective-permute-start(bf16[640,1024]{1,0:T(8,128)(2,1)} %get-tuple-element.30.refs_1_), channel_id=1, source_target_pairs={{0,1},{1,0},{2,3},{3,2},{4,5},{5,4},{6,7},{7,6},{8,9},{9,8},{10,11... | collective-permute-start | bytes 3932168 | tf_op jit(solution)/shard_map/ppermute | solution.py:602
  26.3 15.3 %weight_grad_rep.1 = (f32[2,2,2,192,640]{4,3,2,1,0:T(8,128)S(1)}, bf16[2,2,192,640]{3,2,1,0:T(8,128)(2,1)S(1)}, bf16[2,2,192,640]{3,2,1,0:T(8,128)(2,1)S(1)}, f32[1,128]{1,0:T(1,128)S(1)}) custom-call(s32[3]{0:T(128)S(1)} %pad_add_fusion.refs_0_, bf16[640,1024]{1,0:T(8,128)(2,1)} %get-tuple-element.30.refs_1_, ...), custom_call_target="tpu_custom_call" | custom-call | flops 8388608000 | bytes 13107200 | tf_op jit(solution)/shard_map/weight_grad_rep/pallas_call | solution.py:45
  41.6 1.3 collective-permute-start.6
  42.9 1.2 collective-permute-start.7
  44.2 20.6 %collective-permute-done.6.refs_1_ = bf16[2,2,192,640]{3,2,1,0:T(8,128)(2,1)S(1)} collective-permute-done((bf16[2,2,192,640]{3,2,1,0:T(8,128)(2,1)S(1)}, bf16[2,2,192,640]{3,2,1,0:T(8,128)(2,1)S(1)}, u32[]{:S(2)}, u32[]{:S(2)}) %collective-permute-start.6) | collective-permute-done | bytes 983072 | tf_op jit(solution)/shard_map/ppermute | solution.py:602
  65.8 1.3 collective-permute-start.8
  67.5 1.7 %prepare.1.refs_0_ = bf16[3,1088,640]{2,1,0:T(8,128)(2,1)S(1)} custom-call(bf16[1024,640]{1,0:T(8,128)(2,1)S(1)} %bitcast.23, f32[2,640]{1,0:T(2,128)S(1)} %norm_stats.1.refs_1_.refs_2_, bf16[3,640]{1,0:T(4,128)(2,1)S(1)} %reshape.38.refs_2_.refs_3_.refs_1_, f32[1,128]{1,0:T(1,128)S(1)} %get-tuple-element.34.refs_3_), custom_call_target="tpu_custom_call" | custom-call | flops 13107200 | bytes 5242880 | tf_op jit(solution)/shard_map/prepare/pallas_call | solution.py:45
  69.1 2.0 %copy-done.3 = bf16[3,1088,640]{2,1,0:T(8,128)(2,1)} copy-done((bf16[3,1088,640]{2,1,0:T(8,128)(2,1)}, bf16[3,1088,640]{2,1,0:T(8,128)(2,1)S(1)}, u32[]{:S(2)}) %copy-start.3) | copy-done | bytes 4177944
  71.1 6.2 %collective-permute-done.8.refs_3_ = bf16[2,192,640]{2,1,0:T(8,128)(2,1)S(1)} collective-permute-done((bf16[2,192,640]{2,1,0:T(8,128)(2,1)S(1)}, bf16[2,192,640]{2,1,0:T(8,128)(2,1)S(1)}, u32[]{:S(2)}, u32[]{:S(2)}) %collective-permute-start.8) | collective-permute-done | bytes 491552 | tf_op jit(solution)/shard_map/ppermute | solution.py:602
  80.0 2.6 %collective-permute-start.11 = (bf16[192,640]{1,0:T(8,128)(2,1)}, bf16[192,640]{1,0:T(8,128)(2,1)}, u32[]{:S(2)}, u32[]{:S(2)}) collective-permute-start(bf16[192,640]{1,0:T(8,128)(2,1)} %get-tuple-element.45), channel_id=1, source_target_pairs={{0,4},{1,5},{2,6},{3,7},{4,0},{5,1},{6,2},{7,3},{8,12},{9,13},{10,... | collective-permute-start | bytes 737288 | tf_op jit(solution)/shard_map/ppermute | solution.py:602
  82.8 3.2 %all-gather.2.cloned.1.call-done.refs_0_ = bf16[5760,640]{1,0:T(8,128)(2,1)} async-done(((bf16[720,640]{1,0:T(8,128)(2,1)}), bf16[5760,640]{1,0:T(8,128)(2,1)}) %all-gather.2.cloned.1.call-update) | async-done | bytes 7372816 | tf_op jit(solution)/shard_map/all_gather | solution.py:637
  86.0 3.2 %arrange_weight.1.refs_4_.refs_2_ = bf16[1920,1920]{1,0:T(8,128)(2,1)S(1)} custom-call(bf16[5760,640]{1,0:T(8,128)(2,1)} %all-gather.2.cloned.1.call-done.refs_0_), custom_call_target="tpu_custom_call" | custom-call | bytes 14745600 | tf_op jit(solution)/shard_map/arrange_weight/pallas_call | solution.py:45
  89.2 13.0 %act_grad.1 = (bf16[1024,640]{1,0:T(8,128)(2,1)}, f32[2,640]{1,0:T(2,128)S(1)}) custom-call(bf16[1024,640]{1,0:T(8,128)(2,1)S(1)} %bitcast.27, bf16[1024,640]{1,0:T(8,128)(2,1)S(1)} %bitcast.24, f32[2,640]{1,0:T(2,128)S(1)} %norm_stats.1.refs_1_.refs_2_, bf16[3,640]{1,0:T(4,128)(2,1)S(1)} %reshape.38.refs_2_.refs_3_.refs_1_, ...), custom_call_target="tpu_custom_call" | custom-call | flops 7549747200 | bytes 15237120 | tf_op jit(solution)/shard_map/act_grad/pallas_call | solution.py:45
  103.4 1.8 %collective-permute-start.13 = (bf16[208,640]{1,0:T(8,128)(2,1)S(1)}, bf16[208,640]{1,0:T(8,128)(2,1)S(1)}, u32[]{:S(2)}, u32[]{:S(2)}) collective-permute-start(bf16[208,640]{1,0:T(8,128)(2,1)S(1)} %get-tuple-element.50.refs_1_.refs_0_), channel_id=1, source_target_pairs={{0,8},{8,0},{16,24},{24,16},{1,9},{9,1},{17,25},{25,17},{2,10},{10... | collective-permute-start | bytes 798728 | tf_op jit(solution)/shard_map/ppermute | solution.py:602
  105.2 1.6 %collective-permute-start.14 = (bf16[208,640]{1,0:T(8,128)(2,1)S(1)}, bf16[208,640]{1,0:T(8,128)(2,1)S(1)}, u32[]{:S(2)}, u32[]{:S(2)}) collective-permute-start(bf16[208,640]{1,0:T(8,128)(2,1)S(1)} %get-tuple-element.50.refs_1_.refs_0_), channel_id=1, source_target_pairs={{0,16},{8,24},{16,0},{24,8},{1,17},{9,25},{17,1},{25,9},{2,18},{10... | collective-permute-start | bytes 798728 | tf_op jit(solution)/shard_map/ppermute | solution.py:602
  106.8 9.8 %conv_forward.1 = (bf16[1024,640]{1,0:T(8,128)(2,1)}, f32[1,128]{1,0:T(1,128)S(1)}) custom-call(bf16[3,1088,640]{2,1,0:T(8,128)(2,1)S(1)} %copy-done.4, bf16[3,640]{1,0:T(4,128)(2,1)S(1)} %reshape.38.refs_2_.refs_3_.refs_1_, bf16[1920,1920]{1,0:T(8,128)(2,1)S(1)} %arrange_weight.1.refs_4_.refs_2_, f32[1,128]{1,0:T(1,128)S(1)} %get-tuple-element.47.refs_3_), custom_call_target="tpu_custom_call" | custom-call | flops 7549747200 | bytes 9994240 | tf_op jit(solution)/shard_map/conv_forward/pallas_call | solution.py:45
  118.8 3.5 %collective-permute-start.18 = (f32[3,640]{1,0:T(4,128)S(1)}, f32[3,640]{1,0:T(4,128)S(1)}, u32[]{:S(2)}, u32[]{:S(2)}) collective-permute-start(f32[3,640]{1,0:T(4,128)S(1)} %add_small_of.1.refs_0_), channel_id=1, source_target_pairs={{0,6},{1,7},{2,4},{3,5},{4,2},{5,3},{6,0},{7,1},{8,14},{9,15},{10,... | collective-permute-start | bytes 23048 | tf_op jit(solution)/shard_map/ppermute | solution.py:602
  122.3 2.0 %join_pieces.1 = (f32[720,640]{1,0:T(8,128)}, f32[1,128]{1,0:T(1,128)S(1)}) custom-call(s32[3]{0:T(128)S(1)} %pad_add_fusion.refs_0_, bf16[208,640]{1,0:T(8,128)(2,1)S(1)} %get-tuple-element.50.refs_1_.refs_0_, bf16[208,640]{1,0:T(8,128)(2,1)S(1)} %collective-permute-done.13.refs_2_.refs_1_, bf16[208,640]{1,0:T(8,128)(2,1)S(1)} %collective-permute-done.14.refs_3_.refs_2_, ...), custom_call_target="tpu_custom_call" | custom-call | flops 460800 | bytes 2764800 | tf_op jit(solution)/shard_map/join_pieces/pallas_call | solution.py:45
  124.3 3.1 %collective-permute-start.19 = (f32[3,640]{1,0:T(4,128)S(1)}, f32[3,640]{1,0:T(4,128)S(1)}, u32[]{:S(2)}, u32[]{:S(2)}) collective-permute-start(f32[3,640]{1,0:T(4,128)S(1)} %add_small.1), channel_id=1, source_target_pairs={{0,1},{1,0},{2,3},{3,2},{4,5},{5,4},{6,7},{7,6},{8,9},{9,8},{10,11... | collective-permute-start | bytes 23048 | tf_op jit(solution)/shard_map/ppermute | solution.py:602
  (57 shorter events, 15.3 us)
Async XLA Ops:
  7.2 78.8 %all-gather.2.cloned.1.call-start = ((), (), s32[]{:S(2)}) async-start(), calls=%async_computation | async-start | bytes 8294400 | tf_op jit(solution)/shard_map/all_gather | solution.py:637
  8.6 1.3 collective-permute-start
  8.7 15.6 %collective-permute-start.5 = (bf16[1024,640]{1,0:T(8,128)(2,1)}, bf16[1024,640]{1,0:T(8,128)(2,1)S(1)}, u32[]{:S(2)}, u32[]{:S(2)}) collective-permute-start(bf16[1024,640]{1,0:T(8,128)(2,1)} %bitcast.25), channel_id=1, source_target_pairs={{0,1},{1,0},{2,3},{3,2},{4,5},{5,4},{6,7},{7,6},{8,9},{9,8},{10,11... | collective-permute-start | bytes 3932168 | tf_op jit(solution)/shard_map/ppermute | solution.py:602
  9.9 8.2 %collective-permute-start.1 = (bf16[2,3,80]{2,1,0:T(4,128)(2,1)S(1)}, bf16[2,3,80]{2,1,0:T(4,128)(2,1)S(1)}, u32[]{:S(2)}, u32[]{:S(2)}) collective-permute-start(bf16[2,3,80]{2,1,0:T(4,128)(2,1)S(1)} %maximum_select_fusion), channel_id=1, source_target_pairs={{0,6},{1,7},{2,4},{3,5},{4,2},{5,3},{6,0},{7,1},{8,14},{9,15},{10,... | collective-permute-start | bytes 2888 | tf_op jit(solution)/shard_map/ppermute | solution.py:602
  14.4 3.7 %collective-permute-start.2 = (bf16[2,3,80]{2,1,0:T(4,128)(2,1)S(1)}, bf16[2,3,80]{2,1,0:T(4,128)(2,1)S(1)}, u32[]{:S(2)}, u32[]{:S(2)}) collective-permute-start(bf16[2,3,80]{2,1,0:T(4,128)(2,1)S(1)} %maximum_select_fusion), channel_id=1, source_target_pairs={{0,4},{1,5},{2,6},{3,7},{4,0},{5,1},{6,2},{7,3},{8,12},{9,13},{10,... | collective-permute-start | bytes 2888 | tf_op jit(solution)/shard_map/ppermute | solution.py:602
  14.4 3.7 %collective-permute-start.3 = (bf16[2,3,80]{2,1,0:T(4,128)(2,1)S(1)}, bf16[2,3,80]{2,1,0:T(4,128)(2,1)S(1)}, u32[]{:S(2)}, u32[]{:S(2)}) collective-permute-start(bf16[2,3,80]{2,1,0:T(4,128)(2,1)S(1)} %maximum_select_fusion), channel_id=1, source_target_pairs={{0,2},{1,3},{2,0},{3,1},{4,6},{5,7},{6,4},{7,5},{8,10},{9,11},{10,... | collective-permute-start | bytes 2888 | tf_op jit(solution)/shard_map/ppermute | solution.py:602
  16.1 7.3 %copy-start.5 = (bf16[1,32,32,640]{3,2,1,0:T(8,128)(2,1)S(1)}, bf16[1,32,32,640]{3,2,1,0:T(8,128)(2,1)}, u32[]{:S(2)}) copy-start(bf16[1,32,32,640]{3,2,1,0:T(8,128)(2,1)} %param.7) | copy-start | bytes 3932164
  21.8 4.5 %collective-permute-start.4 = (bf16[640,1024]{1,0:T(8,128)(2,1)}, bf16[640,1024]{1,0:T(8,128)(2,1)}, u32[]{:S(2)}, u32[]{:S(2)}) collective-permute-start(bf16[640,1024]{1,0:T(8,128)(2,1)} %get-tuple-element.30.refs_1_), channel_id=1, source_target_pairs={{0,1},{1,0},{2,3},{3,2},{4,5},{5,4},{6,7},{7,6},{8,9},{9,8},{10,11... | collective-permute-start | bytes 3932168 | tf_op jit(solution)/shard_map/ppermute | solution.py:602
  41.6 23.1 %collective-permute-start.6 = (bf16[2,2,192,640]{3,2,1,0:T(8,128)(2,1)S(1)}, bf16[2,2,192,640]{3,2,1,0:T(8,128)(2,1)S(1)}, u32[]{:S(2)}, u32[]{:S(2)}) collective-permute-start(bf16[2,2,192,640]{3,2,1,0:T(8,128)(2,1)S(1)} %get-tuple-element.37), channel_id=1, source_target_pairs={{0,8},{8,0},{16,24},{24,16},{1,9},{9,1},{17,25},{25,17},{2,10},{10... | collective-permute-start | bytes 2949128 | tf_op jit(solution)/shard_map/ppermute | solution.py:602
  42.9 22.7 %collective-permute-start.7 = (bf16[2,2,192,640]{3,2,1,0:T(8,128)(2,1)S(1)}, bf16[2,2,192,640]{3,2,1,0:T(8,128)(2,1)S(1)}, u32[]{:S(2)}, u32[]{:S(2)}) collective-permute-start(bf16[2,2,192,640]{3,2,1,0:T(8,128)(2,1)S(1)} %get-tuple-element.38), channel_id=1, source_target_pairs={{0,16},{8,24},{16,0},{24,8},{1,17},{9,25},{17,1},{25,9},{2,18},{10... | collective-permute-start | bytes 2949128 | tf_op jit(solution)/shard_map/ppermute | solution.py:602
  65.8 11.5 %collective-permute-start.8 = (bf16[2,192,640]{2,1,0:T(8,128)(2,1)S(1)}, bf16[2,192,640]{2,1,0:T(8,128)(2,1)S(1)}, u32[]{:S(2)}, u32[]{:S(2)}) collective-permute-start(bf16[2,192,640]{2,1,0:T(8,128)(2,1)S(1)} %get-tuple-element.39), channel_id=1, source_target_pairs={{0,16},{8,24},{16,0},{24,8},{1,17},{9,25},{17,1},{25,9},{2,18},{10... | collective-permute-start | bytes 1474568 | tf_op jit(solution)/shard_map/ppermute | solution.py:602
  67.1 11.1 %collective-permute-start.9 = (bf16[2,192,640]{2,1,0:T(8,128)(2,1)S(1)}, bf16[2,192,640]{2,1,0:T(8,128)(2,1)S(1)}, u32[]{:S(2)}, u32[]{:S(2)}) collective-permute-start(bf16[2,192,640]{2,1,0:T(8,128)(2,1)S(1)} %get-tuple-element.40), channel_id=1, source_target_pairs={{0,8},{8,0},{16,24},{24,16},{1,9},{9,1},{17,25},{25,17},{2,10},{10... | collective-permute-start | bytes 1474568 | tf_op jit(solution)/shard_map/ppermute | solution.py:602
  69.1 2.0 %copy-start.3 = (bf16[3,1088,640]{2,1,0:T(8,128)(2,1)}, bf16[3,1088,640]{2,1,0:T(8,128)(2,1)S(1)}, u32[]{:S(2)}) copy-start(bf16[3,1088,640]{2,1,0:T(8,128)(2,1)S(1)} %prepare.1.refs_0_) | copy-start | bytes 12533764
  79.3 22.9 %collective-permute-start.10 = (bf16[192,640]{1,0:T(8,128)(2,1)}, bf16[192,640]{1,0:T(8,128)(2,1)S(1)}, u32[]{:S(2)}, u32[]{:S(2)}) collective-permute-start(bf16[192,640]{1,0:T(8,128)(2,1)} %get-tuple-element.44), channel_id=1, source_target_pairs={{0,2},{1,3},{2,0},{3,1},{4,6},{5,7},{6,4},{7,5},{8,10},{9,11},{10,... | collective-permute-start | bytes 737288 | tf_op jit(solution)/shard_map/ppermute | solution.py:602
  80.0 22.2 %collective-permute-start.11 = (bf16[192,640]{1,0:T(8,128)(2,1)}, bf16[192,640]{1,0:T(8,128)(2,1)}, u32[]{:S(2)}, u32[]{:S(2)}) collective-permute-start(bf16[192,640]{1,0:T(8,128)(2,1)} %get-tuple-element.45), channel_id=1, source_target_pairs={{0,4},{1,5},{2,6},{3,7},{4,0},{5,1},{6,2},{7,3},{8,12},{9,13},{10,... | collective-permute-start | bytes 737288 | tf_op jit(solution)/shard_map/ppermute | solution.py:602
  82.6 19.6 %collective-permute-start.12 = (bf16[192,640]{1,0:T(8,128)(2,1)}, bf16[192,640]{1,0:T(8,128)(2,1)}, u32[]{:S(2)}, u32[]{:S(2)}) collective-permute-start(bf16[192,640]{1,0:T(8,128)(2,1)} %get-tuple-element.46), channel_id=1, source_target_pairs={{0,6},{1,7},{2,4},{3,5},{4,2},{5,3},{6,0},{7,1},{8,14},{9,15},{10,... | collective-permute-start | bytes 737288 | tf_op jit(solution)/shard_map/ppermute | solution.py:602
  89.2 17.6 %copy-start.4 = (bf16[3,1088,640]{2,1,0:T(8,128)(2,1)S(1)}, bf16[3,1088,640]{2,1,0:T(8,128)(2,1)}, u32[]{:S(2)}) copy-start(bf16[3,1088,640]{2,1,0:T(8,128)(2,1)} %copy-done.3) | copy-start | bytes 12533764
  103.4 13.3 %collective-permute-start.13 = (bf16[208,640]{1,0:T(8,128)(2,1)S(1)}, bf16[208,640]{1,0:T(8,128)(2,1)S(1)}, u32[]{:S(2)}, u32[]{:S(2)}) collective-permute-start(bf16[208,640]{1,0:T(8,128)(2,1)S(1)} %get-tuple-element.50.refs_1_.refs_0_), channel_id=1, source_target_pairs={{0,8},{8,0},{16,24},{24,16},{1,9},{9,1},{17,25},{25,17},{2,10},{10... | collective-permute-start | bytes 798728 | tf_op jit(solution)/shard_map/ppermute | solution.py:602
  105.2 12.5 %collective-permute-start.14 = (bf16[208,640]{1,0:T(8,128)(2,1)S(1)}, bf16[208,640]{1,0:T(8,128)(2,1)S(1)}, u32[]{:S(2)}, u32[]{:S(2)}) collective-permute-start(bf16[208,640]{1,0:T(8,128)(2,1)S(1)} %get-tuple-element.50.refs_1_.refs_0_), channel_id=1, source_target_pairs={{0,16},{8,24},{16,0},{24,8},{1,17},{9,25},{17,1},{25,9},{2,18},{10... | collective-permute-start | bytes 798728 | tf_op jit(solution)/shard_map/ppermute | solution.py:602
  106.8 11.9 %collective-permute-start.15 = (bf16[208,640]{1,0:T(8,128)(2,1)S(1)}, bf16[208,640]{1,0:T(8,128)(2,1)S(1)}, u32[]{:S(2)}, u32[]{:S(2)}) collective-permute-start(bf16[208,640]{1,0:T(8,128)(2,1)S(1)} %get-tuple-element.50.refs_1_.refs_0_), channel_id=1, source_target_pairs={{0,24},{8,16},{16,8},{24,0},{1,25},{9,17},{17,9},{25,1},{2,26},{10... | collective-permute-start | bytes 798728 | tf_op jit(solution)/shard_map/ppermute | solution.py:602
  118.7 5.6 %collective-permute-start.16 = (f32[3,640]{1,0:T(4,128)S(1)}, f32[3,640]{1,0:T(4,128)S(1)}, u32[]{:S(2)}, u32[]{:S(2)}) collective-permute-start(f32[3,640]{1,0:T(4,128)S(1)} %add_small_of.1.refs_0_), channel_id=1, source_target_pairs={{0,2},{1,3},{2,0},{3,1},{4,6},{5,7},{6,4},{7,5},{8,10},{9,11},{10,... | collective-permute-start | bytes 23048 | tf_op jit(solution)/shard_map/ppermute | solution.py:602
  118.8 5.5 %collective-permute-start.17 = (f32[3,640]{1,0:T(4,128)S(1)}, f32[3,640]{1,0:T(4,128)S(1)}, u32[]{:S(2)}, u32[]{:S(2)}) collective-permute-start(f32[3,640]{1,0:T(4,128)S(1)} %add_small_of.1.refs_0_), channel_id=1, source_target_pairs={{0,4},{1,5},{2,6},{3,7},{4,0},{5,1},{6,2},{7,3},{8,12},{9,13},{10,... | collective-permute-start | bytes 23048 | tf_op jit(solution)/shard_map/ppermute | solution.py:602
  118.8 5.5 %collective-permute-start.18 = (f32[3,640]{1,0:T(4,128)S(1)}, f32[3,640]{1,0:T(4,128)S(1)}, u32[]{:S(2)}, u32[]{:S(2)}) collective-permute-start(f32[3,640]{1,0:T(4,128)S(1)} %add_small_of.1.refs_0_), channel_id=1, source_target_pairs={{0,6},{1,7},{2,4},{3,5},{4,2},{5,3},{6,0},{7,1},{8,14},{9,15},{10,... | collective-permute-start | bytes 23048 | tf_op jit(solution)/shard_map/ppermute | solution.py:602
  124.3 3.9 %collective-permute-start.19 = (f32[3,640]{1,0:T(4,128)S(1)}, f32[3,640]{1,0:T(4,128)S(1)}, u32[]{:S(2)}, u32[]{:S(2)}) collective-permute-start(f32[3,640]{1,0:T(4,128)S(1)} %add_small.1), channel_id=1, source_target_pairs={{0,1},{1,0},{2,3},{3,2},{4,5},{5,4},{6,7},{7,6},{8,9},{9,8},{10,11... | collective-permute-start | bytes 23048 | tf_op jit(solution)/shard_map/ppermute | solution.py:602
  (3 other events, 4.5 us)
Sparse Core Ops, SparseCore 0:
  9.6 76.3 all-gather.1

commit v5 on v4

--- a/solution.py
+++ b/solution.py
@@ -194,8 +194,10 @@
     step = (chans + extra - piece) // (reps - 1)
 
     def rows_of(rel):
-        at = pl.multiple_of(extra * core + step * (r ^ rel), 16)
-        return block_ref[pl.ds(at, piece), :]
+        at = extra * core + step * (r ^ rel)
+        past = at % 8
+        rows = block_ref[pl.ds(pl.multiple_of(at - past, 8), piece + piece % 8), :]
+        return jnp.where(past == 0, rows[:piece], rows[piece % 8 :])
 
     for k in weight_blocks(
         side, extra, 2 * half, core, own_t, sib_t, own_g, sib_g, first, count, block_ref
@@ -257,14 +259,15 @@
     for ref in refs[1:-1]:
         total = total + ref[...].astype(F32)
     piece = total.shape[0]
-    out_ref[0:piece, :] = total.astype(BF16)
+    head = out_ref.shape[0] - piece
+    out_ref[head:, :] = total.astype(BF16)
     small = jnp.concatenate([bias_ref[...], param_ref[...]], axis=0)
     high = small.astype(BF16).astype(F32)
     middle = (small - high).astype(BF16).astype(F32)
     parts = [high, middle, small - high - middle]
-    spare = out_ref.shape[0] - piece - 3 * small.shape[0]
+    spare = head - 3 * small.shape[0]
     parts.append(jnp.zeros((spare, small.shape[1]), F32))
-    out_ref[piece:, :] = jnp.concatenate(parts, axis=0).astype(BF16)
+    out_ref[0:head, :] = jnp.concatenate(parts, axis=0).astype(BF16)
 
 
 def finish(terms, small):
@@ -290,7 +293,7 @@
     count = out_ref.shape[0]
     terms = []
     for ref in refs[:-1]:
-        rows = ref[piece:, :].astype(F32)
+        rows = ref[0 : ref.shape[0] - piece, :].astype(F32)
         terms.append(rows[0:count] + rows[count : 2 * count] + rows[2 * count : 3 * count])
     out_ref[...] = tree_sum(terms)
 
@@ -472,7 +475,7 @@
     pixels, chans = x.shape
     outs = g.shape[1]
     return call(
-        functools.partial(grad_kernel, side, pixels // 2),
+        functools.partial(grad_kernel, side, pixels),
         (g, x, stat, vecs, weight),
         [VMEM] * 5,
         tokens,
@@ -482,7 +485,7 @@
             pltpu.VMEM((pixels, chans), F32),
             pltpu.VMEM((pixels + 2 * side, outs), BF16),
         ],
-        compiler_params=params(24),
+        compiler_params=params(32),
         cost_estimate=pl.CostEstimate(
             flops=18 * chans * outs * pixels,
             bytes_accessed=18 * chans * outs + 12 * pixels * chans,
@@ -550,7 +553,7 @@
 
             @pl.when((q ^ r) == rel)
             def _():
-                out_ref[step * q : step * q + piece, :] = ref[0:piece, :].astype(F32) * scale
+                out_ref[step * q : step * q + piece, :] = ref[ref.shape[0] - piece :, :].astype(F32) * scale
 
 
 def join(place, pieces, rows, piece, scale, tokens):
@@ -629,7 +632,7 @@
     r, f = lax.axis_index("rep"), lax.axis_index("fsdp")
     z, core = f // 2, f % 2
     extra = rows - chans
-    piece = round_up(-(-rows // reps), 16)
+    piece = -(-rows // reps)
     x = features.reshape(pixels, chans)
     g = out_grad.reshape(pixels, outs)
     place = jnp.stack([r, z, core]).astype(jnp.int32)
@@ -691,13 +694,14 @@
         return False
     if chans != outs or rows * shards != 9 * chans or chans % 128 or side % 16 or outs < 3 * 128:
         return False
-    extra, piece = rows - chans, round_up(-(-rows // reps), 16)
+    extra, piece = rows - chans, -(-rows // reps)
     step = (rows - piece) // (reps - 1)
     return (
         extra % 16 == 0
         and step * (reps - 1) == rows - piece
-        and step % 16 == 0
-        and piece % 32 == 0
+        and step == piece
+        and piece % 8 in (0, 4)
+        and extra % 8 == 0
     )
 
 

time: 136 us -> 136 us (level)
  waiting for transfers between devices: 36.3 us -> 33.8 us
  local copies, waits for them, and re-layouts: 5.45 us -> 7.1 us
    ppermute x20, waiting for transfers between devices: 32.5 us -> 30.3 us  [swap(): return lax.ppermute(x, axis, [(i, i ^ mask) for i in range(n)])]
    pallas_call x0 -> x2, local copies, waits for them, and re-layouts: none -> 1.42 us  [call(): pl.pallas_call(body, in_specs=list(in_specs) + [VMEM] * len(tokens), **op...]
  transfers between devices with their start and end apart: 21 -> 21, of which waited for: 9 -> 9; matrix products, arithmetic and copies ran while one was open for 1% -> 2% of each run, Pallas kernels for 38% -> 39%
where the time goes in v5:
time: 136 us; the launch traced here: 135 us
  Pallas kernels  53.5 us (39%)
  waiting for transfers between devices  33.8 us (25%)
  starting transfers between devices  25.1 us (18%)
  between operations  14.3 us (11%)
  local copies, waits for them, and re-layouts  7.1 us (5%)
  other arithmetic  1.52 us (1%)
    pallas_call x14, Pallas kernels, call(): pl.pallas_call(body, in_specs=list(in_specs) + [VMEM] * len(tokens), **op...  51.4 us
    ppermute x20, waiting for transfers between devices, swap(): return lax.ppermute(x, axis, [(i, i ^ mask) for i in range(n)])  30.3 us
    ppermute x20, starting transfers between devices, swap(): return lax.ppermute(x, axis, [(i, i ^ mask) for i in range(n)])  25 us
    unnamed x12, local copies, waits for them, and re-layouts  4.74 us
    all_gather x1, waiting for transfers between devices, local_fast(): weight = lax.all_gather(conv_weight, 'fsdp', axis=0, tiled=True)  2.77 us
  transfers between devices with their start and end apart: 21, of which 9 were waited for; matrix products, arithmetic and copies ran while one was open for 2% of the time, Pallas kernels for 39%

profile of v5, /device:TPU:1, one launch (start us, length us, event | category | flops | bytes accessed | tf_op | source)
XLA Modules:
  0.0 135.2 jit_solution(14589619943261348845)
XLA Ops:
  9.9 4.5 %collective-permute-start.1 = (bf16[2,3,80]{2,1,0:T(4,128)(2,1)S(1)}, bf16[2,3,80]{2,1,0:T(4,128)(2,1)S(1)}, u32[]{:S(2)}, u32[]{:S(2)}) collective-permute-start(bf16[2,3,80]{2,1,0:T(4,128)(2,1)S(1)} %maximum_select_fusion), channel_id=1, source_target_pairs={{0,6},{1,7},{2,4},{3,5},{4,2},{5,3},{6,0},{7,1},{8,14},{9,15},{10,... | collective-permute-start | bytes 2888 | tf_op jit(solution)/shard_map/ppermute | solution.py:605
  14.7 1.3 copy-done
  16.1 2.0 %norm_stats.1.refs_1_.refs_2_ = f32[2,640]{1,0:T(2,128)S(1)} custom-call(bf16[1024,640]{1,0:T(8,128)(2,1)S(1)} %bitcast.21), custom_call_target="tpu_custom_call" | custom-call | flops 3276800 | bytes 1310720 | tf_op jit(solution)/shard_map/norm_stats/pallas_call | solution.py:124
  18.3 1.4 %copy-done.1 = bf16[1,32,32,640]{3,2,1,0:T(8,128)(2,1)S(1)} copy-done((bf16[1,32,32,640]{3,2,1,0:T(8,128)(2,1)S(1)}, bf16[1,32,32,640]{3,2,1,0:T(8,128)(2,1)}, u32[]{:S(2)}) %copy-start.1) | copy-done | bytes 1310744
  19.7 2.1 %activate.1 = (bf16[640,1024]{1,0:T(8,128)(2,1)}, f32[1,128]{1,0:T(1,128)S(1)}) custom-call(bf16[1024,640]{1,0:T(8,128)(2,1)S(1)} %bitcast.22, f32[2,640]{1,0:T(2,128)S(1)} %norm_stats.1.refs_1_.refs_2_, bf16[3,640]{1,0:T(4,128)(2,1)S(1)} %reshape.38.refs_2_.refs_3_.refs_1_), custom_call_target="tpu_custom_call" | custom-call | flops 6553600 | bytes 2621440 | tf_op jit(solution)/shard_map/activate/pallas_call | solution.py:45
  21.8 1.5 %collective-permute-start.4 = (bf16[640,1024]{1,0:T(8,128)(2,1)}, bf16[640,1024]{1,0:T(8,128)(2,1)}, u32[]{:S(2)}, u32[]{:S(2)}) collective-permute-start(bf16[640,1024]{1,0:T(8,128)(2,1)} %get-tuple-element.30.refs_1_), channel_id=1, source_target_pairs={{0,1},{1,0},{2,3},{3,2},{4,5},{5,4},{6,7},{7,6},{8,9},{9,8},{10,11... | collective-permute-start | bytes 3932168 | tf_op jit(solution)/shard_map/ppermute | solution.py:605
  26.3 15.8 %weight_grad_rep.1 = (f32[2,2,2,180,640]{4,3,2,1,0:T(8,128)S(1)}, bf16[2,2,180,640]{3,2,1,0:T(8,128)(2,1)S(1)}, bf16[2,2,180,640]{3,2,1,0:T(8,128)(2,1)S(1)}, f32[1,128]{1,0:T(1,128)S(1)}) custom-call(s32[3]{0:T(128)S(1)} %pad_add_fusion.refs_0_, bf16[640,1024]{1,0:T(8,128)(2,1)} %get-tuple-element.30.refs_1_, ...), custom_call_target="tpu_custom_call" | custom-call | flops 8388608000 | bytes 13107200 | tf_op jit(solution)/shard_map/weight_grad_rep/pallas_call | solution.py:45
  44.9 1.3 collective-permute-start.7
  46.2 18.5 %collective-permute-done.6 = bf16[2,2,180,640]{3,1,2,0:T(2,128)(2,1)S(1)} collective-permute-done((bf16[2,2,180,640]{3,1,2,0:T(2,128)(2,1)S(1)}, bf16[2,2,180,640]{3,1,2,0:T(2,128)(2,1)S(1)}, u32[]{:S(2)}, u32[]{:S(2)}) %collective-permute-start.6) | collective-permute-done | bytes 921632 | tf_op jit(solution)/shard_map/ppermute | solution.py:605
  64.8 1.6 %collective-permute-done.7 = bf16[2,2,180,640]{3,1,2,0:T(2,128)(2,1)S(1)} collective-permute-done((bf16[2,2,180,640]{3,1,2,0:T(2,128)(2,1)S(1)}, bf16[2,2,180,640]{3,1,2,0:T(2,128)(2,1)S(1)}, u32[]{:S(2)}, u32[]{:S(2)}) %collective-permute-start.7) | collective-permute-done | bytes 921632 | tf_op jit(solution)/shard_map/ppermute | solution.py:605
  66.7 1.3 collective-permute-start.8
  68.2 1.7 %prepare.1.refs_0_ = bf16[3,1088,640]{2,1,0:T(8,128)(2,1)S(1)} custom-call(bf16[1024,640]{1,0:T(8,128)(2,1)S(1)} %bitcast.23, f32[2,640]{1,0:T(2,128)S(1)} %norm_stats.1.refs_1_.refs_2_, bf16[3,640]{1,0:T(4,128)(2,1)S(1)} %reshape.38.refs_2_.refs_3_.refs_1_, f32[1,128]{1,0:T(1,128)S(1)} %get-tuple-element.34.refs_3_), custom_call_target="tpu_custom_call" | custom-call | flops 13107200 | bytes 5242880 | tf_op jit(solution)/shard_map/prepare/pallas_call | solution.py:45
  69.9 2.0 %copy-done.3 = bf16[3,1088,640]{2,1,0:T(8,128)(2,1)} copy-done((bf16[3,1088,640]{2,1,0:T(8,128)(2,1)}, bf16[3,1088,640]{2,1,0:T(8,128)(2,1)S(1)}, u32[]{:S(2)}) %copy-start.3) | copy-done | bytes 4177944
  71.9 5.8 %collective-permute-done.8.refs_3_ = bf16[2,180,640]{2,1,0:T(8,128)(2,1)S(1)} collective-permute-done((bf16[2,180,640]{2,1,0:T(8,128)(2,1)S(1)}, bf16[2,180,640]{2,1,0:T(8,128)(2,1)S(1)}, u32[]{:S(2)}, u32[]{:S(2)}) %collective-permute-start.8) | collective-permute-done | bytes 460832 | tf_op jit(solution)/shard_map/ppermute | solution.py:605
  80.3 2.6 %collective-permute-start.11 = (bf16[180,640]{1,0:T(8,128)(2,1)}, bf16[180,640]{1,0:T(8,128)(2,1)}, u32[]{:S(2)}, u32[]{:S(2)}) collective-permute-start(bf16[180,640]{1,0:T(8,128)(2,1)} %get-tuple-element.45), channel_id=1, source_target_pairs={{0,4},{1,5},{2,6},{3,7},{4,0},{5,1},{6,2},{7,3},{8,12},{9,13},{10,... | collective-permute-start | bytes 691208 | tf_op jit(solution)/shard_map/ppermute | solution.py:605
  83.2 2.8 %all-gather.2.cloned.1.call-done.refs_0_ = bf16[5760,640]{1,0:T(8,128)(2,1)} async-done(((bf16[720,640]{1,0:T(8,128)(2,1)}), bf16[5760,640]{1,0:T(8,128)(2,1)}) %all-gather.2.cloned.1.call-update) | async-done | bytes 7372816 | tf_op jit(solution)/shard_map/all_gather | solution.py:640
  85.9 3.2 %arrange_weight.1.refs_4_.refs_2_ = bf16[1920,1920]{1,0:T(8,128)(2,1)S(1)} custom-call(bf16[5760,640]{1,0:T(8,128)(2,1)} %all-gather.2.cloned.1.call-done.refs_0_), custom_call_target="tpu_custom_call" | custom-call | bytes 14745600 | tf_op jit(solution)/shard_map/arrange_weight/pallas_call | solution.py:45
  89.1 12.5 %act_grad.1 = (bf16[1024,640]{1,0:T(8,128)(2,1)}, f32[2,640]{1,0:T(2,128)S(1)}) custom-call(bf16[1024,640]{1,0:T(8,128)(2,1)S(1)} %bitcast.27, bf16[1024,640]{1,0:T(8,128)(2,1)S(1)} %bitcast.24, f32[2,640]{1,0:T(2,128)S(1)} %norm_stats.1.refs_1_.refs_2_, bf16[3,640]{1,0:T(4,128)(2,1)S(1)} %reshape.38.refs_2_.refs_3_.refs_1_, ...), custom_call_target="tpu_custom_call" | custom-call | flops 7549747200 | bytes 15237120 | tf_op jit(solution)/shard_map/act_grad/pallas_call | solution.py:45
  102.8 1.7 %collective-permute-start.13 = (bf16[196,640]{1,0:T(8,128)(2,1)S(1)}, bf16[196,640]{1,0:T(8,128)(2,1)S(1)}, u32[]{:S(2)}, u32[]{:S(2)}) collective-permute-start(bf16[196,640]{1,0:T(8,128)(2,1)S(1)} %get-tuple-element.50.refs_1_.refs_0_), channel_id=1, source_target_pairs={{0,8},{8,0},{16,24},{24,16},{1,9},{9,1},{17,25},{25,17},{2,10},{10... | collective-permute-start | bytes 752648 | tf_op jit(solution)/shard_map/ppermute | solution.py:605
  104.5 1.7 %collective-permute-start.14 = (bf16[196,640]{1,0:T(8,128)(2,1)S(1)}, bf16[196,640]{1,0:T(8,128)(2,1)S(1)}, u32[]{:S(2)}, u32[]{:S(2)}) collective-permute-start(bf16[196,640]{1,0:T(8,128)(2,1)S(1)} %get-tuple-element.50.refs_1_.refs_0_), channel_id=1, source_target_pairs={{0,16},{8,24},{16,0},{24,8},{1,17},{9,25},{17,1},{25,9},{2,18},{10... | collective-permute-start | bytes 752648 | tf_op jit(solution)/shard_map/ppermute | solution.py:605
  106.2 9.8 %conv_forward.1 = (bf16[1024,640]{1,0:T(8,128)(2,1)}, f32[1,128]{1,0:T(1,128)S(1)}) custom-call(bf16[3,1088,640]{2,1,0:T(8,128)(2,1)S(1)} %copy-done.4, bf16[3,640]{1,0:T(4,128)(2,1)S(1)} %reshape.38.refs_2_.refs_3_.refs_1_, bf16[1920,1920]{1,0:T(8,128)(2,1)S(1)} %arrange_weight.1.refs_4_.refs_2_, f32[1,128]{1,0:T(1,128)S(1)} %get-tuple-element.47.refs_3_), custom_call_target="tpu_custom_call" | custom-call | flops 7549747200 | bytes 9994240 | tf_op jit(solution)/shard_map/conv_forward/pallas_call | solution.py:45
  117.9 3.5 %collective-permute-start.18 = (f32[3,640]{1,0:T(4,128)S(1)}, f32[3,640]{1,0:T(4,128)S(1)}, u32[]{:S(2)}, u32[]{:S(2)}) collective-permute-start(f32[3,640]{1,0:T(4,128)S(1)} %add_small_of.1.refs_0_), channel_id=1, source_target_pairs={{0,6},{1,7},{2,4},{3,5},{4,2},{5,3},{6,0},{7,1},{8,14},{9,15},{10,... | collective-permute-start | bytes 23048 | tf_op jit(solution)/shard_map/ppermute | solution.py:605
  121.4 2.0 %join_pieces.1 = (f32[720,640]{1,0:T(8,128)}, f32[1,128]{1,0:T(1,128)S(1)}) custom-call(s32[3]{0:T(128)S(1)} %pad_add_fusion.refs_0_, bf16[196,640]{1,0:T(8,128)(2,1)S(1)} %get-tuple-element.50.refs_1_.refs_0_, bf16[196,640]{1,0:T(8,128)(2,1)S(1)} %collective-permute-done.13.refs_2_.refs_1_, bf16[196,640]{1,0:T(8,128)(2,1)S(1)} %collective-permute-done.14.refs_3_.refs_2_, ...), custom_call_target="tpu_custom_call" | custom-call | flops 460800 | bytes 2764800 | tf_op jit(solution)/shard_map/join_pieces/pallas_call | solution.py:45
  123.4 3.5 %collective-permute-start.19 = (f32[3,640]{1,0:T(4,128)S(1)}, f32[3,640]{1,0:T(4,128)S(1)}, u32[]{:S(2)}, u32[]{:S(2)}) collective-permute-start(f32[3,640]{1,0:T(4,128)S(1)} %add_small.1), channel_id=1, source_target_pairs={{0,1},{1,0},{2,3},{3,2},{4,5},{5,4},{6,7},{7,6},{8,9},{9,8},{10,11... | collective-permute-start | bytes 23048 | tf_op jit(solution)/shard_map/ppermute | solution.py:605
  (61 shorter events, 16.9 us)
Async XLA Ops:
  7.2 78.8 %all-gather.2.cloned.1.call-start = ((), (), s32[]{:S(2)}) async-start(), calls=%async_computation | async-start | bytes 8294400 | tf_op jit(solution)/shard_map/all_gather | solution.py:640
  8.6 1.3 collective-permute-start
  8.7 15.6 %collective-permute-start.5 = (bf16[1024,640]{1,0:T(8,128)(2,1)}, bf16[1024,640]{1,0:T(8,128)(2,1)S(1)}, u32[]{:S(2)}, u32[]{:S(2)}) collective-permute-start(bf16[1024,640]{1,0:T(8,128)(2,1)} %bitcast.25), channel_id=1, source_target_pairs={{0,1},{1,0},{2,3},{3,2},{4,5},{5,4},{6,7},{7,6},{8,9},{9,8},{10,11... | collective-permute-start | bytes 3932168 | tf_op jit(solution)/shard_map/ppermute | solution.py:605
  9.9 8.2 %collective-permute-start.1 = (bf16[2,3,80]{2,1,0:T(4,128)(2,1)S(1)}, bf16[2,3,80]{2,1,0:T(4,128)(2,1)S(1)}, u32[]{:S(2)}, u32[]{:S(2)}) collective-permute-start(bf16[2,3,80]{2,1,0:T(4,128)(2,1)S(1)} %maximum_select_fusion), channel_id=1, source_target_pairs={{0,6},{1,7},{2,4},{3,5},{4,2},{5,3},{6,0},{7,1},{8,14},{9,15},{10,... | collective-permute-start | bytes 2888 | tf_op jit(solution)/shard_map/ppermute | solution.py:605
  14.4 3.7 %collective-permute-start.2 = (bf16[2,3,80]{2,1,0:T(4,128)(2,1)S(1)}, bf16[2,3,80]{2,1,0:T(4,128)(2,1)S(1)}, u32[]{:S(2)}, u32[]{:S(2)}) collective-permute-start(bf16[2,3,80]{2,1,0:T(4,128)(2,1)S(1)} %maximum_select_fusion), channel_id=1, source_target_pairs={{0,4},{1,5},{2,6},{3,7},{4,0},{5,1},{6,2},{7,3},{8,12},{9,13},{10,... | collective-permute-start | bytes 2888 | tf_op jit(solution)/shard_map/ppermute | solution.py:605
  14.4 3.7 %collective-permute-start.3 = (bf16[2,3,80]{2,1,0:T(4,128)(2,1)S(1)}, bf16[2,3,80]{2,1,0:T(4,128)(2,1)S(1)}, u32[]{:S(2)}, u32[]{:S(2)}) collective-permute-start(bf16[2,3,80]{2,1,0:T(4,128)(2,1)S(1)} %maximum_select_fusion), channel_id=1, source_target_pairs={{0,2},{1,3},{2,0},{3,1},{4,6},{5,7},{6,4},{7,5},{8,10},{9,11},{10,... | collective-permute-start | bytes 2888 | tf_op jit(solution)/shard_map/ppermute | solution.py:605
  16.1 7.3 %copy-start.5 = (bf16[1,32,32,640]{3,2,1,0:T(8,128)(2,1)S(1)}, bf16[1,32,32,640]{3,2,1,0:T(8,128)(2,1)}, u32[]{:S(2)}) copy-start(bf16[1,32,32,640]{3,2,1,0:T(8,128)(2,1)} %param.7) | copy-start | bytes 3932164
  21.8 4.5 %collective-permute-start.4 = (bf16[640,1024]{1,0:T(8,128)(2,1)}, bf16[640,1024]{1,0:T(8,128)(2,1)}, u32[]{:S(2)}, u32[]{:S(2)}) collective-permute-start(bf16[640,1024]{1,0:T(8,128)(2,1)} %get-tuple-element.30.refs_1_), channel_id=1, source_target_pairs={{0,1},{1,0},{2,3},{3,2},{4,5},{5,4},{6,7},{7,6},{8,9},{9,8},{10,11... | collective-permute-start | bytes 3932168 | tf_op jit(solution)/shard_map/ppermute | solution.py:605
  42.9 21.8 %collective-permute-start.6 = (bf16[2,2,180,640]{3,1,2,0:T(2,128)(2,1)S(1)}, bf16[2,2,180,640]{3,1,2,0:T(2,128)(2,1)S(1)}, u32[]{:S(2)}, u32[]{:S(2)}) collective-permute-start(bf16[2,2,180,640]{3,1,2,0:T(2,128)(2,1)S(1)} %copy.14), channel_id=1, source_target_pairs={{0,8},{8,0},{16,24},{24,16},{1,9},{9,1},{17,25},{25,17},{2,10},{10... | collective-permute-start | bytes 2764808 | tf_op jit(solution)/shard_map/ppermute | solution.py:605
  44.9 21.5 %collective-permute-start.7 = (bf16[2,2,180,640]{3,1,2,0:T(2,128)(2,1)S(1)}, bf16[2,2,180,640]{3,1,2,0:T(2,128)(2,1)S(1)}, u32[]{:S(2)}, u32[]{:S(2)}) collective-permute-start(bf16[2,2,180,640]{3,1,2,0:T(2,128)(2,1)S(1)} %copy.15), channel_id=1, source_target_pairs={{0,16},{8,24},{16,0},{24,8},{1,17},{9,25},{17,1},{25,9},{2,18},{10... | collective-permute-start | bytes 2764808 | tf_op jit(solution)/shard_map/ppermute | solution.py:605
  66.7 11.0 %collective-permute-start.8 = (bf16[2,180,640]{2,1,0:T(8,128)(2,1)S(1)}, bf16[2,180,640]{2,1,0:T(8,128)(2,1)S(1)}, u32[]{:S(2)}, u32[]{:S(2)}) collective-permute-start(bf16[2,180,640]{2,1,0:T(8,128)(2,1)S(1)} %get-tuple-element.39), channel_id=1, source_target_pairs={{0,16},{8,24},{16,0},{24,8},{1,17},{9,25},{17,1},{25,9},{2,18},{10... | collective-permute-start | bytes 1382408 | tf_op jit(solution)/shard_map/ppermute | solution.py:605
  68.0 10.7 %collective-permute-start.9 = (bf16[2,180,640]{2,1,0:T(8,128)(2,1)S(1)}, bf16[2,180,640]{2,1,0:T(8,128)(2,1)S(1)}, u32[]{:S(2)}, u32[]{:S(2)}) collective-permute-start(bf16[2,180,640]{2,1,0:T(8,128)(2,1)S(1)} %get-tuple-element.40), channel_id=1, source_target_pairs={{0,8},{8,0},{16,24},{24,16},{1,9},{9,1},{17,25},{25,17},{2,10},{10... | collective-permute-start | bytes 1382408 | tf_op jit(solution)/shard_map/ppermute | solution.py:605
  69.9 2.0 %copy-start.3 = (bf16[3,1088,640]{2,1,0:T(8,128)(2,1)}, bf16[3,1088,640]{2,1,0:T(8,128)(2,1)S(1)}, u32[]{:S(2)}) copy-start(bf16[3,1088,640]{2,1,0:T(8,128)(2,1)S(1)} %prepare.1.refs_0_) | copy-start | bytes 12533764
  79.6 22.0 %collective-permute-start.10 = (bf16[180,640]{1,0:T(8,128)(2,1)}, bf16[180,640]{1,0:T(8,128)(2,1)S(1)}, u32[]{:S(2)}, u32[]{:S(2)}) collective-permute-start(bf16[180,640]{1,0:T(8,128)(2,1)} %get-tuple-element.44), channel_id=1, source_target_pairs={{0,2},{1,3},{2,0},{3,1},{4,6},{5,7},{6,4},{7,5},{8,10},{9,11},{10,... | collective-permute-start | bytes 691208 | tf_op jit(solution)/shard_map/ppermute | solution.py:605
  80.3 21.3 %collective-permute-start.11 = (bf16[180,640]{1,0:T(8,128)(2,1)}, bf16[180,640]{1,0:T(8,128)(2,1)}, u32[]{:S(2)}, u32[]{:S(2)}) collective-permute-start(bf16[180,640]{1,0:T(8,128)(2,1)} %get-tuple-element.45), channel_id=1, source_target_pairs={{0,4},{1,5},{2,6},{3,7},{4,0},{5,1},{6,2},{7,3},{8,12},{9,13},{10,... | collective-permute-start | bytes 691208 | tf_op jit(solution)/shard_map/ppermute | solution.py:605
  83.0 18.7 %collective-permute-start.12 = (bf16[180,640]{1,0:T(8,128)(2,1)}, bf16[180,640]{1,0:T(8,128)(2,1)}, u32[]{:S(2)}, u32[]{:S(2)}) collective-permute-start(bf16[180,640]{1,0:T(8,128)(2,1)} %get-tuple-element.46), channel_id=1, source_target_pairs={{0,6},{1,7},{2,4},{3,5},{4,2},{5,3},{6,0},{7,1},{8,14},{9,15},{10,... | collective-permute-start | bytes 691208 | tf_op jit(solution)/shard_map/ppermute | solution.py:605
  89.1 17.1 %copy-start.4 = (bf16[3,1088,640]{2,1,0:T(8,128)(2,1)S(1)}, bf16[3,1088,640]{2,1,0:T(8,128)(2,1)}, u32[]{:S(2)}) copy-start(bf16[3,1088,640]{2,1,0:T(8,128)(2,1)} %copy-done.3) | copy-start | bytes 12533764
  102.8 13.3 %collective-permute-start.13 = (bf16[196,640]{1,0:T(8,128)(2,1)S(1)}, bf16[196,640]{1,0:T(8,128)(2,1)S(1)}, u32[]{:S(2)}, u32[]{:S(2)}) collective-permute-start(bf16[196,640]{1,0:T(8,128)(2,1)S(1)} %get-tuple-element.50.refs_1_.refs_0_), channel_id=1, source_target_pairs={{0,8},{8,0},{16,24},{24,16},{1,9},{9,1},{17,25},{25,17},{2,10},{10... | collective-permute-start | bytes 752648 | tf_op jit(solution)/shard_map/ppermute | solution.py:605
  104.5 12.1 %collective-permute-start.14 = (bf16[196,640]{1,0:T(8,128)(2,1)S(1)}, bf16[196,640]{1,0:T(8,128)(2,1)S(1)}, u32[]{:S(2)}, u32[]{:S(2)}) collective-permute-start(bf16[196,640]{1,0:T(8,128)(2,1)S(1)} %get-tuple-element.50.refs_1_.refs_0_), channel_id=1, source_target_pairs={{0,16},{8,24},{16,0},{24,8},{1,17},{9,25},{17,1},{25,9},{2,18},{10... | collective-permute-start | bytes 752648 | tf_op jit(solution)/shard_map/ppermute | solution.py:605
  106.2 11.5 %collective-permute-start.15 = (bf16[196,640]{1,0:T(8,128)(2,1)S(1)}, bf16[196,640]{1,0:T(8,128)(2,1)S(1)}, u32[]{:S(2)}, u32[]{:S(2)}) collective-permute-start(bf16[196,640]{1,0:T(8,128)(2,1)S(1)} %get-tuple-element.50.refs_1_.refs_0_), channel_id=1, source_target_pairs={{0,24},{8,16},{16,8},{24,0},{1,25},{9,17},{17,9},{25,1},{2,26},{10... | collective-permute-start | bytes 752648 | tf_op jit(solution)/shard_map/ppermute | solution.py:605
  117.7 5.7 %collective-permute-start.16 = (f32[3,640]{1,0:T(4,128)S(1)}, f32[3,640]{1,0:T(4,128)S(1)}, u32[]{:S(2)}, u32[]{:S(2)}) collective-permute-start(f32[3,640]{1,0:T(4,128)S(1)} %add_small_of.1.refs_0_), channel_id=1, source_target_pairs={{0,2},{1,3},{2,0},{3,1},{4,6},{5,7},{6,4},{7,5},{8,10},{9,11},{10,... | collective-permute-start | bytes 23048 | tf_op jit(solution)/shard_map/ppermute | solution.py:605
  117.8 5.6 %collective-permute-start.17 = (f32[3,640]{1,0:T(4,128)S(1)}, f32[3,640]{1,0:T(4,128)S(1)}, u32[]{:S(2)}, u32[]{:S(2)}) collective-permute-start(f32[3,640]{1,0:T(4,128)S(1)} %add_small_of.1.refs_0_), channel_id=1, source_target_pairs={{0,4},{1,5},{2,6},{3,7},{4,0},{5,1},{6,2},{7,3},{8,12},{9,13},{10,... | collective-permute-start | bytes 23048 | tf_op jit(solution)/shard_map/ppermute | solution.py:605
  117.9 5.5 %collective-permute-start.18 = (f32[3,640]{1,0:T(4,128)S(1)}, f32[3,640]{1,0:T(4,128)S(1)}, u32[]{:S(2)}, u32[]{:S(2)}) collective-permute-start(f32[3,640]{1,0:T(4,128)S(1)} %add_small_of.1.refs_0_), channel_id=1, source_target_pairs={{0,6},{1,7},{2,4},{3,5},{4,2},{5,3},{6,0},{7,1},{8,14},{9,15},{10,... | collective-permute-start | bytes 23048 | tf_op jit(solution)/shard_map/ppermute | solution.py:605
  123.4 4.3 %collective-permute-start.19 = (f32[3,640]{1,0:T(4,128)S(1)}, f32[3,640]{1,0:T(4,128)S(1)}, u32[]{:S(2)}, u32[]{:S(2)}) collective-permute-start(f32[3,640]{1,0:T(4,128)S(1)} %add_small.1), channel_id=1, source_target_pairs={{0,1},{1,0},{2,3},{3,2},{4,5},{5,4},{6,7},{7,6},{8,9},{9,8},{10,11... | collective-permute-start | bytes 23048 | tf_op jit(solution)/shard_map/ppermute | solution.py:605
  (3 other events, 4.5 us)
Sparse Core Ops, SparseCore 0:
  9.6 76.2 all-gather.1

commit v6 on v5

--- a/solution.py
+++ b/solution.py
@@ -259,8 +259,9 @@
     for ref in refs[1:-1]:
         total = total + ref[...].astype(F32)
     piece = total.shape[0]
-    head = out_ref.shape[0] - piece
-    out_ref[head:, :] = total.astype(BF16)
+    head = 16
+    rest = jnp.zeros((out_ref.shape[0] - head - piece, total.shape[1]), F32)
+    out_ref[head:, :] = jnp.concatenate([total, rest], axis=0).astype(BF16)
     small = jnp.concatenate([bias_ref[...], param_ref[...]], axis=0)
     high = small.astype(BF16).astype(F32)
     middle = (small - high).astype(BF16).astype(F32)
@@ -278,7 +279,7 @@
         [VMEM] * (2 + len(terms)),
         (),
         True,
-        out_shape=struct((piece + 16, outs), BF16),
+        out_shape=struct((16 + round_up(piece, 16), outs), BF16),
         out_specs=VMEM,
         compiler_params=params(8),
         cost_estimate=pl.CostEstimate(
@@ -293,7 +294,7 @@
     count = out_ref.shape[0]
     terms = []
     for ref in refs[:-1]:
-        rows = ref[0 : ref.shape[0] - piece, :].astype(F32)
+        rows = ref[0:16, :].astype(F32)
         terms.append(rows[0:count] + rows[count : 2 * count] + rows[2 * count : 3 * count])
     out_ref[...] = tree_sum(terms)
 
@@ -553,7 +554,7 @@
 
             @pl.when((q ^ r) == rel)
             def _():
-                out_ref[step * q : step * q + piece, :] = ref[ref.shape[0] - piece :, :].astype(F32) * scale
+                out_ref[step * q : step * q + piece, :] = ref[16:, :].astype(F32)[:piece] * scale
 
 
 def join(place, pieces, rows, piece, scale, tokens):

time: 136 us -> 136 us (level)
  no operation moved by 1% of the time
where the time goes in v6:
time: 136 us; the launch traced here: 135 us
  Pallas kernels  53.5 us (39%)
  waiting for transfers between devices  34.2 us (25%)
  starting transfers between devices  24.6 us (18%)
  between operations  14.3 us (11%)
  local copies, waits for them, and re-layouts  7.1 us (5%)
  other arithmetic  1.52 us (1%)
    pallas_call x14, Pallas kernels, call(): pl.pallas_call(body, in_specs=list(in_specs) + [VMEM] * len(tokens), **op...  51.4 us
    ppermute x20, waiting for transfers between devices, swap(): return lax.ppermute(x, axis, [(i, i ^ mask) for i in range(n)])  30.8 us
    ppermute x20, starting transfers between devices, swap(): return lax.ppermute(x, axis, [(i, i ^ mask) for i in range(n)])  24.6 us
    unnamed x12, local copies, waits for them, and re-layouts  4.74 us
    all_gather x1, waiting for transfers between devices, local_fast(): weight = lax.all_gather(conv_weight, 'fsdp', axis=0, tiled=True)  2.77 us
  transfers between devices with their start and end apart: 21, of which 9 were waited for; matrix products, arithmetic and copies ran while one was open for 2% of the time, Pallas kernels for 39%

profile of v6, /device:TPU:1, one launch (start us, length us, event | category | flops | bytes accessed | tf_op | source)
XLA Modules:
  0.0 135.2 jit_solution(10551732887631959843)
XLA Ops:
  9.9 4.5 %collective-permute-start.1 = (bf16[2,3,80]{2,1,0:T(4,128)(2,1)S(1)}, bf16[2,3,80]{2,1,0:T(4,128)(2,1)S(1)}, u32[]{:S(2)}, u32[]{:S(2)}) collective-permute-start(bf16[2,3,80]{2,1,0:T(4,128)(2,1)S(1)} %maximum_select_fusion), channel_id=1, source_target_pairs={{0,6},{1,7},{2,4},{3,5},{4,2},{5,3},{6,0},{7,1},{8,14},{9,15},{10,... | collective-permute-start | bytes 2888 | tf_op jit(solution)/shard_map/ppermute | solution.py:606
  14.7 1.3 copy-done
  16.1 2.0 %norm_stats.1.refs_1_.refs_2_ = f32[2,640]{1,0:T(2,128)S(1)} custom-call(bf16[1024,640]{1,0:T(8,128)(2,1)S(1)} %bitcast.21), custom_call_target="tpu_custom_call" | custom-call | flops 3276800 | bytes 1310720 | tf_op jit(solution)/shard_map/norm_stats/pallas_call | solution.py:124
  18.3 1.4 %copy-done.1 = bf16[1,32,32,640]{3,2,1,0:T(8,128)(2,1)S(1)} copy-done((bf16[1,32,32,640]{3,2,1,0:T(8,128)(2,1)S(1)}, bf16[1,32,32,640]{3,2,1,0:T(8,128)(2,1)}, u32[]{:S(2)}) %copy-start.1) | copy-done | bytes 1310744
  19.7 2.1 %activate.1 = (bf16[640,1024]{1,0:T(8,128)(2,1)}, f32[1,128]{1,0:T(1,128)S(1)}) custom-call(bf16[1024,640]{1,0:T(8,128)(2,1)S(1)} %bitcast.22, f32[2,640]{1,0:T(2,128)S(1)} %norm_stats.1.refs_1_.refs_2_, bf16[3,640]{1,0:T(4,128)(2,1)S(1)} %reshape.38.refs_2_.refs_3_.refs_1_), custom_call_target="tpu_custom_call" | custom-call | flops 6553600 | bytes 2621440 | tf_op jit(solution)/shard_map/activate/pallas_call | solution.py:45
  21.8 1.5 %collective-permute-start.4 = (bf16[640,1024]{1,0:T(8,128)(2,1)}, bf16[640,1024]{1,0:T(8,128)(2,1)}, u32[]{:S(2)}, u32[]{:S(2)}) collective-permute-start(bf16[640,1024]{1,0:T(8,128)(2,1)} %get-tuple-element.30.refs_1_), channel_id=1, source_target_pairs={{0,1},{1,0},{2,3},{3,2},{4,5},{5,4},{6,7},{7,6},{8,9},{9,8},{10,11... | collective-permute-start | bytes 3932168 | tf_op jit(solution)/shard_map/ppermute | solution.py:606
  26.3 15.8 %weight_grad_rep.1 = (f32[2,2,2,180,640]{4,3,2,1,0:T(8,128)S(1)}, bf16[2,2,180,640]{3,2,1,0:T(8,128)(2,1)S(1)}, bf16[2,2,180,640]{3,2,1,0:T(8,128)(2,1)S(1)}, f32[1,128]{1,0:T(1,128)S(1)}) custom-call(s32[3]{0:T(128)S(1)} %pad_add_fusion.refs_0_, bf16[640,1024]{1,0:T(8,128)(2,1)} %get-tuple-element.30.refs_1_, ...), custom_call_target="tpu_custom_call" | custom-call | flops 8388608000 | bytes 13107200 | tf_op jit(solution)/shard_map/weight_grad_rep/pallas_call | solution.py:45
  44.9 1.3 collective-permute-start.7
  46.2 18.5 %collective-permute-done.6 = bf16[2,2,180,640]{3,1,2,0:T(2,128)(2,1)S(1)} collective-permute-done((bf16[2,2,180,640]{3,1,2,0:T(2,128)(2,1)S(1)}, bf16[2,2,180,640]{3,1,2,0:T(2,128)(2,1)S(1)}, u32[]{:S(2)}, u32[]{:S(2)}) %collective-permute-start.6) | collective-permute-done | bytes 921632 | tf_op jit(solution)/shard_map/ppermute | solution.py:606
  64.8 1.6 %collective-permute-done.7 = bf16[2,2,180,640]{3,1,2,0:T(2,128)(2,1)S(1)} collective-permute-done((bf16[2,2,180,640]{3,1,2,0:T(2,128)(2,1)S(1)}, bf16[2,2,180,640]{3,1,2,0:T(2,128)(2,1)S(1)}, u32[]{:S(2)}, u32[]{:S(2)}) %collective-permute-start.7) | collective-permute-done | bytes 921632 | tf_op jit(solution)/shard_map/ppermute | solution.py:606
  66.7 1.3 collective-permute-start.8
  68.2 1.7 %prepare.1.refs_0_ = bf16[3,1088,640]{2,1,0:T(8,128)(2,1)S(1)} custom-call(bf16[1024,640]{1,0:T(8,128)(2,1)S(1)} %bitcast.23, f32[2,640]{1,0:T(2,128)S(1)} %norm_stats.1.refs_1_.refs_2_, bf16[3,640]{1,0:T(4,128)(2,1)S(1)} %reshape.38.refs_2_.refs_3_.refs_1_, f32[1,128]{1,0:T(1,128)S(1)} %get-tuple-element.34.refs_3_), custom_call_target="tpu_custom_call" | custom-call | flops 13107200 | bytes 5242880 | tf_op jit(solution)/shard_map/prepare/pallas_call | solution.py:45
  69.9 2.0 %copy-done.3 = bf16[3,1088,640]{2,1,0:T(8,128)(2,1)} copy-done((bf16[3,1088,640]{2,1,0:T(8,128)(2,1)}, bf16[3,1088,640]{2,1,0:T(8,128)(2,1)S(1)}, u32[]{:S(2)}) %copy-start.3) | copy-done | bytes 4177944
  71.9 5.8 %collective-permute-done.8.refs_3_ = bf16[2,180,640]{2,1,0:T(8,128)(2,1)S(1)} collective-permute-done((bf16[2,180,640]{2,1,0:T(8,128)(2,1)S(1)}, bf16[2,180,640]{2,1,0:T(8,128)(2,1)S(1)}, u32[]{:S(2)}, u32[]{:S(2)}) %collective-permute-start.8) | collective-permute-done | bytes 460832 | tf_op jit(solution)/shard_map/ppermute | solution.py:606
  80.3 2.6 %collective-permute-start.11 = (bf16[180,640]{1,0:T(8,128)(2,1)}, bf16[180,640]{1,0:T(8,128)(2,1)}, u32[]{:S(2)}, u32[]{:S(2)}) collective-permute-start(bf16[180,640]{1,0:T(8,128)(2,1)} %get-tuple-element.45), channel_id=1, source_target_pairs={{0,4},{1,5},{2,6},{3,7},{4,0},{5,1},{6,2},{7,3},{8,12},{9,13},{10,... | collective-permute-start | bytes 691208 | tf_op jit(solution)/shard_map/ppermute | solution.py:606
  83.2 2.8 %all-gather.2.cloned.1.call-done.refs_0_ = bf16[5760,640]{1,0:T(8,128)(2,1)} async-done(((bf16[720,640]{1,0:T(8,128)(2,1)}), bf16[5760,640]{1,0:T(8,128)(2,1)}) %all-gather.2.cloned.1.call-update) | async-done | bytes 7372816 | tf_op jit(solution)/shard_map/all_gather | solution.py:641
  85.9 3.2 %arrange_weight.1.refs_4_.refs_2_ = bf16[1920,1920]{1,0:T(8,128)(2,1)S(1)} custom-call(bf16[5760,640]{1,0:T(8,128)(2,1)} %all-gather.2.cloned.1.call-done.refs_0_), custom_call_target="tpu_custom_call" | custom-call | bytes 14745600 | tf_op jit(solution)/shard_map/arrange_weight/pallas_call | solution.py:45
  89.1 12.5 %act_grad.1 = (bf16[1024,640]{1,0:T(8,128)(2,1)}, f32[2,640]{1,0:T(2,128)S(1)}) custom-call(bf16[1024,640]{1,0:T(8,128)(2,1)S(1)} %bitcast.27, bf16[1024,640]{1,0:T(8,128)(2,1)S(1)} %bitcast.24, f32[2,640]{1,0:T(2,128)S(1)} %norm_stats.1.refs_1_.refs_2_, bf16[3,640]{1,0:T(4,128)(2,1)S(1)} %reshape.38.refs_2_.refs_3_.refs_1_, ...), custom_call_target="tpu_custom_call" | custom-call | flops 7549747200 | bytes 15237120 | tf_op jit(solution)/shard_map/act_grad/pallas_call | solution.py:45
  102.8 1.7 %collective-permute-start.13 = (bf16[208,640]{1,0:T(8,128)(2,1)S(1)}, bf16[208,640]{1,0:T(8,128)(2,1)S(1)}, u32[]{:S(2)}, u32[]{:S(2)}) collective-permute-start(bf16[208,640]{1,0:T(8,128)(2,1)S(1)} %get-tuple-element.50.refs_1_.refs_0_), channel_id=1, source_target_pairs={{0,8},{8,0},{16,24},{24,16},{1,9},{9,1},{17,25},{25,17},{2,10},{10... | collective-permute-start | bytes 798728 | tf_op jit(solution)/shard_map/ppermute | solution.py:606
  104.5 1.7 %collective-permute-start.14 = (bf16[208,640]{1,0:T(8,128)(2,1)S(1)}, bf16[208,640]{1,0:T(8,128)(2,1)S(1)}, u32[]{:S(2)}, u32[]{:S(2)}) collective-permute-start(bf16[208,640]{1,0:T(8,128)(2,1)S(1)} %get-tuple-element.50.refs_1_.refs_0_), channel_id=1, source_target_pairs={{0,16},{8,24},{16,0},{24,8},{1,17},{9,25},{17,1},{25,9},{2,18},{10... | collective-permute-start | bytes 798728 | tf_op jit(solution)/shard_map/ppermute | solution.py:606
  106.2 9.8 %conv_forward.1 = (bf16[1024,640]{1,0:T(8,128)(2,1)}, f32[1,128]{1,0:T(1,128)S(1)}) custom-call(bf16[3,1088,640]{2,1,0:T(8,128)(2,1)S(1)} %copy-done.4, bf16[3,640]{1,0:T(4,128)(2,1)S(1)} %reshape.38.refs_2_.refs_3_.refs_1_, bf16[1920,1920]{1,0:T(8,128)(2,1)S(1)} %arrange_weight.1.refs_4_.refs_2_, f32[1,128]{1,0:T(1,128)S(1)} %get-tuple-element.47.refs_3_), custom_call_target="tpu_custom_call" | custom-call | flops 7549747200 | bytes 9994240 | tf_op jit(solution)/shard_map/conv_forward/pallas_call | solution.py:45
  118.3 3.5 %collective-permute-start.18 = (f32[3,640]{1,0:T(4,128)S(1)}, f32[3,640]{1,0:T(4,128)S(1)}, u32[]{:S(2)}, u32[]{:S(2)}) collective-permute-start(f32[3,640]{1,0:T(4,128)S(1)} %add_small_of.1.refs_0_), channel_id=1, source_target_pairs={{0,6},{1,7},{2,4},{3,5},{4,2},{5,3},{6,0},{7,1},{8,14},{9,15},{10,... | collective-permute-start | bytes 23048 | tf_op jit(solution)/shard_map/ppermute | solution.py:606
  121.8 2.0 %join_pieces.1 = (f32[720,640]{1,0:T(8,128)}, f32[1,128]{1,0:T(1,128)S(1)}) custom-call(s32[3]{0:T(128)S(1)} %pad_add_fusion.refs_0_, bf16[208,640]{1,0:T(8,128)(2,1)S(1)} %get-tuple-element.50.refs_1_.refs_0_, bf16[208,640]{1,0:T(8,128)(2,1)S(1)} %collective-permute-done.13.refs_2_.refs_1_, bf16[208,640]{1,0:T(8,128)(2,1)S(1)} %collective-permute-done.14.refs_3_.refs_2_, ...), custom_call_target="tpu_custom_call" | custom-call | flops 460800 | bytes 2764800 | tf_op jit(solution)/shard_map/join_pieces/pallas_call | solution.py:45
  123.9 3.0 %collective-permute-start.19 = (f32[3,640]{1,0:T(4,128)S(1)}, f32[3,640]{1,0:T(4,128)S(1)}, u32[]{:S(2)}, u32[]{:S(2)}) collective-permute-start(f32[3,640]{1,0:T(4,128)S(1)} %add_small.1), channel_id=1, source_target_pairs={{0,1},{1,0},{2,3},{3,2},{4,5},{5,4},{6,7},{7,6},{8,9},{9,8},{10,11... | collective-permute-start | bytes 23048 | tf_op jit(solution)/shard_map/ppermute | solution.py:606
  (61 shorter events, 17.4 us)
Async XLA Ops:
  7.2 78.8 %all-gather.2.cloned.1.call-start = ((), (), s32[]{:S(2)}) async-start(), calls=%async_computation | async-start | bytes 8294400 | tf_op jit(solution)/shard_map/all_gather | solution.py:641
  8.6 1.3 collective-permute-start
  8.7 15.6 %collective-permute-start.5 = (bf16[1024,640]{1,0:T(8,128)(2,1)}, bf16[1024,640]{1,0:T(8,128)(2,1)S(1)}, u32[]{:S(2)}, u32[]{:S(2)}) collective-permute-start(bf16[1024,640]{1,0:T(8,128)(2,1)} %bitcast.25), channel_id=1, source_target_pairs={{0,1},{1,0},{2,3},{3,2},{4,5},{5,4},{6,7},{7,6},{8,9},{9,8},{10,11... | collective-permute-start | bytes 3932168 | tf_op jit(solution)/shard_map/ppermute | solution.py:606
  9.9 8.2 %collective-permute-start.1 = (bf16[2,3,80]{2,1,0:T(4,128)(2,1)S(1)}, bf16[2,3,80]{2,1,0:T(4,128)(2,1)S(1)}, u32[]{:S(2)}, u32[]{:S(2)}) collective-permute-start(bf16[2,3,80]{2,1,0:T(4,128)(2,1)S(1)} %maximum_select_fusion), channel_id=1, source_target_pairs={{0,6},{1,7},{2,4},{3,5},{4,2},{5,3},{6,0},{7,1},{8,14},{9,15},{10,... | collective-permute-start | bytes 2888 | tf_op jit(solution)/shard_map/ppermute | solution.py:606
  14.4 3.7 %collective-permute-start.2 = (bf16[2,3,80]{2,1,0:T(4,128)(2,1)S(1)}, bf16[2,3,80]{2,1,0:T(4,128)(2,1)S(1)}, u32[]{:S(2)}, u32[]{:S(2)}) collective-permute-start(bf16[2,3,80]{2,1,0:T(4,128)(2,1)S(1)} %maximum_select_fusion), channel_id=1, source_target_pairs={{0,4},{1,5},{2,6},{3,7},{4,0},{5,1},{6,2},{7,3},{8,12},{9,13},{10,... | collective-permute-start | bytes 2888 | tf_op jit(solution)/shard_map/ppermute | solution.py:606
  14.4 3.7 %collective-permute-start.3 = (bf16[2,3,80]{2,1,0:T(4,128)(2,1)S(1)}, bf16[2,3,80]{2,1,0:T(4,128)(2,1)S(1)}, u32[]{:S(2)}, u32[]{:S(2)}) collective-permute-start(bf16[2,3,80]{2,1,0:T(4,128)(2,1)S(1)} %maximum_select_fusion), channel_id=1, source_target_pairs={{0,2},{1,3},{2,0},{3,1},{4,6},{5,7},{6,4},{7,5},{8,10},{9,11},{10,... | collective-permute-start | bytes 2888 | tf_op jit(solution)/shard_map/ppermute | solution.py:606
  16.1 7.3 %copy-start.5 = (bf16[1,32,32,640]{3,2,1,0:T(8,128)(2,1)S(1)}, bf16[1,32,32,640]{3,2,1,0:T(8,128)(2,1)}, u32[]{:S(2)}) copy-start(bf16[1,32,32,640]{3,2,1,0:T(8,128)(2,1)} %param.7) | copy-start | bytes 3932164
  21.8 4.5 %collective-permute-start.4 = (bf16[640,1024]{1,0:T(8,128)(2,1)}, bf16[640,1024]{1,0:T(8,128)(2,1)}, u32[]{:S(2)}, u32[]{:S(2)}) collective-permute-start(bf16[640,1024]{1,0:T(8,128)(2,1)} %get-tuple-element.30.refs_1_), channel_id=1, source_target_pairs={{0,1},{1,0},{2,3},{3,2},{4,5},{5,4},{6,7},{7,6},{8,9},{9,8},{10,11... | collective-permute-start | bytes 3932168 | tf_op jit(solution)/shard_map/ppermute | solution.py:606
  42.9 21.8 %collective-permute-start.6 = (bf16[2,2,180,640]{3,1,2,0:T(2,128)(2,1)S(1)}, bf16[2,2,180,640]{3,1,2,0:T(2,128)(2,1)S(1)}, u32[]{:S(2)}, u32[]{:S(2)}) collective-permute-start(bf16[2,2,180,640]{3,1,2,0:T(2,128)(2,1)S(1)} %copy.14), channel_id=1, source_target_pairs={{0,8},{8,0},{16,24},{24,16},{1,9},{9,1},{17,25},{25,17},{2,10},{10... | collective-permute-start | bytes 2764808 | tf_op jit(solution)/shard_map/ppermute | solution.py:606
  44.9 21.5 %collective-permute-start.7 = (bf16[2,2,180,640]{3,1,2,0:T(2,128)(2,1)S(1)}, bf16[2,2,180,640]{3,1,2,0:T(2,128)(2,1)S(1)}, u32[]{:S(2)}, u32[]{:S(2)}) collective-permute-start(bf16[2,2,180,640]{3,1,2,0:T(2,128)(2,1)S(1)} %copy.15), channel_id=1, source_target_pairs={{0,16},{8,24},{16,0},{24,8},{1,17},{9,25},{17,1},{25,9},{2,18},{10... | collective-permute-start | bytes 2764808 | tf_op jit(solution)/shard_map/ppermute | solution.py:606
  66.7 11.0 %collective-permute-start.8 = (bf16[2,180,640]{2,1,0:T(8,128)(2,1)S(1)}, bf16[2,180,640]{2,1,0:T(8,128)(2,1)S(1)}, u32[]{:S(2)}, u32[]{:S(2)}) collective-permute-start(bf16[2,180,640]{2,1,0:T(8,128)(2,1)S(1)} %get-tuple-element.39), channel_id=1, source_target_pairs={{0,16},{8,24},{16,0},{24,8},{1,17},{9,25},{17,1},{25,9},{2,18},{10... | collective-permute-start | bytes 1382408 | tf_op jit(solution)/shard_map/ppermute | solution.py:606
  68.0 10.7 %collective-permute-start.9 = (bf16[2,180,640]{2,1,0:T(8,128)(2,1)S(1)}, bf16[2,180,640]{2,1,0:T(8,128)(2,1)S(1)}, u32[]{:S(2)}, u32[]{:S(2)}) collective-permute-start(bf16[2,180,640]{2,1,0:T(8,128)(2,1)S(1)} %get-tuple-element.40), channel_id=1, source_target_pairs={{0,8},{8,0},{16,24},{24,16},{1,9},{9,1},{17,25},{25,17},{2,10},{10... | collective-permute-start | bytes 1382408 | tf_op jit(solution)/shard_map/ppermute | solution.py:606
  69.9 2.0 %copy-start.3 = (bf16[3,1088,640]{2,1,0:T(8,128)(2,1)}, bf16[3,1088,640]{2,1,0:T(8,128)(2,1)S(1)}, u32[]{:S(2)}) copy-start(bf16[3,1088,640]{2,1,0:T(8,128)(2,1)S(1)} %prepare.1.refs_0_) | copy-start | bytes 12533764
  79.6 22.0 %collective-permute-start.10 = (bf16[180,640]{1,0:T(8,128)(2,1)}, bf16[180,640]{1,0:T(8,128)(2,1)S(1)}, u32[]{:S(2)}, u32[]{:S(2)}) collective-permute-start(bf16[180,640]{1,0:T(8,128)(2,1)} %get-tuple-element.44), channel_id=1, source_target_pairs={{0,2},{1,3},{2,0},{3,1},{4,6},{5,7},{6,4},{7,5},{8,10},{9,11},{10,... | collective-permute-start | bytes 691208 | tf_op jit(solution)/shard_map/ppermute | solution.py:606
  80.3 21.3 %collective-permute-start.11 = (bf16[180,640]{1,0:T(8,128)(2,1)}, bf16[180,640]{1,0:T(8,128)(2,1)}, u32[]{:S(2)}, u32[]{:S(2)}) collective-permute-start(bf16[180,640]{1,0:T(8,128)(2,1)} %get-tuple-element.45), channel_id=1, source_target_pairs={{0,4},{1,5},{2,6},{3,7},{4,0},{5,1},{6,2},{7,3},{8,12},{9,13},{10,... | collective-permute-start | bytes 691208 | tf_op jit(solution)/shard_map/ppermute | solution.py:606
  83.0 18.7 %collective-permute-start.12 = (bf16[180,640]{1,0:T(8,128)(2,1)}, bf16[180,640]{1,0:T(8,128)(2,1)}, u32[]{:S(2)}, u32[]{:S(2)}) collective-permute-start(bf16[180,640]{1,0:T(8,128)(2,1)} %get-tuple-element.46), channel_id=1, source_target_pairs={{0,6},{1,7},{2,4},{3,5},{4,2},{5,3},{6,0},{7,1},{8,14},{9,15},{10,... | collective-permute-start | bytes 691208 | tf_op jit(solution)/shard_map/ppermute | solution.py:606
  89.1 17.1 %copy-start.4 = (bf16[3,1088,640]{2,1,0:T(8,128)(2,1)S(1)}, bf16[3,1088,640]{2,1,0:T(8,128)(2,1)}, u32[]{:S(2)}) copy-start(bf16[3,1088,640]{2,1,0:T(8,128)(2,1)} %copy-done.3) | copy-start | bytes 12533764
  102.8 13.3 %collective-permute-start.13 = (bf16[208,640]{1,0:T(8,128)(2,1)S(1)}, bf16[208,640]{1,0:T(8,128)(2,1)S(1)}, u32[]{:S(2)}, u32[]{:S(2)}) collective-permute-start(bf16[208,640]{1,0:T(8,128)(2,1)S(1)} %get-tuple-element.50.refs_1_.refs_0_), channel_id=1, source_target_pairs={{0,8},{8,0},{16,24},{24,16},{1,9},{9,1},{17,25},{25,17},{2,10},{10... | collective-permute-start | bytes 798728 | tf_op jit(solution)/shard_map/ppermute | solution.py:606
  104.5 12.6 %collective-permute-start.14 = (bf16[208,640]{1,0:T(8,128)(2,1)S(1)}, bf16[208,640]{1,0:T(8,128)(2,1)S(1)}, u32[]{:S(2)}, u32[]{:S(2)}) collective-permute-start(bf16[208,640]{1,0:T(8,128)(2,1)S(1)} %get-tuple-element.50.refs_1_.refs_0_), channel_id=1, source_target_pairs={{0,16},{8,24},{16,0},{24,8},{1,17},{9,25},{17,1},{25,9},{2,18},{10... | collective-permute-start | bytes 798728 | tf_op jit(solution)/shard_map/ppermute | solution.py:606
  106.2 11.9 %collective-permute-start.15 = (bf16[208,640]{1,0:T(8,128)(2,1)S(1)}, bf16[208,640]{1,0:T(8,128)(2,1)S(1)}, u32[]{:S(2)}, u32[]{:S(2)}) collective-permute-start(bf16[208,640]{1,0:T(8,128)(2,1)S(1)} %get-tuple-element.50.refs_1_.refs_0_), channel_id=1, source_target_pairs={{0,24},{8,16},{16,8},{24,0},{1,25},{9,17},{17,9},{25,1},{2,26},{10... | collective-permute-start | bytes 798728 | tf_op jit(solution)/shard_map/ppermute | solution.py:606
  118.2 5.7 %collective-permute-start.16 = (f32[3,640]{1,0:T(4,128)S(1)}, f32[3,640]{1,0:T(4,128)S(1)}, u32[]{:S(2)}, u32[]{:S(2)}) collective-permute-start(f32[3,640]{1,0:T(4,128)S(1)} %add_small_of.1.refs_0_), channel_id=1, source_target_pairs={{0,2},{1,3},{2,0},{3,1},{4,6},{5,7},{6,4},{7,5},{8,10},{9,11},{10,... | collective-permute-start | bytes 23048 | tf_op jit(solution)/shard_map/ppermute | solution.py:606
  118.3 5.6 %collective-permute-start.17 = (f32[3,640]{1,0:T(4,128)S(1)}, f32[3,640]{1,0:T(4,128)S(1)}, u32[]{:S(2)}, u32[]{:S(2)}) collective-permute-start(f32[3,640]{1,0:T(4,128)S(1)} %add_small_of.1.refs_0_), channel_id=1, source_target_pairs={{0,4},{1,5},{2,6},{3,7},{4,0},{5,1},{6,2},{7,3},{8,12},{9,13},{10,... | collective-permute-start | bytes 23048 | tf_op jit(solution)/shard_map/ppermute | solution.py:606
  118.3 5.5 %collective-permute-start.18 = (f32[3,640]{1,0:T(4,128)S(1)}, f32[3,640]{1,0:T(4,128)S(1)}, u32[]{:S(2)}, u32[]{:S(2)}) collective-permute-start(f32[3,640]{1,0:T(4,128)S(1)} %add_small_of.1.refs_0_), channel_id=1, source_target_pairs={{0,6},{1,7},{2,4},{3,5},{4,2},{5,3},{6,0},{7,1},{8,14},{9,15},{10,... | collective-permute-start | bytes 23048 | tf_op jit(solution)/shard_map/ppermute | solution.py:606
  123.9 3.8 %collective-permute-start.19 = (f32[3,640]{1,0:T(4,128)S(1)}, f32[3,640]{1,0:T(4,128)S(1)}, u32[]{:S(2)}, u32[]{:S(2)}) collective-permute-start(f32[3,640]{1,0:T(4,128)S(1)} %add_small.1), channel_id=1, source_target_pairs={{0,1},{1,0},{2,3},{3,2},{4,5},{5,4},{6,7},{7,6},{8,9},{9,8},{10,11... | collective-permute-start | bytes 23048 | tf_op jit(solution)/shard_map/ppermute | solution.py:606
  (3 other events, 4.5 us)
Sparse Core Ops, SparseCore 0:
  9.6 76.2 all-gather.1

commit v7 on v6

--- a/solution.py
+++ b/solution.py
@@ -465,9 +465,9 @@
     means = group_means(jnp.concatenate([sum_ref[...] * gain, rest], axis=0), pixels)
     cross, center = means[0:1], means[1:2]
 
-    @pl.loop(0, pixels // 128)
+    @pl.loop(0, pixels // 256)
     def _(i):
-        rows = pl.ds(pl.multiple_of(i * 128, 128), 128)
+        rows = pl.ds(pl.multiple_of(i * 256, 256), 256)
         normed = (x_ref[rows, :].astype(F32) - mean) * inv
         out_ref[rows, :] = ((scaled[rows, :] - center - normed * cross) * inv).astype(BF16)
 

time: 136 us -> 136 us (level)
  no operation moved by 1% of the time
where the time goes in v7:
time: 136 us; the launch traced here: 135 us
  Pallas kernels  53.4 us (39%)
  waiting for transfers between devices  34.2 us (25%)
  starting transfers between devices  24.7 us (18%)
  between operations  14.3 us (11%)
  local copies, waits for them, and re-layouts  7.1 us (5%)
  other arithmetic  1.52 us (1%)
    pallas_call x14, Pallas kernels, call(): pl.pallas_call(body, in_specs=list(in_specs) + [VMEM] * len(tokens), **op...  51.4 us
    ppermute x20, waiting for transfers between devices, swap(): return lax.ppermute(x, axis, [(i, i ^ mask) for i in range(n)])  30.8 us
    ppermute x20, starting transfers between devices, swap(): return lax.ppermute(x, axis, [(i, i ^ mask) for i in range(n)])  24.6 us
    unnamed x12, local copies, waits for them, and re-layouts  4.74 us
    all_gather x1, waiting for transfers between devices, local_fast(): weight = lax.all_gather(conv_weight, 'fsdp', axis=0, tiled=True)  2.77 us
  transfers between devices with their start and end apart: 21, of which 9 were waited for; matrix products, arithmetic and copies ran while one was open for 2% of the time, Pallas kernels for 39%

profile of v7, /device:TPU:1, one launch (start us, length us, event | category | flops | bytes accessed | tf_op | source)
XLA Modules:
  0.0 135.2 jit_solution(872387714627860799)
XLA Ops:
  9.9 4.5 %collective-permute-start.1 = (bf16[2,3,80]{2,1,0:T(4,128)(2,1)S(1)}, bf16[2,3,80]{2,1,0:T(4,128)(2,1)S(1)}, u32[]{:S(2)}, u32[]{:S(2)}) collective-permute-start(bf16[2,3,80]{2,1,0:T(4,128)(2,1)S(1)} %maximum_select_fusion), channel_id=1, source_target_pairs={{0,6},{1,7},{2,4},{3,5},{4,2},{5,3},{6,0},{7,1},{8,14},{9,15},{10,... | collective-permute-start | bytes 2888 | tf_op jit(solution)/shard_map/ppermute | solution.py:606
  14.7 1.3 copy-done
  16.1 2.0 %norm_stats.1.refs_1_.refs_2_ = f32[2,640]{1,0:T(2,128)S(1)} custom-call(bf16[1024,640]{1,0:T(8,128)(2,1)S(1)} %bitcast.21), custom_call_target="tpu_custom_call" | custom-call | flops 3276800 | bytes 1310720 | tf_op jit(solution)/shard_map/norm_stats/pallas_call | solution.py:124
  18.3 1.4 %copy-done.1 = bf16[1,32,32,640]{3,2,1,0:T(8,128)(2,1)S(1)} copy-done((bf16[1,32,32,640]{3,2,1,0:T(8,128)(2,1)S(1)}, bf16[1,32,32,640]{3,2,1,0:T(8,128)(2,1)}, u32[]{:S(2)}) %copy-start.1) | copy-done | bytes 1310744
  19.7 2.1 %activate.1 = (bf16[640,1024]{1,0:T(8,128)(2,1)}, f32[1,128]{1,0:T(1,128)S(1)}) custom-call(bf16[1024,640]{1,0:T(8,128)(2,1)S(1)} %bitcast.22, f32[2,640]{1,0:T(2,128)S(1)} %norm_stats.1.refs_1_.refs_2_, bf16[3,640]{1,0:T(4,128)(2,1)S(1)} %reshape.38.refs_2_.refs_3_.refs_1_), custom_call_target="tpu_custom_call" | custom-call | flops 6553600 | bytes 2621440 | tf_op jit(solution)/shard_map/activate/pallas_call | solution.py:45
  21.8 1.5 %collective-permute-start.4 = (bf16[640,1024]{1,0:T(8,128)(2,1)}, bf16[640,1024]{1,0:T(8,128)(2,1)}, u32[]{:S(2)}, u32[]{:S(2)}) collective-permute-start(bf16[640,1024]{1,0:T(8,128)(2,1)} %get-tuple-element.30.refs_1_), channel_id=1, source_target_pairs={{0,1},{1,0},{2,3},{3,2},{4,5},{5,4},{6,7},{7,6},{8,9},{9,8},{10,11... | collective-permute-start | bytes 3932168 | tf_op jit(solution)/shard_map/ppermute | solution.py:606
  26.3 15.8 %weight_grad_rep.1 = (f32[2,2,2,180,640]{4,3,2,1,0:T(8,128)S(1)}, bf16[2,2,180,640]{3,2,1,0:T(8,128)(2,1)S(1)}, bf16[2,2,180,640]{3,2,1,0:T(8,128)(2,1)S(1)}, f32[1,128]{1,0:T(1,128)S(1)}) custom-call(s32[3]{0:T(128)S(1)} %pad_add_fusion.refs_0_, bf16[640,1024]{1,0:T(8,128)(2,1)} %get-tuple-element.30.refs_1_, ...), custom_call_target="tpu_custom_call" | custom-call | flops 8388608000 | bytes 13107200 | tf_op jit(solution)/shard_map/weight_grad_rep/pallas_call | solution.py:45
  44.9 1.3 collective-permute-start.7
  46.2 18.5 %collective-permute-done.6 = bf16[2,2,180,640]{3,1,2,0:T(2,128)(2,1)S(1)} collective-permute-done((bf16[2,2,180,640]{3,1,2,0:T(2,128)(2,1)S(1)}, bf16[2,2,180,640]{3,1,2,0:T(2,128)(2,1)S(1)}, u32[]{:S(2)}, u32[]{:S(2)}) %collective-permute-start.6) | collective-permute-done | bytes 921632 | tf_op jit(solution)/shard_map/ppermute | solution.py:606
  64.8 1.6 %collective-permute-done.7 = bf16[2,2,180,640]{3,1,2,0:T(2,128)(2,1)S(1)} collective-permute-done((bf16[2,2,180,640]{3,1,2,0:T(2,128)(2,1)S(1)}, bf16[2,2,180,640]{3,1,2,0:T(2,128)(2,1)S(1)}, u32[]{:S(2)}, u32[]{:S(2)}) %collective-permute-start.7) | collective-permute-done | bytes 921632 | tf_op jit(solution)/shard_map/ppermute | solution.py:606
  66.7 1.3 collective-permute-start.8
  68.2 1.7 %prepare.1.refs_0_ = bf16[3,1088,640]{2,1,0:T(8,128)(2,1)S(1)} custom-call(bf16[1024,640]{1,0:T(8,128)(2,1)S(1)} %bitcast.23, f32[2,640]{1,0:T(2,128)S(1)} %norm_stats.1.refs_1_.refs_2_, bf16[3,640]{1,0:T(4,128)(2,1)S(1)} %reshape.38.refs_2_.refs_3_.refs_1_, f32[1,128]{1,0:T(1,128)S(1)} %get-tuple-element.34.refs_3_), custom_call_target="tpu_custom_call" | custom-call | flops 13107200 | bytes 5242880 | tf_op jit(solution)/shard_map/prepare/pallas_call | solution.py:45
  69.9 2.0 %copy-done.3 = bf16[3,1088,640]{2,1,0:T(8,128)(2,1)} copy-done((bf16[3,1088,640]{2,1,0:T(8,128)(2,1)}, bf16[3,1088,640]{2,1,0:T(8,128)(2,1)S(1)}, u32[]{:S(2)}) %copy-start.3) | copy-done | bytes 4177944
  71.9 5.8 %collective-permute-done.8.refs_3_ = bf16[2,180,640]{2,1,0:T(8,128)(2,1)S(1)} collective-permute-done((bf16[2,180,640]{2,1,0:T(8,128)(2,1)S(1)}, bf16[2,180,640]{2,1,0:T(8,128)(2,1)S(1)}, u32[]{:S(2)}, u32[]{:S(2)}) %collective-permute-start.8) | collective-permute-done | bytes 460832 | tf_op jit(solution)/shard_map/ppermute | solution.py:606
  80.3 2.6 %collective-permute-start.11 = (bf16[180,640]{1,0:T(8,128)(2,1)}, bf16[180,640]{1,0:T(8,128)(2,1)}, u32[]{:S(2)}, u32[]{:S(2)}) collective-permute-start(bf16[180,640]{1,0:T(8,128)(2,1)} %get-tuple-element.45), channel_id=1, source_target_pairs={{0,4},{1,5},{2,6},{3,7},{4,0},{5,1},{6,2},{7,3},{8,12},{9,13},{10,... | collective-permute-start | bytes 691208 | tf_op jit(solution)/shard_map/ppermute | solution.py:606
  83.2 2.8 %all-gather.2.cloned.1.call-done.refs_0_ = bf16[5760,640]{1,0:T(8,128)(2,1)} async-done(((bf16[720,640]{1,0:T(8,128)(2,1)}), bf16[5760,640]{1,0:T(8,128)(2,1)}) %all-gather.2.cloned.1.call-update) | async-done | bytes 7372816 | tf_op jit(solution)/shard_map/all_gather | solution.py:641
  85.9 3.2 %arrange_weight.1.refs_4_.refs_2_ = bf16[1920,1920]{1,0:T(8,128)(2,1)S(1)} custom-call(bf16[5760,640]{1,0:T(8,128)(2,1)} %all-gather.2.cloned.1.call-done.refs_0_), custom_call_target="tpu_custom_call" | custom-call | bytes 14745600 | tf_op jit(solution)/shard_map/arrange_weight/pallas_call | solution.py:45
  89.1 12.4 %act_grad.1 = (bf16[1024,640]{1,0:T(8,128)(2,1)}, f32[2,640]{1,0:T(2,128)S(1)}) custom-call(bf16[1024,640]{1,0:T(8,128)(2,1)S(1)} %bitcast.27, bf16[1024,640]{1,0:T(8,128)(2,1)S(1)} %bitcast.24, f32[2,640]{1,0:T(2,128)S(1)} %norm_stats.1.refs_1_.refs_2_, bf16[3,640]{1,0:T(4,128)(2,1)S(1)} %reshape.38.refs_2_.refs_3_.refs_1_, ...), custom_call_target="tpu_custom_call" | custom-call | flops 7549747200 | bytes 15237120 | tf_op jit(solution)/shard_map/act_grad/pallas_call | solution.py:45
  102.8 1.7 %collective-permute-start.13 = (bf16[208,640]{1,0:T(8,128)(2,1)S(1)}, bf16[208,640]{1,0:T(8,128)(2,1)S(1)}, u32[]{:S(2)}, u32[]{:S(2)}) collective-permute-start(bf16[208,640]{1,0:T(8,128)(2,1)S(1)} %get-tuple-element.50.refs_1_.refs_0_), channel_id=1, source_target_pairs={{0,8},{8,0},{16,24},{24,16},{1,9},{9,1},{17,25},{25,17},{2,10},{10... | collective-permute-start | bytes 798728 | tf_op jit(solution)/shard_map/ppermute | solution.py:606
  104.5 1.7 %collective-permute-start.14 = (bf16[208,640]{1,0:T(8,128)(2,1)S(1)}, bf16[208,640]{1,0:T(8,128)(2,1)S(1)}, u32[]{:S(2)}, u32[]{:S(2)}) collective-permute-start(bf16[208,640]{1,0:T(8,128)(2,1)S(1)} %get-tuple-element.50.refs_1_.refs_0_), channel_id=1, source_target_pairs={{0,16},{8,24},{16,0},{24,8},{1,17},{9,25},{17,1},{25,9},{2,18},{10... | collective-permute-start | bytes 798728 | tf_op jit(solution)/shard_map/ppermute | solution.py:606
  106.2 9.8 %conv_forward.1 = (bf16[1024,640]{1,0:T(8,128)(2,1)}, f32[1,128]{1,0:T(1,128)S(1)}) custom-call(bf16[3,1088,640]{2,1,0:T(8,128)(2,1)S(1)} %copy-done.4, bf16[3,640]{1,0:T(4,128)(2,1)S(1)} %reshape.38.refs_2_.refs_3_.refs_1_, bf16[1920,1920]{1,0:T(8,128)(2,1)S(1)} %arrange_weight.1.refs_4_.refs_2_, f32[1,128]{1,0:T(1,128)S(1)} %get-tuple-element.47.refs_3_), custom_call_target="tpu_custom_call" | custom-call | flops 7549747200 | bytes 9994240 | tf_op jit(solution)/shard_map/conv_forward/pallas_call | solution.py:45
  118.3 3.5 %collective-permute-start.18 = (f32[3,640]{1,0:T(4,128)S(1)}, f32[3,640]{1,0:T(4,128)S(1)}, u32[]{:S(2)}, u32[]{:S(2)}) collective-permute-start(f32[3,640]{1,0:T(4,128)S(1)} %add_small_of.1.refs_0_), channel_id=1, source_target_pairs={{0,6},{1,7},{2,4},{3,5},{4,2},{5,3},{6,0},{7,1},{8,14},{9,15},{10,... | collective-permute-start | bytes 23048 | tf_op jit(solution)/shard_map/ppermute | solution.py:606
  121.8 2.0 %join_pieces.1 = (f32[720,640]{1,0:T(8,128)}, f32[1,128]{1,0:T(1,128)S(1)}) custom-call(s32[3]{0:T(128)S(1)} %pad_add_fusion.refs_0_, bf16[208,640]{1,0:T(8,128)(2,1)S(1)} %get-tuple-element.50.refs_1_.refs_0_, bf16[208,640]{1,0:T(8,128)(2,1)S(1)} %collective-permute-done.13.refs_2_.refs_1_, bf16[208,640]{1,0:T(8,128)(2,1)S(1)} %collective-permute-done.14.refs_3_.refs_2_, ...), custom_call_target="tpu_custom_call" | custom-call | flops 460800 | bytes 2764800 | tf_op jit(solution)/shard_map/join_pieces/pallas_call | solution.py:45
  123.8 3.0 %collective-permute-start.19 = (f32[3,640]{1,0:T(4,128)S(1)}, f32[3,640]{1,0:T(4,128)S(1)}, u32[]{:S(2)}, u32[]{:S(2)}) collective-permute-start(f32[3,640]{1,0:T(4,128)S(1)} %add_small.1), channel_id=1, source_target_pairs={{0,1},{1,0},{2,3},{3,2},{4,5},{5,4},{6,7},{7,6},{8,9},{9,8},{10,11... | collective-permute-start | bytes 23048 | tf_op jit(solution)/shard_map/ppermute | solution.py:606
  (61 shorter events, 17.4 us)
Async XLA Ops:
  7.2 78.8 %all-gather.2.cloned.1.call-start = ((), (), s32[]{:S(2)}) async-start(), calls=%async_computation | async-start | bytes 8294400 | tf_op jit(solution)/shard_map/all_gather | solution.py:641
  8.6 1.3 collective-permute-start
  8.7 15.6 %collective-permute-start.5 = (bf16[1024,640]{1,0:T(8,128)(2,1)}, bf16[1024,640]{1,0:T(8,128)(2,1)S(1)}, u32[]{:S(2)}, u32[]{:S(2)}) collective-permute-start(bf16[1024,640]{1,0:T(8,128)(2,1)} %bitcast.25), channel_id=1, source_target_pairs={{0,1},{1,0},{2,3},{3,2},{4,5},{5,4},{6,7},{7,6},{8,9},{9,8},{10,11... | collective-permute-start | bytes 3932168 | tf_op jit(solution)/shard_map/ppermute | solution.py:606
  9.9 8.2 %collective-permute-start.1 = (bf16[2,3,80]{2,1,0:T(4,128)(2,1)S(1)}, bf16[2,3,80]{2,1,0:T(4,128)(2,1)S(1)}, u32[]{:S(2)}, u32[]{:S(2)}) collective-permute-start(bf16[2,3,80]{2,1,0:T(4,128)(2,1)S(1)} %maximum_select_fusion), channel_id=1, source_target_pairs={{0,6},{1,7},{2,4},{3,5},{4,2},{5,3},{6,0},{7,1},{8,14},{9,15},{10,... | collective-permute-start | bytes 2888 | tf_op jit(solution)/shard_map/ppermute | solution.py:606
  14.4 3.7 %collective-permute-start.2 = (bf16[2,3,80]{2,1,0:T(4,128)(2,1)S(1)}, bf16[2,3,80]{2,1,0:T(4,128)(2,1)S(1)}, u32[]{:S(2)}, u32[]{:S(2)}) collective-permute-start(bf16[2,3,80]{2,1,0:T(4,128)(2,1)S(1)} %maximum_select_fusion), channel_id=1, source_target_pairs={{0,4},{1,5},{2,6},{3,7},{4,0},{5,1},{6,2},{7,3},{8,12},{9,13},{10,... | collective-permute-start | bytes 2888 | tf_op jit(solution)/shard_map/ppermute | solution.py:606
  14.4 3.7 %collective-permute-start.3 = (bf16[2,3,80]{2,1,0:T(4,128)(2,1)S(1)}, bf16[2,3,80]{2,1,0:T(4,128)(2,1)S(1)}, u32[]{:S(2)}, u32[]{:S(2)}) collective-permute-start(bf16[2,3,80]{2,1,0:T(4,128)(2,1)S(1)} %maximum_select_fusion), channel_id=1, source_target_pairs={{0,2},{1,3},{2,0},{3,1},{4,6},{5,7},{6,4},{7,5},{8,10},{9,11},{10,... | collective-permute-start | bytes 2888 | tf_op jit(solution)/shard_map/ppermute | solution.py:606
  16.1 7.3 %copy-start.5 = (bf16[1,32,32,640]{3,2,1,0:T(8,128)(2,1)S(1)}, bf16[1,32,32,640]{3,2,1,0:T(8,128)(2,1)}, u32[]{:S(2)}) copy-start(bf16[1,32,32,640]{3,2,1,0:T(8,128)(2,1)} %param.7) | copy-start | bytes 3932164
  21.8 4.5 %collective-permute-start.4 = (bf16[640,1024]{1,0:T(8,128)(2,1)}, bf16[640,1024]{1,0:T(8,128)(2,1)}, u32[]{:S(2)}, u32[]{:S(2)}) collective-permute-start(bf16[640,1024]{1,0:T(8,128)(2,1)} %get-tuple-element.30.refs_1_), channel_id=1, source_target_pairs={{0,1},{1,0},{2,3},{3,2},{4,5},{5,4},{6,7},{7,6},{8,9},{9,8},{10,11... | collective-permute-start | bytes 3932168 | tf_op jit(solution)/shard_map/ppermute | solution.py:606
  42.9 21.8 %collective-permute-start.6 = (bf16[2,2,180,640]{3,1,2,0:T(2,128)(2,1)S(1)}, bf16[2,2,180,640]{3,1,2,0:T(2,128)(2,1)S(1)}, u32[]{:S(2)}, u32[]{:S(2)}) collective-permute-start(bf16[2,2,180,640]{3,1,2,0:T(2,128)(2,1)S(1)} %copy.14), channel_id=1, source_target_pairs={{0,8},{8,0},{16,24},{24,16},{1,9},{9,1},{17,25},{25,17},{2,10},{10... | collective-permute-start | bytes 2764808 | tf_op jit(solution)/shard_map/ppermute | solution.py:606
  44.9 21.5 %collective-permute-start.7 = (bf16[2,2,180,640]{3,1,2,0:T(2,128)(2,1)S(1)}, bf16[2,2,180,640]{3,1,2,0:T(2,128)(2,1)S(1)}, u32[]{:S(2)}, u32[]{:S(2)}) collective-permute-start(bf16[2,2,180,640]{3,1,2,0:T(2,128)(2,1)S(1)} %copy.15), channel_id=1, source_target_pairs={{0,16},{8,24},{16,0},{24,8},{1,17},{9,25},{17,1},{25,9},{2,18},{10... | collective-permute-start | bytes 2764808 | tf_op jit(solution)/shard_map/ppermute | solution.py:606
  66.7 11.0 %collective-permute-start.8 = (bf16[2,180,640]{2,1,0:T(8,128)(2,1)S(1)}, bf16[2,180,640]{2,1,0:T(8,128)(2,1)S(1)}, u32[]{:S(2)}, u32[]{:S(2)}) collective-permute-start(bf16[2,180,640]{2,1,0:T(8,128)(2,1)S(1)} %get-tuple-element.39), channel_id=1, source_target_pairs={{0,16},{8,24},{16,0},{24,8},{1,17},{9,25},{17,1},{25,9},{2,18},{10... | collective-permute-start | bytes 1382408 | tf_op jit(solution)/shard_map/ppermute | solution.py:606
  68.0 10.7 %collective-permute-start.9 = (bf16[2,180,640]{2,1,0:T(8,128)(2,1)S(1)}, bf16[2,180,640]{2,1,0:T(8,128)(2,1)S(1)}, u32[]{:S(2)}, u32[]{:S(2)}) collective-permute-start(bf16[2,180,640]{2,1,0:T(8,128)(2,1)S(1)} %get-tuple-element.40), channel_id=1, source_target_pairs={{0,8},{8,0},{16,24},{24,16},{1,9},{9,1},{17,25},{25,17},{2,10},{10... | collective-permute-start | bytes 1382408 | tf_op jit(solution)/shard_map/ppermute | solution.py:606
  69.9 2.0 %copy-start.3 = (bf16[3,1088,640]{2,1,0:T(8,128)(2,1)}, bf16[3,1088,640]{2,1,0:T(8,128)(2,1)S(1)}, u32[]{:S(2)}) copy-start(bf16[3,1088,640]{2,1,0:T(8,128)(2,1)S(1)} %prepare.1.refs_0_) | copy-start | bytes 12533764
  79.6 22.0 %collective-permute-start.10 = (bf16[180,640]{1,0:T(8,128)(2,1)}, bf16[180,640]{1,0:T(8,128)(2,1)S(1)}, u32[]{:S(2)}, u32[]{:S(2)}) collective-permute-start(bf16[180,640]{1,0:T(8,128)(2,1)} %get-tuple-element.44), channel_id=1, source_target_pairs={{0,2},{1,3},{2,0},{3,1},{4,6},{5,7},{6,4},{7,5},{8,10},{9,11},{10,... | collective-permute-start | bytes 691208 | tf_op jit(solution)/shard_map/ppermute | solution.py:606
  80.3 21.2 %collective-permute-start.11 = (bf16[180,640]{1,0:T(8,128)(2,1)}, bf16[180,640]{1,0:T(8,128)(2,1)}, u32[]{:S(2)}, u32[]{:S(2)}) collective-permute-start(bf16[180,640]{1,0:T(8,128)(2,1)} %get-tuple-element.45), channel_id=1, source_target_pairs={{0,4},{1,5},{2,6},{3,7},{4,0},{5,1},{6,2},{7,3},{8,12},{9,13},{10,... | collective-permute-start | bytes 691208 | tf_op jit(solution)/shard_map/ppermute | solution.py:606
  83.0 18.6 %collective-permute-start.12 = (bf16[180,640]{1,0:T(8,128)(2,1)}, bf16[180,640]{1,0:T(8,128)(2,1)}, u32[]{:S(2)}, u32[]{:S(2)}) collective-permute-start(bf16[180,640]{1,0:T(8,128)(2,1)} %get-tuple-element.46), channel_id=1, source_target_pairs={{0,6},{1,7},{2,4},{3,5},{4,2},{5,3},{6,0},{7,1},{8,14},{9,15},{10,... | collective-permute-start | bytes 691208 | tf_op jit(solution)/shard_map/ppermute | solution.py:606
  89.1 17.1 %copy-start.4 = (bf16[3,1088,640]{2,1,0:T(8,128)(2,1)S(1)}, bf16[3,1088,640]{2,1,0:T(8,128)(2,1)}, u32[]{:S(2)}) copy-start(bf16[3,1088,640]{2,1,0:T(8,128)(2,1)} %copy-done.3) | copy-start | bytes 12533764
  102.8 13.3 %collective-permute-start.13 = (bf16[208,640]{1,0:T(8,128)(2,1)S(1)}, bf16[208,640]{1,0:T(8,128)(2,1)S(1)}, u32[]{:S(2)}, u32[]{:S(2)}) collective-permute-start(bf16[208,640]{1,0:T(8,128)(2,1)S(1)} %get-tuple-element.50.refs_1_.refs_0_), channel_id=1, source_target_pairs={{0,8},{8,0},{16,24},{24,16},{1,9},{9,1},{17,25},{25,17},{2,10},{10... | collective-permute-start | bytes 798728 | tf_op jit(solution)/shard_map/ppermute | solution.py:606
  104.5 12.6 %collective-permute-start.14 = (bf16[208,640]{1,0:T(8,128)(2,1)S(1)}, bf16[208,640]{1,0:T(8,128)(2,1)S(1)}, u32[]{:S(2)}, u32[]{:S(2)}) collective-permute-start(bf16[208,640]{1,0:T(8,128)(2,1)S(1)} %get-tuple-element.50.refs_1_.refs_0_), channel_id=1, source_target_pairs={{0,16},{8,24},{16,0},{24,8},{1,17},{9,25},{17,1},{25,9},{2,18},{10... | collective-permute-start | bytes 798728 | tf_op jit(solution)/shard_map/ppermute | solution.py:606
  106.2 11.9 %collective-permute-start.15 = (bf16[208,640]{1,0:T(8,128)(2,1)S(1)}, bf16[208,640]{1,0:T(8,128)(2,1)S(1)}, u32[]{:S(2)}, u32[]{:S(2)}) collective-permute-start(bf16[208,640]{1,0:T(8,128)(2,1)S(1)} %get-tuple-element.50.refs_1_.refs_0_), channel_id=1, source_target_pairs={{0,24},{8,16},{16,8},{24,0},{1,25},{9,17},{17,9},{25,1},{2,26},{10... | collective-permute-start | bytes 798728 | tf_op jit(solution)/shard_map/ppermute | solution.py:606
  118.2 5.7 %collective-permute-start.16 = (f32[3,640]{1,0:T(4,128)S(1)}, f32[3,640]{1,0:T(4,128)S(1)}, u32[]{:S(2)}, u32[]{:S(2)}) collective-permute-start(f32[3,640]{1,0:T(4,128)S(1)} %add_small_of.1.refs_0_), channel_id=1, source_target_pairs={{0,2},{1,3},{2,0},{3,1},{4,6},{5,7},{6,4},{7,5},{8,10},{9,11},{10,... | collective-permute-start | bytes 23048 | tf_op jit(solution)/shard_map/ppermute | solution.py:606
  118.2 5.6 %collective-permute-start.17 = (f32[3,640]{1,0:T(4,128)S(1)}, f32[3,640]{1,0:T(4,128)S(1)}, u32[]{:S(2)}, u32[]{:S(2)}) collective-permute-start(f32[3,640]{1,0:T(4,128)S(1)} %add_small_of.1.refs_0_), channel_id=1, source_target_pairs={{0,4},{1,5},{2,6},{3,7},{4,0},{5,1},{6,2},{7,3},{8,12},{9,13},{10,... | collective-permute-start | bytes 23048 | tf_op jit(solution)/shard_map/ppermute | solution.py:606
  118.3 5.5 %collective-permute-start.18 = (f32[3,640]{1,0:T(4,128)S(1)}, f32[3,640]{1,0:T(4,128)S(1)}, u32[]{:S(2)}, u32[]{:S(2)}) collective-permute-start(f32[3,640]{1,0:T(4,128)S(1)} %add_small_of.1.refs_0_), channel_id=1, source_target_pairs={{0,6},{1,7},{2,4},{3,5},{4,2},{5,3},{6,0},{7,1},{8,14},{9,15},{10,... | collective-permute-start | bytes 23048 | tf_op jit(solution)/shard_map/ppermute | solution.py:606
  123.8 3.9 %collective-permute-start.19 = (f32[3,640]{1,0:T(4,128)S(1)}, f32[3,640]{1,0:T(4,128)S(1)}, u32[]{:S(2)}, u32[]{:S(2)}) collective-permute-start(f32[3,640]{1,0:T(4,128)S(1)} %add_small.1), channel_id=1, source_target_pairs={{0,1},{1,0},{2,3},{3,2},{4,5},{5,4},{6,7},{7,6},{8,9},{9,8},{10,11... | collective-permute-start | bytes 23048 | tf_op jit(solution)/shard_map/ppermute | solution.py:606
  (3 other events, 4.5 us)
Sparse Core Ops, SparseCore 0:
  9.6 76.2 all-gather.1
